TPU v7x, 32 devices: a whole 2x2x4 slice. The times are simulated.
32 devices in a mesh: tiles: 32 (over z, y, x, core).
Axes of the slice: x: 2, y: 2, z: 4, core: 2. Of those that a mesh axis runs over, the one named last changes fastest.
Arguments:
- fields: bfloat16 [32, 64, 64, 128], P('tiles')
- cotangent: bfloat16 [32, 64, 64, 128], P('tiles'), may hold values from -6 to 6
- ocean_mask: int32 [32, 64, 64], P('tiles'), may hold values from 0 to 1
- neighbours: int32 [32, 8], P('tiles'), may hold values from -1 to 31, as said below
- kernel: float32 [7, 7, 128], replicated, may hold values from -0.875 to 0.875
- conv_bias: float32 [128], replicated, may hold values from -0.5 to 0.5
- ln_gain: float32 [128], replicated, may hold values from 0.5 to 1.5
- ln_bias: float32 [128], replicated, may hold values from -1.5 to 1.5
- weight_in: bfloat16 [128, 512], replicated, may hold values from -0.5 to 0.5
- bias_in: float32 [512], replicated, may hold values from -1.5 to 1.5
- weight_out: bfloat16 [512, 128], replicated, may hold values from -0.25 to 0.25
- bias_out: float32 [128], replicated, may hold values from -1.5 to 1.5
- layer_scale: float32 [128], replicated, may hold values from 0.3 to 1.5
Outputs:
- updated: bfloat16 [32, 64, 64, 128], P('tiles')
- d_fields: float32 [32, 64, 64, 128], P('tiles')
- d_kernel: float32 [7, 7, 128], replicated
- d_conv_bias: float32 [128], replicated
- d_ln_gain: float32 [128], replicated
- d_ln_bias: float32 [128], replicated
- d_weight_in: float32 [128, 512], replicated
- d_bias_in: float32 [512], replicated
- d_weight_out: float32 [512, 128], replicated
- d_bias_out: float32 [128], replicated
- d_layer_scale: float32 [128], replicated
Inputs may be any that keep to these rules, and one draw needn't show every extreme that they name: `neighbours`: entries name tiles across the north, south, west, east, north-west, north-east, south-west and south-east sides; the lists are mutual (a tile lists its neighbour on one side and is listed on the opposite one) and follow one grid of tiles (where a tile and its listed neighbour both list a tile, it is the one the grid places there; a tile listed by nobody around it holds no ocean). Every listed tile is held by a device at most 7 indices away along tiles, and some listed tile is exactly 7 away; the index offset of a given side is not the same for all tiles.
All inputs are finite; a program needn't handle non-finite values.
Results may differ from a plain program's by a relative error of at most 0.0062.
Values may be sent and summed in bfloat16 or wider, within the bound.
No kernel may reach another device: no remote copies, remote signals or barrier semaphores. Data moves between devices by JAX's collectives and lax.ppermute only.
A program may use at most 448 MiB of HBM per device.

v0:
```python
import math

import jax
import jax.numpy as jnp
from jax import lax
from jax.sharding import PartitionSpec as P

REACH = 7


EPS = 1e-06
GELU_K = 0.7978845608028654
GELU_C = 0.044715
CONTRACT_LAST = (((1,), (1,)), ((), ()))
CONTRACT_ROWS = (((0,), (0,)), ((), ()))


def shifted(value, axis, by):
    peers = lax.axis_size(axis)
    pairs = [(i, i + by) for i in range(peers) if 0 <= i + by < peers]
    return lax.ppermute(value, axis, pairs)


def gelu_parts(hidden):
    cube = hidden * hidden * hidden
    tanh_part = jnp.tanh(GELU_K * (hidden + GELU_C * cube))
    gelu_value = 0.5 * hidden * (1.0 + tanh_part)
    gelu_slope = 0.5 * (1.0 + tanh_part) + 0.5 * hidden * (1.0 - tanh_part * tanh_part) * GELU_K * (
        1.0 + 3.0 * GELU_C * hidden * hidden
    )
    return (gelu_value, gelu_slope)


def block_core(
    conv, signal, ln_gain, ln_bias, weight_in, bias_in, weight_out, bias_out, layer_scale
):
    mean_part = jnp.mean(conv, axis=-1, keepdims=True)
    centred = conv - mean_part
    inv_std = lax.rsqrt(jnp.mean(centred * centred, axis=-1, keepdims=True) + EPS)
    normed = centred * inv_std
    lifted = (normed * ln_gain + ln_bias).astype(jnp.bfloat16)
    hidden = jnp.dot(lifted, weight_in, preferred_element_type=jnp.float32) + bias_in
    gelu_value, gelu_slope = gelu_parts(hidden)
    activated = gelu_value.astype(jnp.bfloat16)
    branch = jnp.dot(activated, weight_out, preferred_element_type=jnp.float32) + bias_out
    d_branch = signal * layer_scale
    branch_low = d_branch.astype(jnp.bfloat16)
    d_activated = lax.dot_general(
        branch_low, weight_out, CONTRACT_LAST, preferred_element_type=jnp.float32
    )
    d_hidden = d_activated * gelu_slope
    hidden_low = d_hidden.astype(jnp.bfloat16)
    d_lifted = lax.dot_general(
        hidden_low, weight_in, CONTRACT_LAST, preferred_element_type=jnp.float32
    )
    d_normed = d_lifted * ln_gain
    d_conv = inv_std * (
        d_normed
        - jnp.mean(d_normed, axis=-1, keepdims=True)
        - normed * jnp.mean(d_normed * normed, axis=-1, keepdims=True)
    )
    partials = (
        jnp.sum(signal * branch, axis=0),
        jnp.sum(d_branch, axis=0),
        lax.dot_general(activated, branch_low, CONTRACT_ROWS, preferred_element_type=jnp.float32),
        jnp.sum(d_hidden, axis=0),
        lax.dot_general(lifted, hidden_low, CONTRACT_ROWS, preferred_element_type=jnp.float32),
        jnp.sum(d_lifted * normed, axis=0),
        jnp.sum(d_lifted, axis=0),
    )
    return (branch, d_conv, partials)


def frame_strips(stack, radius):
    extent = stack.shape[1]
    top_rows = stack[:, :radius]
    bottom_rows = stack[:, extent - radius :]
    left_cols = jnp.swapaxes(stack[:, :, :radius], 1, 2)
    right_cols = jnp.swapaxes(stack[:, :, extent - radius :], 1, 2)
    return jnp.stack([top_rows, bottom_rows, left_cols, right_cols], axis=1)


def assemble(middle, picked, radius):
    extent = middle.shape[1]
    top_mid = picked[:, 0, 1]
    bottom_mid = picked[:, 1, 0]
    left_mid = jnp.swapaxes(picked[:, 2, 3], 1, 2)
    right_mid = jnp.swapaxes(picked[:, 3, 2], 1, 2)
    north_west = picked[:, 4, 1, :, extent - radius :]
    north_east = picked[:, 5, 1, :, :radius]
    south_west = picked[:, 6, 0, :, extent - radius :]
    south_east = picked[:, 7, 0, :, :radius]
    upper = jnp.concatenate([north_west, top_mid, north_east], axis=2)
    centre_band = jnp.concatenate([left_mid, middle, right_mid], axis=2)
    lower = jnp.concatenate([south_west, bottom_mid, south_east], axis=2)
    return jnp.concatenate([upper, centre_band, lower], axis=1)


def depthwise(padded, kernel):
    ksize = kernel.shape[0]
    out_size = padded.shape[1] - ksize + 1
    total = jnp.zeros((padded.shape[0], out_size, out_size, padded.shape[3]), jnp.float32)
    for row_tap in range(ksize):
        for col_tap in range(ksize):
            total = (
                total
                + padded[:, row_tap : row_tap + out_size, col_tap : col_tap + out_size, :]
                * kernel[row_tap, col_tap]
            )
    return total


def kernel_grad(padded, d_conv, ksize):
    out_size = d_conv.shape[1]
    rows_list = []
    for row_tap in range(ksize):
        cols_list = []
        for col_tap in range(ksize):
            window = padded[:, row_tap : row_tap + out_size, col_tap : col_tap + out_size, :]
            cols_list.append(jnp.sum(window * d_conv, axis=(0, 1, 2)))
        rows_list.append(jnp.stack(cols_list))
    return jnp.stack(rows_list)


def direct_pool(stacks, mover):
    pieces = []
    for offset in range(-REACH, REACH + 1):
        if offset == 0:
            pieces.append(stacks)
        else:
            pieces.append(mover(stacks, -offset))
    return jnp.concatenate(pieces, axis=0)


def per_device(
    fields,
    cotangent,
    ocean_mask,
    neighbours,
    kernel,
    conv_bias,
    ln_gain,
    ln_bias,
    weight_in,
    bias_in,
    weight_out,
    bias_out,
    layer_scale,
):
    tile_count = fields.shape[0]
    tile_side = fields.shape[1]
    channels = fields.shape[3]
    ksize = kernel.shape[0]
    radius = ksize // 2
    device = lax.axis_index("tiles")
    mask_float = ocean_mask.astype(jnp.float32)[..., None]
    masked = (fields.astype(jnp.float32) * mask_float).astype(jnp.bfloat16)
    listed = neighbours >= 0
    owner_dev = neighbours // tile_count
    pool_slot = jnp.where(
        listed, (owner_dev - device + REACH) * tile_count + neighbours % tile_count, 0
    )

    def pick(rim_pool):
        chosen = jnp.take(rim_pool, pool_slot, axis=0)
        keep = listed[:, :, None, None, None, None]
        return jnp.where(keep, chosen, jnp.zeros_like(chosen))

    signal = cotangent.astype(jnp.float32) * mask_float
    strips = frame_strips(masked, radius)
    rim_pool = direct_pool(strips, lambda stack, offset: shifted(stack, "tiles", offset))
    padded = assemble(masked, pick(rim_pool), radius).astype(jnp.float32)
    conv = depthwise(padded, kernel) + conv_bias
    branch, d_conv, partials = block_core(
        conv.reshape(-1, channels),
        signal.reshape(-1, channels),
        ln_gain,
        ln_bias,
        weight_in,
        bias_in,
        weight_out,
        bias_out,
        layer_scale,
    )
    branch = branch.reshape(conv.shape)
    d_conv = d_conv.reshape(conv.shape)
    updated = (mask_float * (masked.astype(jnp.float32) + layer_scale * branch)).astype(
        jnp.bfloat16
    )
    kernel_part = kernel_grad(padded, d_conv, ksize)
    bias_part = jnp.sum(d_conv, axis=(0, 1, 2))
    flipped = kernel[::-1, ::-1]
    outgoing = frame_strips(d_conv, radius)
    back_pool = direct_pool(
        outgoing,
        lambda stack, offset: shifted(stack.astype(jnp.bfloat16), "tiles", offset).astype(
            stack.dtype
        ),
    )
    received = pick(back_pool)
    back = depthwise(assemble(d_conv, received, radius), flipped)
    d_fields = mask_float * (signal + back)
    grad_scale = 1.0 / math.sqrt(lax.axis_size("tiles") * tile_count * tile_side * tile_side)
    totals = lax.psum(
        (
            partials[0] * grad_scale,
            partials[1] * grad_scale,
            partials[2] * grad_scale,
            partials[3] * grad_scale,
            partials[4] * grad_scale,
            partials[5] * grad_scale,
            partials[6] * grad_scale,
            kernel_part * grad_scale,
            bias_part * grad_scale,
        ),
        "tiles",
    )
    return (
        updated,
        d_fields,
        totals[7],
        totals[8],
        totals[5],
        totals[6],
        totals[4],
        totals[3],
        totals[2],
        totals[1],
        totals[0],
    )


def solution(mesh):
    placed = (
        P("tiles", None, None, None),
        P("tiles", None, None, None),
        P("tiles", None, None),
        P("tiles", None),
        P(),
        P(),
        P(),
        P(),
        P(),
        P(),
        P(),
        P(),
        P(),
    )
    return jax.shard_map(
        per_device,
        mesh=mesh,
        in_specs=placed,
        out_specs=(
            P("tiles", None, None, None),
            P("tiles", None, None, None),
            P(),
            P(),
            P(),
            P(),
            P(),
            P(),
            P(),
            P(),
            P(),
        ),
        check_vma=False,
    )
```

profile of v0, /device:TPU:15, one launch (start us, length us, event | category | flops | bytes accessed | tf_op | source)
XLA Modules:
  0.0 373.7 jit_solution(18201982747817242116)
XLA Ops:
  26.8 7.5 %collective-permute-done = bf16[1,4,3,64,128]{4,3,2,1,0:T(8,128)(2,1)S(1)} collective-permute-done((bf16[1,4,3,64,128]{4,3,2,1,0:T(8,128)(2,1)S(1)}, bf16[1,4,3,64,128]{4,3,2,1,0:T(8,128)(2,1)S(1)}, u32[]{:S(2)}, u32[]{:S(2)}) %collective-permute-start) | collective-permute-done | bytes 196640 | tf_op jit(solution)/shard_map/ppermute | solution.py:21
  42.3 5.9 %collective-permute-start.4 = (bf16[1,4,3,64,128]{4,3,2,1,0:T(8,128)(2,1)S(1)}, bf16[1,4,3,64,128]{4,3,2,1,0:T(8,128)(2,1)S(1)}, u32[]{:S(2)}, u32[]{:S(2)}) collective-permute-start(bf16[1,4,3,64,128]{4,3,2,1,0:T(8,128)(2,1)S(1)} %pad_maximum_fusion.4), channel_id=1, source_target_pairs={{0,3},{1,4},{2,5},{3,6},{4,7},{5,8},{6,9},{7,10},{8,11},{9,12},{10... | collective-permute-start | bytes 589832 | tf_op jit(solution)/shard_map/ppermute | solution.py:21
  52.2 4.6 %collective-permute-start.6 = (bf16[1,4,3,64,128]{4,3,2,1,0:T(8,128)(2,1)S(1)}, bf16[1,4,3,64,128]{4,3,2,1,0:T(8,128)(2,1)S(1)}, u32[]{:S(2)}, u32[]{:S(2)}) collective-permute-start(bf16[1,4,3,64,128]{4,3,2,1,0:T(8,128)(2,1)S(1)} %pad_maximum_fusion.4), channel_id=1, source_target_pairs={{0,1},{1,2},{2,3},{3,4},{4,5},{5,6},{6,7},{7,8},{8,9},{9,10},{10,1... | collective-permute-start | bytes 589832 | tf_op jit(solution)/shard_map/ppermute | solution.py:21
  64.8 5.2 %collective-permute-done.7 = bf16[1,4,3,64,128]{4,3,2,1,0:T(8,128)(2,1)S(1)} collective-permute-done((bf16[1,4,3,64,128]{4,3,2,1,0:T(8,128)(2,1)S(1)}, bf16[1,4,3,64,128]{4,3,2,1,0:T(8,128)(2,1)S(1)}, u32[]{:S(2)}, u32[]{:S(2)}) %collective-permute-start.7) | collective-permute-done | bytes 196640 | tf_op jit(solution)/shard_map/ppermute | solution.py:21
  91.0 16.8 %fusion.86 = (f32[64,64]{0,1:T(8,128)S(1)}, f32[1,64,64,128]{3,1,2,0:T(8,128)}) fusion(f32[128]{0:T(128)S(1)} %copy-done.19, f32[128]{0:T(128)S(1)} %get-tuple-element.191, f32[1,70,70,128]{3,1,2,0:T(8,128)S(1)} %maximum_convert_fusion, f32[128]{0:T(128)S(1)} %get-tuple-element.192, f32[128]{0:T(128)S(1)} %get-tuple-element.145, ...), kind=kLoop, calls=%fused_computation.343 | loop fusion | flops 51900416 | bytes 104899584 | tf_op jit(solution)/shard_map/reduce_sum | solution.py:37
  122.4 7.5 %multiply_reduce_fusion = (f32[128]{0:T(128)S(1)}, f32[1,64,64,128]{3,1,2,0:T(8,128)S(1)}, bf16[1,64,64,128]{3,1,2,0:T(8,128)(2,1)}) fusion(f32[128]{0:T(128)S(1)} %copy-done.15, f32[64,64]{0,1:T(8,128)S(1)} %copy.173, bf16[1,64,64,128]{3,2,1,0:T(8,128)(2,1)S(1)} %copy-done.8, f32[1,64,64,128]{3,2,1,0:T(8,128)S(1)} %bitcast.278, ...), kind=kLoop, calls=%fused_computation.140 | loop fusion | flops 6291328 | bytes 7357440 | tf_op jit(solution)/shard_map/reduce_sum | solution.py:64
  133.7 6.2 %fusion.87 = (f32[512]{0:T(512)S(1)}, bf16[4096,512]{1,0:T(8,128)(2,1)S(1)}) fusion(f32[4096,512]{1,0:T(8,128)S(1)} %get-tuple-element.195, f32[512]{0:T(512)S(1)} %copy-done.20, bf16[4096,128]{1,0:T(8,128)(2,1)S(1)} %get-tuple-element.123, bf16[512,128]{1,0:T(8,128)(2,1)S(1)} %copy-done.12), kind=kOutput, calls=%fused_computation.344 | convolution fusion | flops 580910592 | bytes 13766656 | tf_op jit(solution)/shard_map/dot_general | solution.py:48
  143.3 5.0 %multiply_reduce_fusion.1 = (f32[128]{0:T(128)S(1)}, f32[4096]{0:T(1024)S(1)}, f32[4096]{0:T(1024)S(1)}, f32[128]{0:T(128)S(1)}, f32[4096,128]{1,0:T(8,128)S(1)}) fusion(f32[1,64,64,128]{3,2,1,0:T(8,128)} %copy.179, f32[4096]{0:T(1024)S(1)} %rsqrt.12, f32[4096]{0:T(1024)S(1)} %div.19, f32[128]{0:T(128)S(1)} %copy-done.16, ...), kind=kOutput, calls=%fused_computation.141 | convolution fusion | flops 541581056 | bytes 8586752 | tf_op jit(solution)/shard_map/dot_general | solution.py:53
  151.1 5.2 %multiply_reduce_fusion.38 = (f32[128]{0:T(128)S(1)}, f32[128]{0:T(128)S(1)}, f32[128]{0:T(128)S(1)}, f32[128]{0:T(128)S(1)}, f32[128]{0:T(128)S(1)}, /*index=5*...) fusion(f32[1,70,70,128]{3,1,2,0:T(8,128)S(1)} %maximum_convert_, ...), kind=kLoop, calls=%fused_computation.178 | loop fusion | flops 13629824 | bytes 29366784 | tf_op jit(solution)/shard_map/reduce_sum | solution.py:120
  156.3 6.1 %multiply_reduce_fusion.20 = (f32[128]{0:T(128)S(1)}, f32[128]{0:T(128)S(1)}, f32[128]{0:T(128)S(1)}, f32[128]{0:T(128)S(1)}, f32[128]{0:T(128)S(1)}, /*index=5*...) fusion(f32[1,70,70,128]{3,1,2,0:T(8,128)S(1)} %maximum_convert_, ...), kind=kLoop, calls=%fused_computation.160 | loop fusion | flops 18872064 | bytes 39855104 | tf_op jit(solution)/shard_map/reduce_sum | solution.py:120
  162.4 6.3 %multiply_reduce_fusion.2 = (f32[128]{0:T(128)S(1)}, f32[128]{0:T(128)S(1)}, f32[128]{0:T(128)S(1)}, f32[128]{0:T(128)S(1)}, f32[128]{0:T(128)S(1)}, /*index=5*/...) fusion(f32[1,70,70,128]{3,1,2,0:T(8,128)S(1)} %maximum_convert_, ...), kind=kLoop, calls=%fused_computation.142 | loop fusion | flops 18872064 | bytes 41952256 | tf_op jit(solution)/shard_map/reduce_sum | solution.py:120
  178.9 5.4 %collective-permute-start.14 = (bf16[1,4,3,64,128]{4,3,2,1,0:T(8,128)(2,1)S(1)}, bf16[1,4,3,64,128]{4,3,2,1,0:T(8,128)(2,1)S(1)}, u32[]{:S(2)}, u32[]{:S(2)}) collective-permute-start(bf16[1,4,3,64,128]{4,3,2,1,0:T(8,128)(2,1)S(1)} %fusion.84), channel_id=1, source_target_pairs={{0,7},{1,8},{2,9},{3,10},{4,11},{5,12},{6,13},{7,14},{8,15},{9,16}... | collective-permute-start | bytes 589832 | tf_op jit(solution)/shard_map/ppermute | solution.py:21
  186.3 39.7 %all-reduce = (f32[7,7,128]{2,1,0:T(8,128)}, f32[128]{0:T(128)}, f32[128]{0:T(128)}, f32[128]{0:T(128)}, f32[512]{0:T(512)}, /*index=5*/f32[128]{0:T(128)}, f32[128]{0:T(128)}) all-reduce(f32[7,7,128]{2,1,0:T(8,128)S(1)} %broadcast_multiply_fusion.1, f32[128]{0:T(128)S(1)} %broadcast_multiply_fusion.9, ...), channel_id=1, replica_groups=mesh['tiles'=32] {'tiles'}, use_global_device_ids=true, to_apply=%region_53.54 | all-reduce | flops 7424 | bytes 59392 | tf_op jit(solution)/shard_map/psum | solution.py:204
  229.3 4.8 %collective-permute-done.15 = bf16[1,4,3,64,128]{4,3,2,1,0:T(8,128)(2,1)S(1)} collective-permute-done((bf16[1,4,3,64,128]{4,3,2,1,0:T(8,128)(2,1)S(1)}, bf16[1,4,3,64,128]{4,3,2,1,0:T(8,128)(2,1)S(1)}, u32[]{:S(2)}, u32[]{:S(2)}) %collective-permute-start.15) | collective-permute-done | bytes 196640 | tf_op jit(solution)/shard_map/ppermute | solution.py:21
  234.1 5.6 %collective-permute-start.16 = (bf16[1,4,3,64,128]{4,3,2,1,0:T(8,128)(2,1)S(1)}, bf16[1,4,3,64,128]{4,3,2,1,0:T(8,128)(2,1)S(1)}, u32[]{:S(2)}, u32[]{:S(2)}) collective-permute-start(bf16[1,4,3,64,128]{4,3,2,1,0:T(8,128)(2,1)S(1)} %fusion.84), channel_id=1, source_target_pairs={{0,5},{1,6},{2,7},{3,8},{4,9},{5,10},{6,11},{7,12},{8,13},{9,14},{... | collective-permute-start | bytes 589832 | tf_op jit(solution)/shard_map/ppermute | solution.py:21
  240.5 4.8 %collective-permute-done.16 = bf16[1,4,3,64,128]{4,3,2,1,0:T(8,128)(2,1)S(1)} collective-permute-done((bf16[1,4,3,64,128]{4,3,2,1,0:T(8,128)(2,1)S(1)}, bf16[1,4,3,64,128]{4,3,2,1,0:T(8,128)(2,1)S(1)}, u32[]{:S(2)}, u32[]{:S(2)}) %collective-permute-start.16) | collective-permute-done | bytes 196640 | tf_op jit(solution)/shard_map/ppermute | solution.py:21
  247.9 5.2 %collective-permute-done.17 = bf16[1,4,3,64,128]{4,3,2,1,0:T(8,128)(2,1)S(1)} collective-permute-done((bf16[1,4,3,64,128]{4,3,2,1,0:T(8,128)(2,1)S(1)}, bf16[1,4,3,64,128]{4,3,2,1,0:T(8,128)(2,1)S(1)}, u32[]{:S(2)}, u32[]{:S(2)}) %collective-permute-start.17) | collective-permute-done | bytes 196640 | tf_op jit(solution)/shard_map/ppermute | solution.py:21
  253.1 4.8 %collective-permute-start.18 = (bf16[1,4,3,64,128]{4,3,2,1,0:T(8,128)(2,1)S(1)}, bf16[1,4,3,64,128]{4,3,2,1,0:T(8,128)(2,1)S(1)}, u32[]{:S(2)}, u32[]{:S(2)}) collective-permute-start(bf16[1,4,3,64,128]{4,3,2,1,0:T(8,128)(2,1)S(1)} %fusion.84), channel_id=1, source_target_pairs={{0,3},{1,4},{2,5},{3,6},{4,7},{5,8},{6,9},{7,10},{8,11},{9,12},{10... | collective-permute-start | bytes 589832 | tf_op jit(solution)/shard_map/ppermute | solution.py:21
  261.4 4.6 %collective-permute-start.19 = (bf16[1,4,3,64,128]{4,3,2,1,0:T(8,128)(2,1)S(1)}, bf16[1,4,3,64,128]{4,3,2,1,0:T(8,128)(2,1)S(1)}, u32[]{:S(2)}, u32[]{:S(2)}) collective-permute-start(bf16[1,4,3,64,128]{4,3,2,1,0:T(8,128)(2,1)S(1)} %fusion.84), channel_id=1, source_target_pairs={{0,2},{1,3},{2,4},{3,5},{4,6},{5,7},{6,8},{7,9},{8,10},{9,11},{10,... | collective-permute-start | bytes 589832 | tf_op jit(solution)/shard_map/ppermute | solution.py:21
  270.4 6.5 %collective-permute-start.20 = (bf16[1,4,3,64,128]{4,3,2,1,0:T(8,128)(2,1)S(1)}, bf16[1,4,3,64,128]{4,3,2,1,0:T(8,128)(2,1)S(1)}, u32[]{:S(2)}, u32[]{:S(2)}) collective-permute-start(bf16[1,4,3,64,128]{4,3,2,1,0:T(8,128)(2,1)S(1)} %fusion.84), channel_id=1, source_target_pairs={{0,1},{1,2},{2,3},{3,4},{4,5},{5,6},{6,7},{7,8},{8,9},{9,10},{10,1... | collective-permute-start | bytes 589832 | tf_op jit(solution)/shard_map/ppermute | solution.py:21
  283.1 6.1 %collective-permute-done.21 = bf16[1,4,3,64,128]{4,3,2,1,0:T(8,128)(2,1)S(1)} collective-permute-done((bf16[1,4,3,64,128]{4,3,2,1,0:T(8,128)(2,1)S(1)}, bf16[1,4,3,64,128]{4,3,2,1,0:T(8,128)(2,1)S(1)}, u32[]{:S(2)}, u32[]{:S(2)}) %collective-permute-start.21) | collective-permute-done | bytes 196640 | tf_op jit(solution)/shard_map/ppermute | solution.py:21
  291.9 5.9 %collective-permute-done.22 = bf16[1,4,3,64,128]{4,3,2,1,0:T(8,128)(2,1)S(1)} collective-permute-done((bf16[1,4,3,64,128]{4,3,2,1,0:T(8,128)(2,1)S(1)}, bf16[1,4,3,64,128]{4,3,2,1,0:T(8,128)(2,1)S(1)}, u32[]{:S(2)}, u32[]{:S(2)}) %collective-permute-start.22) | collective-permute-done | bytes 196640 | tf_op jit(solution)/shard_map/ppermute | solution.py:21
  300.4 6.3 %collective-permute-done.23 = bf16[1,4,3,64,128]{4,3,2,1,0:T(8,128)(2,1)S(1)} collective-permute-done((bf16[1,4,3,64,128]{4,3,2,1,0:T(8,128)(2,1)S(1)}, bf16[1,4,3,64,128]{4,3,2,1,0:T(8,128)(2,1)S(1)}, u32[]{:S(2)}, u32[]{:S(2)}) %collective-permute-start.23) | collective-permute-done | bytes 196640 | tf_op jit(solution)/shard_map/ppermute | solution.py:21
  317.6 41.5 %fusion.46 = f32[1,64,64,128]{3,1,2,0:T(8,128)} fusion(f32[1,67,70,128]{3,1,2,0:T(8,128)} %get-tuple-element.121, f32[1,64,3,128]{3,1,2,0:T(8,128)S(1)} %get-tuple-element.118, f32[1,64,64,128]{3,1,2,0:T(8,128)} %copy-done.2, f32[1,64,3,128]{3,1,2,0:T(8,128)S(1)} %get-tuple-element.119, f32[1,67,70,128]{3,1,2,0:T(8,128)S(1)} %get-tuple-element.120, ...), kind=kLoop, calls=%fused_computation.64 | loop fusion | flops 56098816 | bytes 93561344 | tf_op jit(solution)/shard_map/mul | solution.py:202
  (192 shorter events, 141.1 us)
Async XLA Ops:
  7.2 356.0 %all-reduce.4.cloned.1.call-start = ((), (), s32[]{:S(2)}) async-start(), calls=%async_computation | async-start | bytes 1048576 | tf_op jit(solution)/shard_map/psum | solution.py:204
  11.0 74.8 %collective-permute-start.13 = (bf16[1,4,3,64,128]{4,3,2,1,0:T(8,128)(2,1)S(1)}, bf16[1,4,3,64,128]{4,3,2,1,0:T(8,128)(2,1)S(1)}, u32[]{:S(2)}, u32[]{:S(2)}) collective-permute-start(bf16[1,4,3,64,128]{4,3,2,1,0:T(8,128)(2,1)S(1)} %pad_maximum_fusion.4), channel_id=1, source_target_pairs={{7,0},{8,1},{9,2},{10,3},{11,4},{12,5},{13,6},{14,7},{15,8},{16,9}... | collective-permute-start | bytes 589832 | tf_op jit(solution)/shard_map/ppermute | solution.py:21
  13.7 71.5 %collective-permute-start.12 = (bf16[1,4,3,64,128]{4,3,2,1,0:T(8,128)(2,1)S(1)}, bf16[1,4,3,64,128]{4,3,2,1,0:T(8,128)(2,1)S(1)}, u32[]{:S(2)}, u32[]{:S(2)}) collective-permute-start(bf16[1,4,3,64,128]{4,3,2,1,0:T(8,128)(2,1)S(1)} %pad_maximum_fusion.4), channel_id=1, source_target_pairs={{6,0},{7,1},{8,2},{9,3},{10,4},{11,5},{12,6},{13,7},{14,8},{15,9},... | collective-permute-start | bytes 589832 | tf_op jit(solution)/shard_map/ppermute | solution.py:21
  16.7 67.8 %collective-permute-start.11 = (bf16[1,4,3,64,128]{4,3,2,1,0:T(8,128)(2,1)S(1)}, bf16[1,4,3,64,128]{4,3,2,1,0:T(8,128)(2,1)S(1)}, u32[]{:S(2)}, u32[]{:S(2)}) collective-permute-start(bf16[1,4,3,64,128]{4,3,2,1,0:T(8,128)(2,1)S(1)} %pad_maximum_fusion.4), channel_id=1, source_target_pairs={{5,0},{6,1},{7,2},{8,3},{9,4},{10,5},{11,6},{12,7},{13,8},{14,9},{... | collective-permute-start | bytes 589832 | tf_op jit(solution)/shard_map/ppermute | solution.py:21
  18.6 19.8 %collective-permute-start.1 = (bf16[1,4,3,64,128]{4,3,2,1,0:T(8,128)(2,1)S(1)}, bf16[1,4,3,64,128]{4,3,2,1,0:T(8,128)(2,1)S(1)}, u32[]{:S(2)}, u32[]{:S(2)}) collective-permute-start(bf16[1,4,3,64,128]{4,3,2,1,0:T(8,128)(2,1)S(1)} %pad_maximum_fusion.4), channel_id=1, source_target_pairs={{0,6},{1,7},{2,8},{3,9},{4,10},{5,11},{6,12},{7,13},{8,14},{9,15},... | collective-permute-start | bytes 589832 | tf_op jit(solution)/shard_map/ppermute | solution.py:21
  22.1 12.2 %collective-permute-start = (bf16[1,4,3,64,128]{4,3,2,1,0:T(8,128)(2,1)S(1)}, bf16[1,4,3,64,128]{4,3,2,1,0:T(8,128)(2,1)S(1)}, u32[]{:S(2)}, u32[]{:S(2)}) collective-permute-start(bf16[1,4,3,64,128]{4,3,2,1,0:T(8,128)(2,1)S(1)} %pad_maximum_fusion.4), channel_id=1, source_target_pairs={{0,7},{1,8},{2,9},{3,10},{4,11},{5,12},{6,13},{7,14},{8,15},{9,16}... | collective-permute-start | bytes 589832 | tf_op jit(solution)/shard_map/ppermute | solution.py:21
  38.4 10.5 %collective-permute-start.3 = (bf16[1,4,3,64,128]{4,3,2,1,0:T(8,128)(2,1)S(1)}, bf16[1,4,3,64,128]{4,3,2,1,0:T(8,128)(2,1)S(1)}, u32[]{:S(2)}, u32[]{:S(2)}) collective-permute-start(bf16[1,4,3,64,128]{4,3,2,1,0:T(8,128)(2,1)S(1)} %pad_maximum_fusion.4), channel_id=1, source_target_pairs={{0,4},{1,5},{2,6},{3,7},{4,8},{5,9},{6,10},{7,11},{8,12},{9,13},{1... | collective-permute-start | bytes 589832 | tf_op jit(solution)/shard_map/ppermute | solution.py:21
  42.3 9.9 %collective-permute-start.4 = (bf16[1,4,3,64,128]{4,3,2,1,0:T(8,128)(2,1)S(1)}, bf16[1,4,3,64,128]{4,3,2,1,0:T(8,128)(2,1)S(1)}, u32[]{:S(2)}, u32[]{:S(2)}) collective-permute-start(bf16[1,4,3,64,128]{4,3,2,1,0:T(8,128)(2,1)S(1)} %pad_maximum_fusion.4), channel_id=1, source_target_pairs={{0,3},{1,4},{2,5},{3,6},{4,7},{5,8},{6,9},{7,10},{8,11},{9,12},{10... | collective-permute-start | bytes 589832 | tf_op jit(solution)/shard_map/ppermute | solution.py:21
  48.9 8.6 %collective-permute-start.5 = (bf16[1,4,3,64,128]{4,3,2,1,0:T(8,128)(2,1)S(1)}, bf16[1,4,3,64,128]{4,3,2,1,0:T(8,128)(2,1)S(1)}, u32[]{:S(2)}, u32[]{:S(2)}) collective-permute-start(bf16[1,4,3,64,128]{4,3,2,1,0:T(8,128)(2,1)S(1)} %pad_maximum_fusion.4), channel_id=1, source_target_pairs={{0,2},{1,3},{2,4},{3,5},{4,6},{5,7},{6,8},{7,9},{8,10},{9,11},{10,... | collective-permute-start | bytes 589832 | tf_op jit(solution)/shard_map/ppermute | solution.py:21
  52.2 8.8 %collective-permute-start.6 = (bf16[1,4,3,64,128]{4,3,2,1,0:T(8,128)(2,1)S(1)}, bf16[1,4,3,64,128]{4,3,2,1,0:T(8,128)(2,1)S(1)}, u32[]{:S(2)}, u32[]{:S(2)}) collective-permute-start(bf16[1,4,3,64,128]{4,3,2,1,0:T(8,128)(2,1)S(1)} %pad_maximum_fusion.4), channel_id=1, source_target_pairs={{0,1},{1,2},{2,3},{3,4},{4,5},{5,6},{6,7},{7,8},{8,9},{9,10},{10,1... | collective-permute-start | bytes 589832 | tf_op jit(solution)/shard_map/ppermute | solution.py:21
  57.5 15.0 %collective-permute-start.8 = (bf16[1,4,3,64,128]{4,3,2,1,0:T(8,128)(2,1)S(1)}, bf16[1,4,3,64,128]{4,3,2,1,0:T(8,128)(2,1)S(1)}, u32[]{:S(2)}, u32[]{:S(2)}) collective-permute-start(bf16[1,4,3,64,128]{4,3,2,1,0:T(8,128)(2,1)S(1)} %pad_maximum_fusion.4), channel_id=1, source_target_pairs={{2,0},{3,1},{4,2},{5,3},{6,4},{7,5},{8,6},{9,7},{10,8},{11,9},{12,... | collective-permute-start | bytes 589832 | tf_op jit(solution)/shard_map/ppermute | solution.py:21
  61.0 8.9 %collective-permute-start.7 = (bf16[1,4,3,64,128]{4,3,2,1,0:T(8,128)(2,1)S(1)}, bf16[1,4,3,64,128]{4,3,2,1,0:T(8,128)(2,1)S(1)}, u32[]{:S(2)}, u32[]{:S(2)}) collective-permute-start(bf16[1,4,3,64,128]{4,3,2,1,0:T(8,128)(2,1)S(1)} %pad_maximum_fusion.4), channel_id=1, source_target_pairs={{1,0},{2,1},{3,2},{4,3},{5,4},{6,5},{7,6},{8,7},{9,8},{10,9},{11,1... | collective-permute-start | bytes 589832 | tf_op jit(solution)/shard_map/ppermute | solution.py:21
  69.9 9.0 %collective-permute-start.9 = (bf16[1,4,3,64,128]{4,3,2,1,0:T(8,128)(2,1)S(1)}, bf16[1,4,3,64,128]{4,3,2,1,0:T(8,128)(2,1)S(1)}, u32[]{:S(2)}, u32[]{:S(2)}) collective-permute-start(bf16[1,4,3,64,128]{4,3,2,1,0:T(8,128)(2,1)S(1)} %pad_maximum_fusion.4), channel_id=1, source_target_pairs={{3,0},{4,1},{5,2},{6,3},{7,4},{8,5},{9,6},{10,7},{11,8},{12,9},{13... | collective-permute-start | bytes 589832 | tf_op jit(solution)/shard_map/ppermute | solution.py:21
  72.5 11.3 %collective-permute-start.10 = (bf16[1,4,3,64,128]{4,3,2,1,0:T(8,128)(2,1)S(1)}, bf16[1,4,3,64,128]{4,3,2,1,0:T(8,128)(2,1)S(1)}, u32[]{:S(2)}, u32[]{:S(2)}) collective-permute-start(bf16[1,4,3,64,128]{4,3,2,1,0:T(8,128)(2,1)S(1)} %pad_maximum_fusion.4), channel_id=1, source_target_pairs={{4,0},{5,1},{6,2},{7,3},{8,4},{9,5},{10,6},{11,7},{12,8},{13,9},{1... | collective-permute-start | bytes 589832 | tf_op jit(solution)/shard_map/ppermute | solution.py:21
  170.1 139.8 %collective-permute-start.27 = (bf16[1,4,3,64,128]{4,3,2,1,0:T(8,128)(2,1)S(1)}, bf16[1,4,3,64,128]{4,3,2,1,0:T(8,128)(2,1)S(1)}, u32[]{:S(2)}, u32[]{:S(2)}) collective-permute-start(bf16[1,4,3,64,128]{4,3,2,1,0:T(8,128)(2,1)S(1)} %fusion.84), channel_id=1, source_target_pairs={{7,0},{8,1},{9,2},{10,3},{11,4},{12,5},{13,6},{14,7},{15,8},{16,9}... | collective-permute-start | bytes 589832 | tf_op jit(solution)/shard_map/ppermute | solution.py:21
  172.0 137.1 %collective-permute-start.26 = (bf16[1,4,3,64,128]{4,3,2,1,0:T(8,128)(2,1)S(1)}, bf16[1,4,3,64,128]{4,3,2,1,0:T(8,128)(2,1)S(1)}, u32[]{:S(2)}, u32[]{:S(2)}) collective-permute-start(bf16[1,4,3,64,128]{4,3,2,1,0:T(8,128)(2,1)S(1)} %fusion.84), channel_id=1, source_target_pairs={{6,0},{7,1},{8,2},{9,3},{10,4},{11,5},{12,6},{13,7},{14,8},{15,9},... | collective-permute-start | bytes 589832 | tf_op jit(solution)/shard_map/ppermute | solution.py:21
  173.9 134.3 %collective-permute-start.25 = (bf16[1,4,3,64,128]{4,3,2,1,0:T(8,128)(2,1)S(1)}, bf16[1,4,3,64,128]{4,3,2,1,0:T(8,128)(2,1)S(1)}, u32[]{:S(2)}, u32[]{:S(2)}) collective-permute-start(bf16[1,4,3,64,128]{4,3,2,1,0:T(8,128)(2,1)S(1)} %fusion.84), channel_id=1, source_target_pairs={{5,0},{6,1},{7,2},{8,3},{9,4},{10,5},{11,6},{12,7},{13,8},{14,9},{... | collective-permute-start | bytes 589832 | tf_op jit(solution)/shard_map/ppermute | solution.py:21
  176.4 131.1 %collective-permute-start.24 = (bf16[1,4,3,64,128]{4,3,2,1,0:T(8,128)(2,1)S(1)}, bf16[1,4,3,64,128]{4,3,2,1,0:T(8,128)(2,1)S(1)}, u32[]{:S(2)}, u32[]{:S(2)}) collective-permute-start(bf16[1,4,3,64,128]{4,3,2,1,0:T(8,128)(2,1)S(1)} %fusion.84), channel_id=1, source_target_pairs={{4,0},{5,1},{6,2},{7,3},{8,4},{9,5},{10,6},{11,7},{12,8},{13,9},{1... | collective-permute-start | bytes 589832 | tf_op jit(solution)/shard_map/ppermute | solution.py:21
  178.9 47.1 %collective-permute-start.14 = (bf16[1,4,3,64,128]{4,3,2,1,0:T(8,128)(2,1)S(1)}, bf16[1,4,3,64,128]{4,3,2,1,0:T(8,128)(2,1)S(1)}, u32[]{:S(2)}, u32[]{:S(2)}) collective-permute-start(bf16[1,4,3,64,128]{4,3,2,1,0:T(8,128)(2,1)S(1)} %fusion.84), channel_id=1, source_target_pairs={{0,7},{1,8},{2,9},{3,10},{4,11},{5,12},{6,13},{7,14},{8,15},{9,16}... | collective-permute-start | bytes 589832 | tf_op jit(solution)/shard_map/ppermute | solution.py:21
  234.1 11.1 %collective-permute-start.16 = (bf16[1,4,3,64,128]{4,3,2,1,0:T(8,128)(2,1)S(1)}, bf16[1,4,3,64,128]{4,3,2,1,0:T(8,128)(2,1)S(1)}, u32[]{:S(2)}, u32[]{:S(2)}) collective-permute-start(bf16[1,4,3,64,128]{4,3,2,1,0:T(8,128)(2,1)S(1)} %fusion.84), channel_id=1, source_target_pairs={{0,5},{1,6},{2,7},{3,8},{4,9},{5,10},{6,11},{7,12},{8,13},{9,14},{... | collective-permute-start | bytes 589832 | tf_op jit(solution)/shard_map/ppermute | solution.py:21
  261.4 9.0 %collective-permute-start.19 = (bf16[1,4,3,64,128]{4,3,2,1,0:T(8,128)(2,1)S(1)}, bf16[1,4,3,64,128]{4,3,2,1,0:T(8,128)(2,1)S(1)}, u32[]{:S(2)}, u32[]{:S(2)}) collective-permute-start(bf16[1,4,3,64,128]{4,3,2,1,0:T(8,128)(2,1)S(1)} %fusion.84), channel_id=1, source_target_pairs={{0,2},{1,3},{2,4},{3,5},{4,6},{5,7},{6,8},{7,9},{8,10},{9,11},{10,... | collective-permute-start | bytes 589832 | tf_op jit(solution)/shard_map/ppermute | solution.py:21
  270.4 9.2 %collective-permute-start.20 = (bf16[1,4,3,64,128]{4,3,2,1,0:T(8,128)(2,1)S(1)}, bf16[1,4,3,64,128]{4,3,2,1,0:T(8,128)(2,1)S(1)}, u32[]{:S(2)}, u32[]{:S(2)}) collective-permute-start(bf16[1,4,3,64,128]{4,3,2,1,0:T(8,128)(2,1)S(1)} %fusion.84), channel_id=1, source_target_pairs={{0,1},{1,2},{2,3},{3,4},{4,5},{5,6},{6,7},{7,8},{8,9},{9,10},{10,1... | collective-permute-start | bytes 589832 | tf_op jit(solution)/shard_map/ppermute | solution.py:21
  279.6 9.5 %collective-permute-start.21 = (bf16[1,4,3,64,128]{4,3,2,1,0:T(8,128)(2,1)S(1)}, bf16[1,4,3,64,128]{4,3,2,1,0:T(8,128)(2,1)S(1)}, u32[]{:S(2)}, u32[]{:S(2)}) collective-permute-start(bf16[1,4,3,64,128]{4,3,2,1,0:T(8,128)(2,1)S(1)} %fusion.84), channel_id=1, source_target_pairs={{1,0},{2,1},{3,2},{4,3},{5,4},{6,5},{7,6},{8,7},{9,8},{10,9},{11,1... | collective-permute-start | bytes 589832 | tf_op jit(solution)/shard_map/ppermute | solution.py:21
  297.7 9.0 %collective-permute-start.23 = (bf16[1,4,3,64,128]{4,3,2,1,0:T(8,128)(2,1)S(1)}, bf16[1,4,3,64,128]{4,3,2,1,0:T(8,128)(2,1)S(1)}, u32[]{:S(2)}, u32[]{:S(2)}) collective-permute-start(bf16[1,4,3,64,128]{4,3,2,1,0:T(8,128)(2,1)S(1)} %fusion.84), channel_id=1, source_target_pairs={{3,0},{4,1},{5,2},{6,3},{7,4},{8,5},{9,6},{10,7},{11,8},{12,9},{13... | collective-permute-start | bytes 589832 | tf_op jit(solution)/shard_map/ppermute | solution.py:21
  (26 other events, 291.0 us)
Sparse Core Ops, SparseCore 0:
  186.4 126.0 all-reduce.3
where the time goes:
time: 378 us; the launch traced here: 374 us
  other arithmetic  110 us (29%)
  starting transfers between devices  90.5 us (24%)
  waiting for transfers between devices  61.5 us (16%)
  blocking collectives  39.7 us (11%)
  local copies, waits for them, and re-layouts  37.5 us (10%)
  matrix products  19.2 us (5%)
  between operations  15.2 us (4%)
    ppermute x28, starting transfers between devices, shifted(): return lax.ppermute(value, axis, pairs)  90.5 us
    ppermute x28, waiting for transfers between devices, shifted(): return lax.ppermute(value, axis, pairs)  61.5 us
    mul x1, other arithmetic, per_device(): d_fields = mask_float * (signal + back)  41.5 us
    psum x1, blocking collectives, per_device(): lax.psum((partials[0] * grad_scale, partials[1] * grad_scale, partials[2]...  39.7 us
    unnamed x65, local copies, waits for them, and re-layouts  24.3 us
    reduce_sum x3, other arithmetic, kernel_grad(): cols_list.append(jnp.sum(window * d_conv, axis=(0, 1, 2)))  17.6 us
    reduce_sum x1, other arithmetic, block_core(): mean_part = jnp.mean(conv, axis=-1, keepdims=True)  16.8 us
    unnamed x15, other arithmetic  11.7 us
  transfers between devices with their start and end apart: 29, of which 14 were waited for; matrix products, arithmetic and copies ran while one was open for 20% of the time, Pallas kernels for 0%

commit v1 on v0

--- a/solution.py
+++ b/solution.py
@@ -4,21 +4,12 @@
 import jax.numpy as jnp
 from jax import lax
 from jax.sharding import PartitionSpec as P
-
-REACH = 7
-
 
 EPS = 1e-06
 GELU_K = 0.7978845608028654
 GELU_C = 0.044715
 CONTRACT_LAST = (((1,), (1,)), ((), ()))
 CONTRACT_ROWS = (((0,), (0,)), ((), ()))
-
-
-def shifted(value, axis, by):
-    peers = lax.axis_size(axis)
-    pairs = [(i, i + by) for i in range(peers) if 0 <= i + by < peers]
-    return lax.ppermute(value, axis, pairs)
 
 
 def gelu_parts(hidden):
@@ -82,14 +73,14 @@
 
 def assemble(middle, picked, radius):
     extent = middle.shape[1]
-    top_mid = picked[:, 0, 1]
-    bottom_mid = picked[:, 1, 0]
-    left_mid = jnp.swapaxes(picked[:, 2, 3], 1, 2)
-    right_mid = jnp.swapaxes(picked[:, 3, 2], 1, 2)
-    north_west = picked[:, 4, 1, :, extent - radius :]
-    north_east = picked[:, 5, 1, :, :radius]
-    south_west = picked[:, 6, 0, :, extent - radius :]
-    south_east = picked[:, 7, 0, :, :radius]
+    top_mid = picked[:, 0]
+    bottom_mid = picked[:, 1]
+    left_mid = jnp.swapaxes(picked[:, 2], 1, 2)
+    right_mid = jnp.swapaxes(picked[:, 3], 1, 2)
+    north_west = picked[:, 4, :, extent - radius :]
+    north_east = picked[:, 5, :, :radius]
+    south_west = picked[:, 6, :, extent - radius :]
+    south_east = picked[:, 7, :, :radius]
     upper = jnp.concatenate([north_west, top_mid, north_east], axis=2)
     centre_band = jnp.concatenate([left_mid, middle, right_mid], axis=2)
     lower = jnp.concatenate([south_west, bottom_mid, south_east], axis=2)
@@ -122,14 +113,65 @@
     return jnp.stack(rows_list)
 
 
-def direct_pool(stacks, mover):
-    pieces = []
-    for offset in range(-REACH, REACH + 1):
-        if offset == 0:
-            pieces.append(stacks)
-        else:
-            pieces.append(mover(stacks, -offset))
-    return jnp.concatenate(pieces, axis=0)
+GROUP = 8
+STRIP_FOR = (1, 0, 3, 2, 1, 1, 0, 0)
+OPPOSITE = (1, 0, 3, 2, 7, 6, 5, 4)
+
+
+def halo_maps(neighbours):
+    peers = lax.axis_size("tiles")
+    device = lax.axis_index("tiles")
+    group = device // GROUP
+    place = device % GROUP
+    mine = neighbours[0]
+    below = lax.ppermute(mine, "tiles", [(i, i + GROUP) for i in range(peers - GROUP)])
+    above = lax.ppermute(mine, "tiles", [(i + GROUP, i) for i in range(peers - GROUP)])
+    dest = jnp.arange(GROUP, dtype=jnp.int32)
+    strip_of_side = jnp.array([STRIP_FOR[OPPOSITE[side]] for side in range(8)], jnp.int32)
+
+    def strip_to(listing):
+        hit = listing[None, :] == (group * GROUP + dest)[:, None]
+        return jnp.sum(jnp.where(hit, strip_of_side[None, :], 0), axis=1)
+
+    own = strip_to(mine)
+    relayed = jnp.where(dest < place, 4 + strip_to(below), 8 + strip_to(above))
+    send_index = jnp.stack([own, relayed], axis=1).reshape(-1)
+    listed = mine >= 0
+    slot = jnp.where(listed, (mine % GROUP) * 2 + (mine // GROUP != group), 0)
+    return send_index, slot, listed
+
+
+def exchange(strips, maps):
+    send_index, slot, listed = maps
+    peers = lax.axis_size("tiles")
+    below = lax.ppermute(strips, "tiles", [(i, i + GROUP) for i in range(peers - GROUP)])
+    above = lax.ppermute(strips, "tiles", [(i + GROUP, i) for i in range(peers - GROUP)])
+    table = jnp.concatenate([strips, below, above], axis=0)
+    blocks = jnp.take(table, send_index, axis=0, mode="clip")
+    blocks = blocks.reshape((GROUP, 2) + strips.shape[1:])
+    groups = [list(range(g, g + GROUP)) for g in range(0, peers, GROUP)]
+    arrived = lax.all_to_all(blocks, "tiles", 0, 0, axis_index_groups=groups)
+    arrived = arrived.reshape((GROUP * 2,) + strips.shape[1:])
+    chosen = jnp.take(arrived, slot, axis=0, mode="clip")
+    return jnp.where(listed[:, None, None, None], chosen, jnp.zeros_like(chosen))
+
+
+def sum_over_tiles(parts):
+    peers = lax.axis_size("tiles")
+    flat = jnp.concatenate([part.reshape(-1, 128) for part in parts], axis=0)
+    rows = flat.shape[0]
+    block = -(-rows // (peers * 8)) * 8
+    flat = jnp.pad(flat, ((0, peers * block - rows), (0, 0))).reshape(peers, block, 128)
+    summed = jnp.sum(lax.all_to_all(flat, "tiles", 0, 0), axis=0)
+    shared = jnp.broadcast_to(summed.astype(jnp.bfloat16)[None], (peers, block, 128))
+    total = lax.all_to_all(shared, "tiles", 0, 0).reshape(-1, 128).astype(jnp.float32)
+    out = []
+    at = 0
+    for part in parts:
+        size = part.size // 128
+        out.append(total[at : at + size].reshape(part.shape))
+        at += size
+    return out
 
 
 def per_device(
@@ -152,24 +194,12 @@
     channels = fields.shape[3]
     ksize = kernel.shape[0]
     radius = ksize // 2
-    device = lax.axis_index("tiles")
     mask_float = ocean_mask.astype(jnp.float32)[..., None]
     masked = (fields.astype(jnp.float32) * mask_float).astype(jnp.bfloat16)
-    listed = neighbours >= 0
-    owner_dev = neighbours // tile_count
-    pool_slot = jnp.where(
-        listed, (owner_dev - device + REACH) * tile_count + neighbours % tile_count, 0
-    )
-
-    def pick(rim_pool):
-        chosen = jnp.take(rim_pool, pool_slot, axis=0)
-        keep = listed[:, :, None, None, None, None]
-        return jnp.where(keep, chosen, jnp.zeros_like(chosen))
-
+    maps = halo_maps(neighbours)
     signal = cotangent.astype(jnp.float32) * mask_float
-    strips = frame_strips(masked, radius)
-    rim_pool = direct_pool(strips, lambda stack, offset: shifted(stack, "tiles", offset))
-    padded = assemble(masked, pick(rim_pool), radius).astype(jnp.float32)
+    received = exchange(frame_strips(masked, radius)[0], maps)[None]
+    padded = assemble(masked, received, radius).astype(jnp.float32)
     conv = depthwise(padded, kernel) + conv_bias
     branch, d_conv, partials = block_core(
         conv.reshape(-1, channels),
@@ -190,31 +220,13 @@
     kernel_part = kernel_grad(padded, d_conv, ksize)
     bias_part = jnp.sum(d_conv, axis=(0, 1, 2))
     flipped = kernel[::-1, ::-1]
-    outgoing = frame_strips(d_conv, radius)
-    back_pool = direct_pool(
-        outgoing,
-        lambda stack, offset: shifted(stack.astype(jnp.bfloat16), "tiles", offset).astype(
-            stack.dtype
-        ),
-    )
-    received = pick(back_pool)
+    outgoing = frame_strips(d_conv, radius)[0].astype(jnp.bfloat16)
+    received = exchange(outgoing, maps)[None].astype(jnp.float32)
     back = depthwise(assemble(d_conv, received, radius), flipped)
     d_fields = mask_float * (signal + back)
     grad_scale = 1.0 / math.sqrt(lax.axis_size("tiles") * tile_count * tile_side * tile_side)
-    totals = lax.psum(
-        (
-            partials[0] * grad_scale,
-            partials[1] * grad_scale,
-            partials[2] * grad_scale,
-            partials[3] * grad_scale,
-            partials[4] * grad_scale,
-            partials[5] * grad_scale,
-            partials[6] * grad_scale,
-            kernel_part * grad_scale,
-            bias_part * grad_scale,
-        ),
-        "tiles",
-    )
+    scaled = [piece * grad_scale for piece in partials + (kernel_part, bias_part)]
+    totals = sum_over_tiles(scaled)
     return (
         updated,
         d_fields,

time: 378 us -> 208 us (0.55)
  the two profiles are of different devices: /device:TPU:15 before, /device:TPU:0 now
where the time goes in v1:
time: 208 us; the launch traced here: 207 us
  other arithmetic  96 us (46%)
  starting transfers between devices  35.5 us (17%)
  waiting for transfers between devices  34.4 us (17%)
  local copies, waits for them, and re-layouts  20 us (10%)
  matrix products  18.6 us (9%)
  between operations  2.6 us (1%)
    mul x1, other arithmetic, per_device(): d_fields = mask_float * (signal + back)  38.1 us
    all_to_all x2, waiting for transfers between devices, exchange(): arrived = lax.all_to_all(blocks, 'tiles', 0, 0, axis_index_groups=groups)  18.5 us
    reduce_sum x1, other arithmetic, block_core(): mean_part = jnp.mean(conv, axis=-1, keepdims=True)  15.6 us
    reduce_sum x3, other arithmetic, kernel_grad(): cols_list.append(jnp.sum(window * d_conv, axis=(0, 1, 2)))  15.3 us
    all_to_all x1, waiting for transfers between devices, sum_over_tiles(): summed = jnp.sum(lax.all_to_all(flat, 'tiles', 0, 0), axis=0)  10.7 us
    ppermute x2, starting transfers between devices, exchange(): lax.ppermute(strips, 'tiles', [(i, i + GROUP) for i in range(peers - GROU...  10.2 us
    all_to_all x2, starting transfers between devices, exchange(): arrived = lax.all_to_all(blocks, 'tiles', 0, 0, axis_index_groups=groups)  7.54 us
    dot_general x1, matrix products, block_core(): lax.dot_general(branch_low, weight_out, CONTRACT_LAST, preferred_element_...  6.82 us
  transfers between devices with their start and end apart: 10, of which 6 were waited for; matrix products, arithmetic and copies ran while one was open for 28% of the time, Pallas kernels for 0%

profile of v1, /device:TPU:0, one launch (start us, length us, event | category | flops | bytes accessed | tf_op | source)
XLA Modules:
  0.0 207.1 jit_solution(18242944031214415874)
XLA Ops:
  0.7 5.1 %collective-permute-start.2 = (s32[8]{0:T(128)}, s32[8]{0:T(128)S(1)}, u32[]{:S(2)}, u32[]{:S(2)}) collective-permute-start(s32[8]{0:T(128)} %bitcast.437), channel_id=1, source_target_pairs={{0,8},{1,9},{2,10},{3,11},{4,12},{5,13},{6,14},{7,15},{8,16},{9,17... | collective-permute-start | bytes 104 | tf_op jit(solution)/shard_map/ppermute | solution.py:127
  12.2 5.2 %collective-permute-start = (bf16[4,3,64,128]{3,1,2,0:T(4,128)(2,1)S(1)}, bf16[4,3,64,128]{3,1,2,0:T(4,128)(2,1)S(1)}, u32[]{:S(2)}, u32[]{:S(2)}) collective-permute-start(bf16[4,3,64,128]{3,1,2,0:T(4,128)(2,1)S(1)} %maximum_bitcast_fusion), channel_id=1, source_target_pairs={{0,8},{1,9},{2,10},{3,11},{4,12},{5,13},{6,14},{7,15},{8,16},{9,17... | collective-permute-start | bytes 589832 | tf_op jit(solution)/shard_map/ppermute | solution.py:147
  18.4 2.8 %collective-permute-done.1 = bf16[4,3,64,128]{3,1,2,0:T(4,128)(2,1)S(1)} collective-permute-done((bf16[4,3,64,128]{3,1,2,0:T(4,128)(2,1)S(1)}, bf16[4,3,64,128]{3,1,2,0:T(4,128)(2,1)S(1)}, u32[]{:S(2)}, u32[]{:S(2)}) %collective-permute-start.1) | collective-permute-done | bytes 196640 | tf_op jit(solution)/shard_map/ppermute | solution.py:148
  25.5 3.7 %all-to-all-start = ((bf16[8,2,3,64,128]{4,3,2,1,0:T(8,128)(2,1)}), bf16[8,2,3,64,128]{4,3,2,1,0:T(8,128)(2,1)S(1)}, u32[]{:S(2)}, u32[]{:S(2)}) async-start(bf16[8,2,3,64,128]{4,3,2,1,0:T(8,128)(2,1)} %copy.52), calls=%async_computation | async-start | bytes 1572864 | tf_op jit(solution)/shard_map/all_to_all | solution.py:153
  30.3 11.5 %all-to-all-done = bf16[8,2,3,64,128]{4,3,2,1,0:T(8,128)(2,1)S(1)} async-done(((bf16[8,2,3,64,128]{4,3,2,1,0:T(8,128)(2,1)}), bf16[8,2,3,64,128]{4,3,2,1,0:T(8,128)(2,1)S(1)}, u32[]{:S(2)}, u32[]{:S(2)}) %all-to-all-start) | async-done | bytes 786464 | tf_op jit(solution)/shard_map/all_to_all | solution.py:153
  45.6 15.6 %fusion.83 = (f32[64,64]{1,0:T(8,128)S(1)}, f32[1,64,64,128]{3,2,1,0:T(8,128)}) fusion(f32[128]{0:T(128)S(1)} %copy-done.98, f32[128]{0:T(128)S(1)} %get-tuple-element.156, f32[1,70,70,128]{3,2,1,0:T(8,128)S(1)} %maximum_convert_fusion, f32[128]{0:T(128)S(1)} %get-tuple-element.157, f32[128]{0:T(128)S(1)} %get-tuple-element.110, ...), kind=kLoop, calls=%fused_computation.330 | loop fusion | flops 51900416 | bytes 104899584 | tf_op jit(solution)/shard_map/reduce_sum | solution.py:28
  61.3 2.5 %multiply_reduce_fusion.52 = f32[64,64]{1,0:T(8,128)S(1)} fusion(f32[1,64,64,128]{3,2,1,0:T(8,128)} %get-tuple-element.70, f32[64,64]{1,0:T(8,128)S(1)} %broadcast_multiply_fusion), kind=kLoop, calls=%fused_computation.196 | loop fusion | flops 1568768 | bytes 2129920 | tf_op jit(solution)/shard_map/reduce_sum | solution.py:30
  63.9 3.7 %add_convert_fusion = bf16[4096,128]{1,0:T(8,128)(2,1)S(1)} fusion(f32[1,64,64,128]{3,2,1,0:T(8,128)} %get-tuple-element.70, f32[128]{0:T(128)S(1)} %copy-done.94, f32[128]{0:T(128)S(1)} %copy-done.93, f32[4096]{0:T(1024)S(1)} %rsqrt.12, f32[4096]{0:T(1024)S(1)} %div.42), kind=kLoop, calls=%fused_computation.195 | loop fusion | flops 2621440 | bytes 3179520 | tf_op jit(solution)/shard_map/convert_element_type | solution.py:32
  67.7 3.3 %multiply_convert_fusion = (bf16[4096,512]{1,0:T(8,128)(2,1)S(1)}, f32[4096,512]{1,0:T(8,128)S(1)}) fusion(f32[512]{0:T(512)S(1)} %copy-done.99, bf16[4096,128]{1,0:T(8,128)(2,1)S(1)} %add_convert_fusion, bf16[128,512]{1,0:T(8,128)(2,1)S(1)} %copy-done), kind=kOutput, calls=%fused_computation.14 | convolution fusion | flops 557842432 | bytes 13764608 | tf_op jit(solution)/shard_map/dot_general | solution.py:33
  76.3 6.8 %fusion.87 = (f32[512]{0:T(512)}, bf16[4096,512]{1,0:T(8,128)(2,1)S(1)}) fusion(f32[4096,512]{1,0:T(8,128)S(1)} %get-tuple-element.159, f32[512]{0:T(512)S(1)} %copy-done.99, bf16[4096,128]{1,0:T(8,128)(2,1)S(1)} %get-tuple-element.74, bf16[512,128]{1,0:T(8,128)(2,1)S(1)} %copy-done.9), kind=kOutput, calls=%fused_computation.334 | convolution fusion | flops 580910592 | bytes 13766656 | tf_op jit(solution)/shard_map/dot_general | solution.py:39
  84.7 3.0 %multiply_reduce_fusion.49 = (f32[128]{0:T(128)S(1)}, f32[4096]{0:T(1024)S(1)}, f32[4096]{0:T(1024)S(1)}, f32[128]{0:T(128)}, f32[4096,128]{1,0:T(8,128)S(1)}) fusion(f32[1,64,64,128]{3,2,1,0:T(8,128)S(1)} %copy-done.2, f32[4096]{0:T(1024)S(1)} %rsqrt.12, f32[4096]{0:T(1024)S(1)} %div.42, f32[128]{0:T(128)S(1)} %copy-done.93, ...), kind=kOutput, calls=%fused_computation.185 | convolution fusion | flops 541581056 | bytes 8586752 | tf_op jit(solution)/shard_map/dot_general | solution.py:44
  87.8 3.2 %fusion.82 = (f32[128]{0:T(128)}, f32[4096,128]{1,0:T(8,128)S(1)}) fusion(f32[4096]{0:T(1024)S(1)} %broadcast_multiply_fusion.2, f32[4096]{0:T(1024)S(1)} %div.42, f32[1,64,64,128]{3,2,1,0:T(8,128)S(1)} %copy-done.2, f32[4096]{0:T(1024)S(1)} %broadcast_multiply_fusion.3, f32[4096,128]{1,0:T(8,128)S(1)} %get-tuple-element.160, f32[128]{0:T(128)S(1)} %copy-done.93, ...), kind=kLoop, calls=%fused_computation.329 | loop fusion | flops 4194176 | bytes 6358016 | tf_op jit(solution)/shard_map/reduce_sum | solution.py:221
  91.0 3.9 %multiply_reduce_fusion.36 = (f32[128]{0:T(128)}, f32[128]{0:T(128)}, f32[128]{0:T(128)}, f32[128]{0:T(128)}, f32[128]{0:T(128)}, /*index=5*/f32[128]{0:T(128)},...) fusion(f32[1,70,70,128]{3,2,1,0:T(8,128)S(1)} %maximum_convert_, ...), kind=kLoop, calls=%fused_computation.172 | loop fusion | flops 13629824 | bytes 29366784 | tf_op jit(solution)/shard_map/reduce_sum | solution.py:111
  94.9 5.6 %multiply_reduce_fusion = (f32[128]{0:T(128)S(1)}, f32[128]{0:T(128)S(1)}, f32[128]{0:T(128)}, f32[128]{0:T(128)}, f32[128]{0:T(128)}, /*index=5*/f32[128]{0:T(1...) fusion(f32[1,70,70,128]{3,2,1,0:T(8,128)S(1)} %maximum_convert_, ...), kind=kLoop, calls=%fused_computation.136 | loop fusion | flops 18872064 | bytes 39855104 | tf_op jit(solution)/shard_map/reduce_sum | solution.py:111
  100.5 5.8 %multiply_reduce_fusion.18 = (f32[128]{0:T(128)}, f32[128]{0:T(128)}, f32[128]{0:T(128)}, f32[128]{0:T(128)}, f32[128]{0:T(128)}, /*index=5*/f32[128]{0:T(128)},...) fusion(f32[1,70,70,128]{3,2,1,0:T(8,128)S(1)} %maximum_convert_, ...), kind=kLoop, calls=%fused_computation.154 | loop fusion | flops 18872064 | bytes 39855104 | tf_op jit(solution)/shard_map/reduce_sum | solution.py:111
  108.6 5.0 %collective-permute-start.4 = (bf16[4,3,64,128]{3,1,2,0:T(4,128)(2,1)S(1)}, bf16[4,3,64,128]{3,1,2,0:T(4,128)(2,1)S(1)}, u32[]{:S(2)}, u32[]{:S(2)}) collective-permute-start(bf16[4,3,64,128]{3,1,2,0:T(4,128)(2,1)S(1)} %maximum_bitcast_fusion.1), channel_id=1, source_target_pairs={{0,8},{1,9},{2,10},{3,11},{4,12},{5,13},{6,14},{7,15},{8,16},{9,17... | collective-permute-start | bytes 589832 | tf_op jit(solution)/shard_map/ppermute | solution.py:147
  120.6 3.8 %all-to-all-start.1 = ((bf16[8,2,3,64,128]{4,3,2,1,0:T(8,128)(2,1)}), bf16[8,2,3,64,128]{4,3,2,1,0:T(8,128)(2,1)S(1)}, u32[]{:S(2)}, u32[]{:S(2)}) async-start(bf16[8,2,3,64,128]{4,3,2,1,0:T(8,128)(2,1)} %copy.57), calls=%async_computation.1 | async-start | bytes 1572864 | tf_op jit(solution)/shard_map/all_to_all | solution.py:153
  124.5 3.5 %convolution_multiply_fusion = f32[512,128]{1,0:T(8,128)S(1)} fusion(bf16[4096,512]{1,0:T(8,128)(2,1)} %copy-done.3, bf16[4096,128]{1,0:T(8,128)(2,1)S(1)} %copy-done.8), kind=kOutput, calls=%fused_computation.202 | convolution fusion | flops 536936448 | bytes 5505024 | tf_op jit(solution)/shard_map/dot_general | solution.py:56
  129.9 7.0 %all-to-all-done.1 = bf16[8,2,3,64,128]{4,3,2,1,0:T(8,128)(2,1)S(1)} async-done(((bf16[8,2,3,64,128]{4,3,2,1,0:T(8,128)(2,1)}), bf16[8,2,3,64,128]{4,3,2,1,0:T(8,128)(2,1)S(1)}, u32[]{:S(2)}, u32[]{:S(2)}) %all-to-all-start.1) | async-done | bytes 786464 | tf_op jit(solution)/shard_map/all_to_all | solution.py:153
  136.9 5.3 %all-to-all-start.2 = ((f32[32,40,128]{2,1,0:T(8,128)}), f32[32,40,128]{2,1,0:T(8,128)S(1)}, u32[]{:S(2)}, u32[]{:S(2)}) async-start(f32[32,40,128]{2,1,0:T(8,128)} %bitcast.164), calls=%async_computation.2 | async-start | bytes 1310720 | tf_op jit(solution)/shard_map/all_to_all | solution.py:165
  143.8 5.6 %maximum_maximum_fusion = (f32[1,67,70,128]{3,2,1,0:T(8,128)S(1)}, f32[1,67,70,128]{3,2,1,0:T(8,128)}) fusion(f32[1,64,3,128]{3,2,1,0:T(4,128)S(1)} %copy.59, f32[1,64,64,128]{3,2,1,0:T(8,128)} %bitcast.379, f32[1,64,3,128]{3,2,1,0:T(4,128)S(1)} %copy.58, f32[1,3,3,128]{3,2,1,0:T(4,128)S(1)} %get-tuple-element.88, ...), kind=kLoop, calls=%fused_computation.20 | loop fusion | flops 6003200 | bytes 7311360 | tf_op jit(solution)/shard_map/concatenate | solution.py:87
  149.4 10.7 %all-to-all-done.2 = f32[32,40,128]{2,1,0:T(8,128)S(1)} async-done(((f32[32,40,128]{2,1,0:T(8,128)}), f32[32,40,128]{2,1,0:T(8,128)S(1)}, u32[]{:S(2)}, u32[]{:S(2)}) %all-to-all-start.2) | async-done | bytes 655392 | tf_op jit(solution)/shard_map/all_to_all | solution.py:165
  162.2 3.5 %all-to-all-start.3 = ((bf16[32,40,128]{2,1,0:T(8,128)(2,1)}), bf16[32,40,128]{2,1,0:T(8,128)(2,1)S(1)}, u32[]{:S(2)}, u32[]{:S(2)}) async-start(bf16[32,40,128]{2,1,0:T(8,128)(2,1)} %broadcast_in_dim.47), calls=%async_computation.3 | async-start | bytes 655360 | tf_op jit(solution)/shard_map/all_to_all | solution.py:167
  165.7 38.1 %fusion.45 = f32[1,64,64,128]{3,2,1,0:T(8,128)} fusion(f32[1,67,70,128]{3,2,1,0:T(8,128)} %get-tuple-element.72, f32[1,64,3,128]{3,2,1,0:T(4,128)S(1)} %copy.59, f32[1,64,64,128]{3,2,1,0:T(8,128)} %bitcast.380, f32[1,64,3,128]{3,2,1,0:T(4,128)S(1)} %copy.58, f32[1,67,70,128]{3,2,1,0:T(8,128)S(1)} %get-tuple-element.71, f32[128]{0:T(128)} %copy-done.19, ...), kind=kLoop, calls=%fused_computation.64 | loop fusion | flops 56098816 | bytes 93561344 | tf_op jit(solution)/shard_map/mul | solution.py:226
  (297 shorter events, 40.4 us)
Async XLA Ops:
  0.6 67.0 %copy-start = (bf16[128,512]{1,0:T(8,128)(2,1)S(1)}, bf16[128,512]{1,0:T(8,128)(2,1)}, u32[]{:S(2)}) copy-start(bf16[128,512]{1,0:T(8,128)(2,1)} %param.22) | copy-start | bytes 393220
  0.7 17.4 %copy-start.96 = (s32[8]{0:T(128)S(1)}, s32[8]{0:T(128)}, u32[]{:S(2)}) copy-start(s32[8]{0:T(128)} %constant.85.clone) | copy-start | bytes 100
  0.7 16.8 %copy-start.95 = (s32[1,8]{1,0:T(1,128)S(1)}, s32[1,8]{1,0:T(1,128)}, u32[]{:S(2)}) copy-start(s32[1,8]{1,0:T(1,128)} %param.17) | copy-start | bytes 100
  0.7 17.3 %collective-permute-start.2 = (s32[8]{0:T(128)}, s32[8]{0:T(128)S(1)}, u32[]{:S(2)}, u32[]{:S(2)}) collective-permute-start(s32[8]{0:T(128)} %bitcast.437), channel_id=1, source_target_pairs={{0,8},{1,9},{2,10},{3,11},{4,12},{5,13},{6,14},{7,15},{8,16},{9,17... | collective-permute-start | bytes 104 | tf_op jit(solution)/shard_map/ppermute | solution.py:127
  5.7 12.3 %collective-permute-start.3 = (s32[8]{0:T(128)}, s32[8]{0:T(128)S(1)}, u32[]{:S(2)}, u32[]{:S(2)}) collective-permute-start(s32[8]{0:T(128)} %bitcast.438), channel_id=1, source_target_pairs={{8,0},{9,1},{10,2},{11,3},{12,4},{13,5},{14,6},{15,7},{16,8},{17,9... | collective-permute-start | bytes 104 | tf_op jit(solution)/shard_map/ppermute | solution.py:128
  10.9 10.3 %collective-permute-start.1 = (bf16[4,3,64,128]{3,1,2,0:T(4,128)(2,1)S(1)}, bf16[4,3,64,128]{3,1,2,0:T(4,128)(2,1)S(1)}, u32[]{:S(2)}, u32[]{:S(2)}) collective-permute-start(bf16[4,3,64,128]{3,1,2,0:T(4,128)(2,1)S(1)} %maximum_bitcast_fusion), channel_id=1, source_target_pairs={{8,0},{9,1},{10,2},{11,3},{12,4},{13,5},{14,6},{15,7},{16,8},{17,9... | collective-permute-start | bytes 589832 | tf_op jit(solution)/shard_map/ppermute | solution.py:148
  12.2 10.2 %collective-permute-start = (bf16[4,3,64,128]{3,1,2,0:T(4,128)(2,1)S(1)}, bf16[4,3,64,128]{3,1,2,0:T(4,128)(2,1)S(1)}, u32[]{:S(2)}, u32[]{:S(2)}) collective-permute-start(bf16[4,3,64,128]{3,1,2,0:T(4,128)(2,1)S(1)} %maximum_bitcast_fusion), channel_id=1, source_target_pairs={{0,8},{1,9},{2,10},{3,11},{4,12},{5,13},{6,14},{7,15},{8,16},{9,17... | collective-permute-start | bytes 589832 | tf_op jit(solution)/shard_map/ppermute | solution.py:147
  25.5 16.3 %all-to-all-start = ((bf16[8,2,3,64,128]{4,3,2,1,0:T(8,128)(2,1)}), bf16[8,2,3,64,128]{4,3,2,1,0:T(8,128)(2,1)S(1)}, u32[]{:S(2)}, u32[]{:S(2)}) async-start(bf16[8,2,3,64,128]{4,3,2,1,0:T(8,128)(2,1)} %copy.52), calls=%async_computation | async-start | bytes 1572864 | tf_op jit(solution)/shard_map/all_to_all | solution.py:153
  29.3 15.9 %copy-start.11 = (f32[128]{0:T(128)}, f32[128]{0:T(128)S(1)}, u32[]{:S(2)}) copy-start(f32[128]{0:T(128)S(1)} %get-tuple-element.148) | copy-start | bytes 1540
  29.3 15.9 %copy-start.12 = (f32[128]{0:T(128)}, f32[128]{0:T(128)S(1)}, u32[]{:S(2)}) copy-start(f32[128]{0:T(128)S(1)} %get-tuple-element.149) | copy-start | bytes 1540
  29.3 15.9 %copy-start.13 = (f32[128]{0:T(128)}, f32[128]{0:T(128)S(1)}, u32[]{:S(2)}) copy-start(f32[128]{0:T(128)S(1)} %get-tuple-element.150) | copy-start | bytes 1540
  29.3 15.9 %copy-start.14 = (f32[128]{0:T(128)}, f32[128]{0:T(128)S(1)}, u32[]{:S(2)}) copy-start(f32[128]{0:T(128)S(1)} %get-tuple-element.151) | copy-start | bytes 1540
  29.3 15.9 %copy-start.15 = (f32[128]{0:T(128)}, f32[128]{0:T(128)S(1)}, u32[]{:S(2)}) copy-start(f32[128]{0:T(128)S(1)} %get-tuple-element.152) | copy-start | bytes 1540
  29.4 15.9 %copy-start.16 = (f32[128]{0:T(128)}, f32[128]{0:T(128)S(1)}, u32[]{:S(2)}) copy-start(f32[128]{0:T(128)S(1)} %get-tuple-element.153) | copy-start | bytes 1540
  29.4 15.9 %copy-start.17 = (f32[128]{0:T(128)}, f32[128]{0:T(128)S(1)}, u32[]{:S(2)}) copy-start(f32[128]{0:T(128)S(1)} %get-tuple-element.154) | copy-start | bytes 1540
  29.4 15.9 %copy-start.18 = (f32[128]{0:T(128)}, f32[128]{0:T(128)S(1)}, u32[]{:S(2)}) copy-start(f32[128]{0:T(128)S(1)} %get-tuple-element.155) | copy-start | bytes 1540
  29.4 15.9 %copy-start.19 = (f32[128]{0:T(128)}, f32[128]{0:T(128)S(1)}, u32[]{:S(2)}) copy-start(f32[128]{0:T(128)S(1)} %get-tuple-element.156) | copy-start | bytes 1540
  29.4 15.9 %copy-start.20 = (f32[128]{0:T(128)}, f32[128]{0:T(128)S(1)}, u32[]{:S(2)}) copy-start(f32[128]{0:T(128)S(1)} %get-tuple-element.157) | copy-start | bytes 1540
  29.4 15.9 %copy-start.21 = (f32[128]{0:T(128)}, f32[128]{0:T(128)S(1)}, u32[]{:S(2)}) copy-start(f32[128]{0:T(128)S(1)} %get-tuple-element.109) | copy-start | bytes 1540
  107.3 9.0 %collective-permute-start.5 = (bf16[4,3,64,128]{3,1,2,0:T(4,128)(2,1)S(1)}, bf16[4,3,64,128]{3,1,2,0:T(4,128)(2,1)S(1)}, u32[]{:S(2)}, u32[]{:S(2)}) collective-permute-start(bf16[4,3,64,128]{3,1,2,0:T(4,128)(2,1)S(1)} %maximum_bitcast_fusion.1), channel_id=1, source_target_pairs={{8,0},{9,1},{10,2},{11,3},{12,4},{13,5},{14,6},{15,7},{16,8},{17,9... | collective-permute-start | bytes 589832 | tf_op jit(solution)/shard_map/ppermute | solution.py:148
  108.6 8.9 %collective-permute-start.4 = (bf16[4,3,64,128]{3,1,2,0:T(4,128)(2,1)S(1)}, bf16[4,3,64,128]{3,1,2,0:T(4,128)(2,1)S(1)}, u32[]{:S(2)}, u32[]{:S(2)}) collective-permute-start(bf16[4,3,64,128]{3,1,2,0:T(4,128)(2,1)S(1)} %maximum_bitcast_fusion.1), channel_id=1, source_target_pairs={{0,8},{1,9},{2,10},{3,11},{4,12},{5,13},{6,14},{7,15},{8,16},{9,17... | collective-permute-start | bytes 589832 | tf_op jit(solution)/shard_map/ppermute | solution.py:147
  120.6 16.3 %all-to-all-start.1 = ((bf16[8,2,3,64,128]{4,3,2,1,0:T(8,128)(2,1)}), bf16[8,2,3,64,128]{4,3,2,1,0:T(8,128)(2,1)S(1)}, u32[]{:S(2)}, u32[]{:S(2)}) async-start(bf16[8,2,3,64,128]{4,3,2,1,0:T(8,128)(2,1)} %copy.57), calls=%async_computation.1 | async-start | bytes 1572864 | tf_op jit(solution)/shard_map/all_to_all | solution.py:153
  136.9 23.2 %all-to-all-start.2 = ((f32[32,40,128]{2,1,0:T(8,128)}), f32[32,40,128]{2,1,0:T(8,128)S(1)}, u32[]{:S(2)}, u32[]{:S(2)}) async-start(f32[32,40,128]{2,1,0:T(8,128)} %bitcast.164), calls=%async_computation.2 | async-start | bytes 1310720 | tf_op jit(solution)/shard_map/all_to_all | solution.py:165
  162.2 41.6 %all-to-all-start.3 = ((bf16[32,40,128]{2,1,0:T(8,128)(2,1)}), bf16[32,40,128]{2,1,0:T(8,128)(2,1)S(1)}, u32[]{:S(2)}, u32[]{:S(2)}) async-start(bf16[32,40,128]{2,1,0:T(8,128)(2,1)} %broadcast_in_dim.47), calls=%async_computation.3 | async-start | bytes 655360 | tf_op jit(solution)/shard_map/all_to_all | solution.py:167
  (86 other events, 845.9 us)

commit v2 on v1

v2 whole, which is shorter than its diff:
```python
import math

import jax
import jax.numpy as jnp
from jax import lax
from jax.experimental import pallas as pl
from jax.experimental.pallas import tpu as pltpu
from jax.sharding import PartitionSpec as P

EPS = 1e-06
GELU_K = 0.7978845608028654
GELU_C = 0.044715
CONTRACT_LAST = (((1,), (1,)), ((), ()))
CONTRACT_ROWS = (((0,), (0,)), ((), ()))


SIDE = 64
RADIUS = 3
TAPS = 7
PITCH = 72
ROWS = SIDE + 2 * RADIUS
PAIRS = ROWS // 2
BLOCK = 8
F32 = jnp.float32
BF16 = jnp.bfloat16


def tap_matrices(kernel):
    channels = kernel.shape[2]
    wide = jnp.pad(kernel, ((1, 1), (0, 0), (0, 0)))
    first = wide[1:9]
    second = wide[0:8]
    both = jnp.stack([first, second], axis=1).transpose(2, 0, 1, 3).astype(BF16)
    eye = jnp.eye(channels, dtype=BF16)
    spread = both[:, :, None, :, :] * eye[None, None, :, None, :]
    return spread.reshape(TAPS * 8 * channels, 2 * channels)


def place_strips(pick, padded, stage):
    for r in range(RADIUS):
        padded[r * PITCH + RADIUS : r * PITCH + RADIUS + SIDE, :] = pick(0, r)
        low = (RADIUS + SIDE + r) * PITCH
        padded[low + RADIUS : low + RADIUS + SIDE, :] = pick(1, r)
        padded[pl.ds(RADIUS * PITCH + r, SIDE, stride=PITCH), :] = pick(2, r)
        padded[pl.ds(RADIUS * PITCH + RADIUS + SIDE + r, SIDE, stride=PITCH), :] = pick(3, r)
        stage[0:SIDE, :] = pick(4, r)
        padded[r * PITCH : r * PITCH + RADIUS, :] = stage[SIDE - RADIUS : SIDE, :]
        stage[SIDE : 2 * SIDE, :] = pick(5, r)
        padded[r * PITCH + RADIUS + SIDE : r * PITCH + 2 * RADIUS + SIDE, :] = stage[SIDE : SIDE + RADIUS, :]
        stage[2 * SIDE : 3 * SIDE, :] = pick(6, r)
        padded[low : low + RADIUS, :] = stage[3 * SIDE - RADIUS : 3 * SIDE, :]
        stage[3 * SIDE : 4 * SIDE, :] = pick(7, r)
        padded[low + RADIUS + SIDE : low + 2 * RADIUS + SIDE, :] = stage[3 * SIDE : 3 * SIDE + RADIUS, :]


def shift_copies(padded, shifted):
    def body(pair, carry):
        for half in range(2):
            at = (2 * pair + half) * PITCH
            for tap in range(TAPS):
                row = padded[pl.ds(at + tap, SIDE), :].astype(BF16)
                shifted[tap, pair, :, half * 128 : (half + 1) * 128] = row
        return carry

    lax.fori_loop(0, PAIRS, body, 0)


def conv_block(shifted, taps, first, count):
    total = None
    for tap in range(TAPS):
        rows = [
            shifted[tap, pl.ds(first + move, count)].reshape(count * SIDE, 256) for move in range(4)
        ]
        part = jnp.dot(
            jnp.concatenate(rows, axis=1),
            taps[tap * 1024 : (tap + 1) * 1024, :],
            preferred_element_type=F32,
        )
        total = part if total is None else total + part
    return total


def picker(slot, listed, arrived):
    def pick(side, r):
        value = arrived[slot[side], r].astype(F32)
        return jnp.where(listed[side] > 0, value, 0.0)

    return pick


def core_body(
    slot, listed, fields, arrived, cotangent, mask, taps, conv_bias, ln_gain, ln_bias, weight_in,
    bias_in, weight_out, bias_out, layer_scale,
    updated, d_conv, strips, padded, d_weight_in, d_weight_out, d_bias_in, small,
    shifted, stage,
):
    place_strips(picker(slot, listed, arrived), padded, stage)

    def fill(i, carry):
        padded[pl.ds((i + RADIUS) * PITCH + RADIUS, SIDE), :] = fields[i].astype(F32) * mask[i].astype(F32)
        return carry

    lax.fori_loop(0, SIDE, fill, 0)
    shift_copies(padded, shifted)
    d_weight_in[...] = jnp.zeros_like(d_weight_in)
    d_weight_out[...] = jnp.zeros_like(d_weight_out)
    d_bias_in[...] = jnp.zeros_like(d_bias_in)
    small[...] = jnp.zeros_like(small)
    d_conv[0:6] = jnp.zeros((6, SIDE, 128), F32)
    d_conv[SIDE + 6 : SIDE + 12] = jnp.zeros((6, SIDE, 128), F32)
    count = BLOCK // 2
    points = BLOCK * SIDE

    def by_half(ref, at):
        part = ref[pl.ds(at, BLOCK)].astype(F32).reshape(count, 2, SIDE, 128)
        return jnp.concatenate([part[:, 0], part[:, 1]], axis=0).reshape(points, 128)

    def by_row(value):
        part = value.reshape(2, count, SIDE, 128)
        return jnp.stack([part[0], part[1]], axis=1).reshape(BLOCK, SIDE, 128)

    def fold(value):
        return jnp.sum(value.reshape(-1, 8, value.shape[-1]), axis=0)

    def step(index, carry):
        at = index * BLOCK
        both = conv_block(shifted, taps, index * count, count)
        conv = jnp.concatenate([both[:, :128], both[:, 128:]], axis=0) + conv_bias[...]
        live = by_half(mask, at)
        signal = by_half(cotangent, at) * live
        centred = conv - jnp.mean(conv, axis=-1, keepdims=True)
        inv_std = lax.rsqrt(jnp.mean(centred * centred, axis=-1, keepdims=True) + EPS)
        normed = centred * inv_std
        lifted = (normed * ln_gain[...] + ln_bias[...]).astype(BF16)
        hidden = jnp.dot(lifted, weight_in[...], preferred_element_type=F32) + bias_in[...]
        square = hidden * hidden
        tanh_part = jnp.tanh(hidden * (GELU_K + GELU_K * GELU_C * square))
        half = 0.5 * hidden
        activated = (half + half * tanh_part).astype(BF16)
        slope = (0.5 + 0.5 * tanh_part) + half * (1.0 - tanh_part * tanh_part) * (
            GELU_K + 3.0 * GELU_K * GELU_C * square
        )
        branch = jnp.dot(activated, weight_out[...], preferred_element_type=F32) + bias_out[...]
        d_branch = signal * layer_scale[...]
        branch_low = d_branch.astype(BF16)
        d_hidden = slope * lax.dot_general(
            branch_low, weight_out[...], CONTRACT_LAST, preferred_element_type=F32
        )
        hidden_low = d_hidden.astype(BF16)
        d_lifted = lax.dot_general(
            hidden_low, weight_in[...], CONTRACT_LAST, preferred_element_type=F32
        )
        d_normed = d_lifted * ln_gain[...]
        d_out = inv_std * (
            d_normed
            - jnp.mean(d_normed, axis=-1, keepdims=True)
            - normed * jnp.mean(d_normed * normed, axis=-1, keepdims=True)
        )
        masked = by_half(fields, at) * live
        updated[pl.ds(at, BLOCK)] = by_row(live * (masked + layer_scale[...] * branch)).astype(BF16)
        d_conv[pl.ds(at + 6, BLOCK)] = by_row(d_out)
        d_weight_out[...] += lax.dot_general(
            branch_low, activated, CONTRACT_ROWS, preferred_element_type=F32
        )
        d_weight_in[...] += lax.dot_general(
            lifted, hidden_low, CONTRACT_ROWS, preferred_element_type=F32
        )
        d_bias_in[...] += fold(d_hidden)
        small[0:8] += fold(signal * branch)
        small[8:16] += fold(d_branch)
        small[16:24] += fold(d_lifted * normed)
        small[24:32] += fold(d_lifted)
        small[32:40] += fold(d_out)
        return carry

    lax.fori_loop(0, SIDE // BLOCK, step, 0)
    for r in range(RADIUS):
        strips[0, r] = d_conv[6 + r].astype(BF16)
        strips[1, r] = d_conv[6 + SIDE - RADIUS + r].astype(BF16)
        flat = d_conv.reshape((SIDE + 12) * SIDE, 128)
        strips[2, r] = flat[pl.ds(6 * SIDE + r, SIDE, stride=SIDE), :].astype(BF16)
        strips[3, r] = flat[pl.ds(7 * SIDE - RADIUS + r, SIDE, stride=SIDE), :].astype(BF16)


def kernel_grad_body(padded, d_conv, out):
    flat = d_conv.reshape((SIDE + 12) * SIDE, 128)
    for low, high in ((0, 4), (4, 7)):
        taps_here = high - low

        def column(block, sums, low=low, taps_here=taps_here):
            left = block * 8

            def row(i, state):
                sums, recent = state
                newest = flat[pl.ds(pl.multiple_of((i + 6 - low) * SIDE + left, 8), 8), :]
                window = (newest,) + recent
                new = []
                at = i * PITCH + left
                pieces = [padded[pl.ds(at + b, 8), :] for b in range(TAPS)]
                for a in range(taps_here):
                    for b in range(TAPS):
                        new.append(sums[a * TAPS + b] + pieces[b] * window[a])
                return tuple(new), window[:-1]

            start = tuple(
                flat[pl.ds(pl.multiple_of((5 - low - a) * SIDE + left, 8), 8), :]
                for a in range(taps_here - 1)
            )
            sums, _ = lax.fori_loop(0, ROWS, row, (sums, start), unroll=2)
            return sums

        zero = tuple(jnp.zeros((8, 128), F32) for _ in range(taps_here * TAPS))
        sums = lax.fori_loop(0, SIDE // 8, column, zero)
        for a in range(taps_here):
            for b in range(TAPS):
                at = (low + a) * TAPS + b
                out[at : at + 1, :] = jnp.sum(sums[a * TAPS + b], axis=0, keepdims=True)


def back_body(slot, listed, d_conv, arrived, cotangent, mask, taps, d_fields, padded, shifted, stage):
    place_strips(picker(slot, listed, arrived), padded, stage)

    def fill(i, carry):
        padded[pl.ds((i + RADIUS) * PITCH + RADIUS, SIDE), :] = d_conv[i + 6]
        return carry

    lax.fori_loop(0, SIDE, fill, 0)
    shift_copies(padded, shifted)
    count = BLOCK // 2

    def step(index, carry):
        at = index * BLOCK
        both = conv_block(shifted, taps, index * count, count).reshape(count, SIDE, 256)
        back = jnp.stack([both[:, :, :128], both[:, :, 128:]], axis=1).reshape(BLOCK, SIDE, 128)
        live = mask[pl.ds(at, BLOCK)].astype(F32)
        d_fields[pl.ds(at, BLOCK)] = live * (live * cotangent[pl.ds(at, BLOCK)].astype(F32) + back)
        return carry

    lax.fori_loop(0, SIDE // BLOCK, step, 0)


VMEM_BYTES = 60 * 1024 * 1024
IN_VMEM = pl.BlockSpec(memory_space=pltpu.VMEM)
IN_SMEM = pl.BlockSpec(memory_space=pltpu.SMEM)


def run_core(slot, listed, fields, arrived, cotangent, mask, taps, vectors, weights):
    conv_bias, ln_gain, ln_bias, bias_in, bias_out, layer_scale = vectors
    weight_in, weight_out = weights
    shape = jax.ShapeDtypeStruct
    return pl.pallas_call(
        core_body,
        out_shape=(
            shape((SIDE, SIDE, 128), BF16),
            shape((SIDE + 12, SIDE, 128), F32),
            shape((4, RADIUS, SIDE, 128), BF16),
            shape((ROWS * PITCH, 128), F32),
            shape((128, 512), F32),
            shape((128, 512), F32),
            shape((8, 512), F32),
            shape((40, 128), F32),
        ),
        in_specs=[IN_SMEM, IN_SMEM] + [IN_VMEM] * 13,
        out_specs=(IN_VMEM,) * 8,
        scratch_shapes=[
            pltpu.VMEM((TAPS, PAIRS, SIDE, 256), BF16),
            pltpu.VMEM((4 * SIDE, 128), F32),
        ],
        compiler_params=pltpu.CompilerParams(vmem_limit_bytes=VMEM_BYTES),
        name="core",
    )(slot, listed, fields, arrived, cotangent, mask, taps, conv_bias, ln_gain, ln_bias,
      weight_in, bias_in, weight_out, bias_out, layer_scale)


def run_kernel_grad(padded, d_conv):
    return pl.pallas_call(
        kernel_grad_body,
        out_shape=jax.ShapeDtypeStruct((56, 128), F32),
        in_specs=[IN_VMEM] * 2,
        out_specs=IN_VMEM,
        compiler_params=pltpu.CompilerParams(vmem_limit_bytes=VMEM_BYTES),
        cost_estimate=pl.CostEstimate(flops=80_000_000, bytes_accessed=5_000_000, transcendentals=0),
        name="kernel_grad",
    )(padded, d_conv)


def run_back(slot, listed, d_conv, arrived, cotangent, mask, taps):
    return pl.pallas_call(
        back_body,
        out_shape=jax.ShapeDtypeStruct((SIDE, SIDE, 128), F32),
        in_specs=[IN_SMEM, IN_SMEM] + [IN_VMEM] * 5,
        out_specs=IN_VMEM,
        scratch_shapes=[
            pltpu.VMEM((ROWS * PITCH, 128), F32),
            pltpu.VMEM((TAPS, PAIRS, SIDE, 256), BF16),
            pltpu.VMEM((4 * SIDE, 128), F32),
        ],
        compiler_params=pltpu.CompilerParams(vmem_limit_bytes=VMEM_BYTES),
        cost_estimate=pl.CostEstimate(flops=7_000_000_000, bytes_accessed=8_000_000, transcendentals=0),
        name="back",
    )(slot, listed, d_conv, arrived, cotangent, mask, taps)


def frame_strips(tile, radius):
    extent = tile.shape[0]
    left_cols = jnp.swapaxes(tile[:, :radius], 0, 1)
    right_cols = jnp.swapaxes(tile[:, extent - radius :], 0, 1)
    return jnp.stack([tile[:radius], tile[extent - radius :], left_cols, right_cols], axis=0)


GROUP = 8
STRIP_FOR = (1, 0, 3, 2, 1, 1, 0, 0)
OPPOSITE = (1, 0, 3, 2, 7, 6, 5, 4)


def halo_maps(neighbours):
    peers = lax.axis_size("tiles")
    device = lax.axis_index("tiles")
    group = device // GROUP
    place = device % GROUP
    mine = neighbours[0]
    below = lax.ppermute(mine, "tiles", [(i, i + GROUP) for i in range(peers - GROUP)])
    above = lax.ppermute(mine, "tiles", [(i + GROUP, i) for i in range(peers - GROUP)])
    dest = jnp.arange(GROUP, dtype=jnp.int32)
    strip_of_side = jnp.array([STRIP_FOR[OPPOSITE[side]] for side in range(8)], jnp.int32)

    def strip_to(listing):
        hit = listing[None, :] == (group * GROUP + dest)[:, None]
        return jnp.sum(jnp.where(hit, strip_of_side[None, :], 0), axis=1)

    own = strip_to(mine)
    relayed = jnp.where(dest < place, 4 + strip_to(below), 8 + strip_to(above))
    send_index = jnp.stack([own, relayed], axis=1).reshape(-1)
    listed = mine >= 0
    slot = jnp.where(listed, (mine % GROUP) * 2 + (mine // GROUP != group), 0)
    return send_index, slot.astype(jnp.int32), listed.astype(jnp.int32)


def exchange(strips, maps):
    send_index = maps[0]
    peers = lax.axis_size("tiles")
    below = lax.ppermute(strips, "tiles", [(i, i + GROUP) for i in range(peers - GROUP)])
    above = lax.ppermute(strips, "tiles", [(i + GROUP, i) for i in range(peers - GROUP)])
    table = jnp.concatenate([strips, below, above], axis=0)
    blocks = jnp.take(table, send_index, axis=0, mode="clip")
    blocks = blocks.reshape((GROUP, 2) + strips.shape[1:])
    groups = [list(range(g, g + GROUP)) for g in range(0, peers, GROUP)]
    arrived = lax.all_to_all(blocks, "tiles", 0, 0, axis_index_groups=groups)
    return arrived.reshape((GROUP * 2,) + strips.shape[1:])


def sum_over_tiles(parts):
    peers = lax.axis_size("tiles")
    flat = jnp.concatenate([part.reshape(-1, 128) for part in parts], axis=0)
    rows = flat.shape[0]
    block = -(-rows // (peers * 8)) * 8
    flat = jnp.pad(flat, ((0, peers * block - rows), (0, 0))).reshape(peers, block, 128)
    summed = jnp.sum(lax.all_to_all(flat, "tiles", 0, 0), axis=0)
    shared = jnp.broadcast_to(summed.astype(jnp.bfloat16)[None], (peers, block, 128))
    total = lax.all_to_all(shared, "tiles", 0, 0).reshape(-1, 128).astype(jnp.float32)
    out = []
    at = 0
    for part in parts:
        size = part.size // 128
        out.append(total[at : at + size].reshape(part.shape))
        at += size
    return out


def per_device(
    fields,
    cotangent,
    ocean_mask,
    neighbours,
    kernel,
    conv_bias,
    ln_gain,
    ln_bias,
    weight_in,
    bias_in,
    weight_out,
    bias_out,
    layer_scale,
):
    tile_count = fields.shape[0]
    tile_side = fields.shape[1]
    mask = jnp.broadcast_to(ocean_mask[0].astype(BF16)[..., None], fields.shape[1:])
    masked = fields[0] * mask
    maps = halo_maps(neighbours)
    slot, listed = maps[1], maps[2]
    arrived = exchange(frame_strips(masked, RADIUS), maps)
    vectors = [v.reshape(1, -1) for v in (conv_bias, ln_gain, ln_bias, bias_in, bias_out, layer_scale)]
    updated, d_conv, strips, padded, d_weight_in, d_weight_out, d_bias_in, small = run_core(
        slot, listed, fields[0], arrived, cotangent[0], mask, tap_matrices(kernel), vectors,
        (weight_in, weight_out),
    )
    arrived_back = exchange(strips, maps)
    d_kernel = run_kernel_grad(padded, d_conv)
    grad_scale = 1.0 / math.sqrt(lax.axis_size("tiles") * tile_count * tile_side * tile_side)
    small = jnp.sum(small.reshape(5, 8, 128), axis=1)
    parts = [d_weight_in, d_weight_out, jnp.sum(d_bias_in, axis=0), d_kernel[:49], small]
    totals = sum_over_tiles([part * grad_scale for part in parts])
    d_fields = run_back(
        slot, listed, d_conv, arrived_back, cotangent[0], mask, tap_matrices(kernel[::-1, ::-1])
    )
    t_in, t_out, t_bias_in, t_kernel, t_small = totals
    return (
        updated[None],
        d_fields[None],
        t_kernel.reshape(kernel.shape),
        t_small[4],
        t_small[2],
        t_small[3],
        t_in,
        t_bias_in,
        t_out.T,
        t_small[1],
        t_small[0],
    )


def solution(mesh):
    placed = (
        P("tiles", None, None, None),
        P("tiles", None, None, None),
        P("tiles", None, None),
        P("tiles", None),
        P(),
        P(),
        P(),
        P(),
        P(),
        P(),
        P(),
        P(),
        P(),
    )
    return jax.shard_map(
        per_device,
        mesh=mesh,
        in_specs=placed,
        out_specs=(
            P("tiles", None, None, None),
            P("tiles", None, None, None),
            P(),
            P(),
            P(),
            P(),
            P(),
            P(),
            P(),
            P(),
            P(),
        ),
        check_vma=False,
    )
```

time: 208 us -> 164 us (0.79)
  other arithmetic: 96 us -> 13.6 us
  Pallas kernels: 0 us -> 66.7 us
  matrix products: 18.6 us -> 0 us
  waiting for transfers between devices: 34.4 us -> 24.2 us
    pallas_call x0 -> x3, Pallas kernels: none -> 66.7 us  [the longest x1 35.5 us: run_core(): pl.pallas_call(core_body, out_shape=(shape((SIDE, SIDE, 128), BF16), shap...]
    reduce_sum x8 -> x2, other arithmetic: 38.9 us -> 1.53 us  [the longest x1 0.79 us: per_device(): jnp.sum(d_bias_in, axis=0)]
    mul x9 -> x7, other arithmetic: 39.5 us -> 9.55 us  [the longest x1 6.96 us: tap_matrices(): spread = both[:, :, None, :, :] * eye[None, None, :, None, :]]
    dot_general x6 -> x0, matrix products: 18.6 us -> none  [the longest x1 6.82 us: block_core(): lax.dot_general(branch_low, weight_out, CONTRACT_LAST, preferred_element_...]
    all_to_all x1, waiting for transfers between devices: 10.7 us -> 0.01 us  [sum_over_tiles(): summed = jnp.sum(lax.all_to_all(flat, 'tiles', 0, 0), axis=0)]
    ppermute x2, waiting for transfers between devices: 2.79 us -> 11.1 us  [exchange(): lax.ppermute(strips, 'tiles', [(i + GROUP, i) for i in range(peers - GROU...]
    all_to_all x2, waiting for transfers between devices: 18.5 us -> 10.5 us  [exchange(): arrived = lax.all_to_all(blocks, 'tiles', 0, 0, axis_index_groups=groups)]
    convert_element_type x5, other arithmetic: 8.28 us -> 1.31 us  [the longest x1 0.76 us: per_device(): ocean_mask[0].astype(BF16)[..., None]]
  transfers between devices with their start and end apart: 10 -> 10, of which waited for: 6 -> 4; matrix products, arithmetic and copies ran while one was open for 28% -> 13% of each run, Pallas kernels for 0% -> 10%
where the time goes in v2:
time: 164 us; the launch traced here: 163 us
  Pallas kernels  66.7 us (41%)
  starting transfers between devices  37.1 us (23%)
  waiting for transfers between devices  24.2 us (15%)
  local copies, waits for them, and re-layouts  20.2 us (12%)
  other arithmetic  13.6 us (8%)
    pallas_call x1, Pallas kernels, run_core(): pl.pallas_call(core_body, out_shape=(shape((SIDE, SIDE, 128), BF16), shap...  35.5 us
    pallas_call x1, Pallas kernels, run_back(): pl.pallas_call(back_body, out_shape=jax.ShapeDtypeStruct((SIDE, SIDE, 128...  15.7 us
    pallas_call x1, Pallas kernels, run_kernel_grad(): pl.pallas_call(kernel_grad_body, out_shape=jax.ShapeDtypeStruct((56, 128)...  15.5 us
    ppermute x2, waiting for transfers between devices, exchange(): lax.ppermute(strips, 'tiles', [(i + GROUP, i) for i in range(peers - GROU...  11.1 us
    all_to_all x2, waiting for transfers between devices, exchange(): arrived = lax.all_to_all(blocks, 'tiles', 0, 0, axis_index_groups=groups)  10.5 us
    ppermute x2, starting transfers between devices, exchange(): lax.ppermute(strips, 'tiles', [(i, i + GROUP) for i in range(peers - GROU...  9.75 us
    unnamed x22, local copies, waits for them, and re-layouts  7.85 us
    all_to_all x2, starting transfers between devices, exchange(): arrived = lax.all_to_all(blocks, 'tiles', 0, 0, axis_index_groups=groups)  7.34 us
  transfers between devices with their start and end apart: 10, of which 4 were waited for; matrix products, arithmetic and copies ran while one was open for 13% of the time, Pallas kernels for 10%

profile of v2, /device:TPU:0, one launch (start us, length us, event | category | flops | bytes accessed | tf_op | source)
XLA Modules:
  0.0 162.9 jit_solution(11549693567474967922)
XLA Ops:
  0.7 5.1 %collective-permute-start.2 = (s32[8]{0:T(128)}, s32[8]{0:T(128)S(1)}, u32[]{:S(2)}, u32[]{:S(2)}) collective-permute-start(s32[8]{0:T(128)} %bitcast.106), channel_id=1, source_target_pairs={{0,8},{1,9},{2,10},{3,11},{4,12},{5,13},{6,14},{7,15},{8,16},{9,17... | collective-permute-start | bytes 104 | tf_op jit(solution)/shard_map/ppermute | solution.py:322
  5.7 1.3 collective-permute-start.3
  7.8 1.7 %broadcast_multiply_fusion.2 = bf16[64,64,128]{2,1,0:T(8,128)(2,1)S(1)} fusion(bf16[64,64]{1,0:T(8,128)(2,1)S(1)} %convert_bitcast_fusion, bf16[1,64,64,128]{3,2,1,0:T(8,128)(2,1)} %param.14), kind=kLoop, calls=%fused_computation.7 | loop fusion | flops 524288 | bytes 2105344 | tf_op jit(solution)/shard_map/mul | solution.py:388
  10.0 1.3 collective-permute-start.1
  11.3 5.2 %collective-permute-start = (bf16[4,3,64,128]{3,1,2,0:T(4,128)(2,1)S(1)}, bf16[4,3,64,128]{3,1,2,0:T(4,128)(2,1)S(1)}, u32[]{:S(2)}, u32[]{:S(2)}) collective-permute-start(bf16[4,3,64,128]{3,1,2,0:T(4,128)(2,1)S(1)} %pad_maximum_fusion.1), channel_id=1, source_target_pairs={{0,8},{1,9},{2,10},{3,11},{4,12},{5,13},{6,14},{7,15},{8,16},{9,17... | collective-permute-start | bytes 589832 | tf_op jit(solution)/shard_map/ppermute | solution.py:342
  18.9 2.5 %collective-permute-done = bf16[4,3,64,128]{3,1,2,0:T(4,128)(2,1)S(1)} collective-permute-done((bf16[4,3,64,128]{3,1,2,0:T(4,128)(2,1)S(1)}, bf16[4,3,64,128]{3,1,2,0:T(4,128)(2,1)S(1)}, u32[]{:S(2)}, u32[]{:S(2)}) %collective-permute-start) | collective-permute-done | bytes 196640 | tf_op jit(solution)/shard_map/ppermute | solution.py:342
  21.7 1.4 gather_fusion
  24.2 3.7 %all-to-all-start = ((bf16[8,2,3,64,128]{4,3,2,1,0:T(8,128)(2,1)}), bf16[8,2,3,64,128]{4,3,2,1,0:T(8,128)(2,1)S(1)}, u32[]{:S(2)}, u32[]{:S(2)}) async-start(bf16[8,2,3,64,128]{4,3,2,1,0:T(8,128)(2,1)} %copy.48), calls=%async_computation | async-start | bytes 1572864 | tf_op jit(solution)/shard_map/all_to_all | solution.py:348
  28.0 7.0 %broadcast_multiply_fusion = (bf16[7,8,128,2,128]{4,3,2,1,0:T(2,128)(2,1)}, bf16[7,8,128,2,128]{4,3,2,1,0:T(2,128)(2,1)S(1)}) fusion(bf16[7,8,2,128]{3,2,1,0:T(2,128)(2,1)S(1)} %copy.50, bf16[128,128]{1,0:T(8,128)(2,1)S(1)} %fusion, bf16[7,8,2,128]{3,2,1,0:T(2,128)(2,1)S(1)} %copy.49), kind=kLoop, calls=%fused_computation.4 | loop fusion | flops 3670016 | bytes 7430144 | tf_op jit(solution)/shard_map/mul | solution.py:35
  34.9 2.3 %copy.65 = bf16[896,8,2,128]{3,1,2,0:T(8,128)(2,1)} copy(bf16[896,8,2,128]{3,2,1,0:T(2,128)(2,1)S(1)} %bitcast.90) | data formatting | bytes 7340032
  38.3 2.3 %all-to-all-done = bf16[8,2,3,64,128]{4,3,2,1,0:T(8,128)(2,1)S(1)} async-done(((bf16[8,2,3,64,128]{4,3,2,1,0:T(8,128)(2,1)}), bf16[8,2,3,64,128]{4,3,2,1,0:T(8,128)(2,1)S(1)}, u32[]{:S(2)}, u32[]{:S(2)}) %all-to-all-start) | async-done | bytes 786464 | tf_op jit(solution)/shard_map/all_to_all | solution.py:348
  40.6 1.6 %broadcast_in_dim.57.mask = bf16[64,64,128]{2,1,0:T(8,128)(2,1)} broadcast(bf16[64,64]{1,0:T(8,128)(2,1)S(1)} %convert_bitcast_fusion), dimensions={0,1} | broadcast | bytes 1056768 | tf_op jit(solution)/shard_map/broadcast_in_dim | solution.py:387
  42.2 35.5 %core.1 = (bf16[64,64,128]{2,1,0:T(8,128)(2,1)}, f32[76,64,128]{2,1,0:T(8,128)}, bf16[4,3,64,128]{3,2,1,0:T(8,128)(2,1)}, f32[5040,128]{1,0:T(8,128)}, f32[128,5...) custom-call(s32[8]{0:T(128)} %compare_select_fusion.4.slot, ...), custom_call_target="tpu_custom_call" | custom-call | tf_op jit(solution)/shard_map/core/pallas_call | solution.py:251
  79.3 15.5 %kernel_grad.1 = f32[56,128]{1,0:T(8,128)} custom-call(f32[5040,128]{1,0:T(8,128)} %get-tuple-element.25.padded, f32[76,64,128]{2,1,0:T(8,128)} %get-tuple-element.20.d_conv), custom_call_target="tpu_custom_call" | custom-call | flops 80000000 | bytes 5000000 | tf_op jit(solution)/shard_map/kernel_grad/pallas_call | solution.py:276
  96.8 5.1 %all-to-all-start.2 = ((f32[32,40,128]{2,1,0:T(8,128)}), f32[32,40,128]{2,1,0:T(8,128)S(1)}, u32[]{:S(2)}, u32[]{:S(2)}) async-start(f32[32,40,128]{2,1,0:T(8,128)} %bitcast.35), calls=%async_computation.2 | async-start | bytes 1310720 | tf_op jit(solution)/shard_map/all_to_all | solution.py:358
  102.0 1.3 collective-permute-start.5
  103.3 4.6 %collective-permute-start.4 = (bf16[4,3,64,128]{3,2,1,0:T(8,128)(2,1)S(1)}, bf16[4,3,64,128]{3,2,1,0:T(8,128)(2,1)S(1)}, u32[]{:S(2)}, u32[]{:S(2)}) collective-permute-start(bf16[4,3,64,128]{3,2,1,0:T(8,128)(2,1)S(1)} %copy-done.4), channel_id=1, source_target_pairs={{0,8},{1,9},{2,10},{3,11},{4,12},{5,13},{6,14},{7,15},{8,16},{9,17... | collective-permute-start | bytes 589832 | tf_op jit(solution)/shard_map/ppermute | solution.py:342
  107.8 11.1 %collective-permute-done.5 = bf16[4,3,64,128]{3,2,1,0:T(8,128)(2,1)S(1)} collective-permute-done((bf16[4,3,64,128]{3,2,1,0:T(8,128)(2,1)S(1)}, bf16[4,3,64,128]{3,2,1,0:T(8,128)(2,1)S(1)}, u32[]{:S(2)}, u32[]{:S(2)}) %collective-permute-start.5) | collective-permute-done | bytes 196640 | tf_op jit(solution)/shard_map/ppermute | solution.py:343
  119.0 1.5 gather_fusion.1
  120.6 3.6 %all-to-all-start.1 = ((bf16[8,2,3,64,128]{4,3,2,1,0:T(8,128)(2,1)}), bf16[8,2,3,64,128]{4,3,2,1,0:T(8,128)(2,1)S(1)}, u32[]{:S(2)}, u32[]{:S(2)}) async-start(bf16[8,2,3,64,128]{4,3,2,1,0:T(8,128)(2,1)} %bitcast.27), calls=%async_computation.1 | async-start | bytes 1572864 | tf_op jit(solution)/shard_map/all_to_all | solution.py:348
  124.2 4.3 %copy.64 = bf16[896,8,2,128]{3,1,2,0:T(8,128)(2,1)} copy(bf16[896,8,2,128]{3,2,1,0:T(2,128)(2,1)} %bitcast.88) | data formatting | bytes 7340032
  128.6 8.2 %all-to-all-done.1 = bf16[8,2,3,64,128]{4,3,2,1,0:T(8,128)(2,1)S(1)} async-done(((bf16[8,2,3,64,128]{4,3,2,1,0:T(8,128)(2,1)}), bf16[8,2,3,64,128]{4,3,2,1,0:T(8,128)(2,1)S(1)}, u32[]{:S(2)}, u32[]{:S(2)}) %all-to-all-start.1) | async-done | bytes 786464 | tf_op jit(solution)/shard_map/all_to_all | solution.py:348
  137.6 6.0 %all-to-all-start.3 = ((bf16[32,40,128]{2,1,0:T(8,128)(2,1)}), bf16[32,40,128]{2,1,0:T(8,128)(2,1)S(1)}, u32[]{:S(2)}, u32[]{:S(2)}) async-start(bf16[32,40,128]{2,1,0:T(8,128)(2,1)} %broadcast_in_dim.63), calls=%async_computation.3 | async-start | bytes 655360 | tf_op jit(solution)/shard_map/all_to_all | solution.py:360
  143.7 15.7 %back.1 = f32[64,64,128]{2,1,0:T(8,128)} custom-call(s32[8]{0:T(128)} %compare_select_fusion.4.slot, s32[8]{0:T(128)} %compare_convert_fusion.1.listed, f32[76,64,128]{2,1,0:T(8,128)} %get-tuple-element.20.d_conv, bf16[16,3,64,128]{3,2,1,0:T(8,128)(2,1)} %bitcast.98, bf16[64,64,128]{2,1,0:T(8,128)(2,1)} %bitcast.96, ...), custom_call_target="tpu_custom_call" | custom-call | flops 7000000000 | bytes 8000000 | tf_op jit(solution)/shard_map/back/pallas_call | solution.py:288
  (74 shorter events, 13.8 us)
Async XLA Ops:
  0.6 17.8 %copy-start.6 = (s32[8]{0:T(128)S(1)}, s32[8]{0:T(128)}, u32[]{:S(2)}) copy-start(s32[8]{0:T(128)} %constant.64.clone) | copy-start | bytes 100
  0.7 17.8 %copy-start.5 = (s32[1,8]{1,0:T(1,128)S(1)}, s32[1,8]{1,0:T(1,128)}, u32[]{:S(2)}) copy-start(s32[1,8]{1,0:T(1,128)} %param.17) | copy-start | bytes 100
  0.7 17.8 %collective-permute-start.2 = (s32[8]{0:T(128)}, s32[8]{0:T(128)S(1)}, u32[]{:S(2)}, u32[]{:S(2)}) collective-permute-start(s32[8]{0:T(128)} %bitcast.106), channel_id=1, source_target_pairs={{0,8},{1,9},{2,10},{3,11},{4,12},{5,13},{6,14},{7,15},{8,16},{9,17... | collective-permute-start | bytes 104 | tf_op jit(solution)/shard_map/ppermute | solution.py:322
  5.7 12.7 %collective-permute-start.3 = (s32[8]{0:T(128)}, s32[8]{0:T(128)S(1)}, u32[]{:S(2)}, u32[]{:S(2)}) collective-permute-start(s32[8]{0:T(128)} %bitcast.107), channel_id=1, source_target_pairs={{8,0},{9,1},{10,2},{11,3},{12,4},{13,5},{14,6},{15,7},{16,8},{17,9... | collective-permute-start | bytes 104 | tf_op jit(solution)/shard_map/ppermute | solution.py:323
  10.0 11.6 %collective-permute-start.1 = (bf16[4,3,64,128]{3,1,2,0:T(4,128)(2,1)S(1)}, bf16[4,3,64,128]{3,1,2,0:T(4,128)(2,1)S(1)}, u32[]{:S(2)}, u32[]{:S(2)}) collective-permute-start(bf16[4,3,64,128]{3,1,2,0:T(4,128)(2,1)S(1)} %pad_maximum_fusion.1), channel_id=1, source_target_pairs={{8,0},{9,1},{10,2},{11,3},{12,4},{13,5},{14,6},{15,7},{16,8},{17,9... | collective-permute-start | bytes 589832 | tf_op jit(solution)/shard_map/ppermute | solution.py:343
  11.3 10.2 %collective-permute-start = (bf16[4,3,64,128]{3,1,2,0:T(4,128)(2,1)S(1)}, bf16[4,3,64,128]{3,1,2,0:T(4,128)(2,1)S(1)}, u32[]{:S(2)}, u32[]{:S(2)}) collective-permute-start(bf16[4,3,64,128]{3,1,2,0:T(4,128)(2,1)S(1)} %pad_maximum_fusion.1), channel_id=1, source_target_pairs={{0,8},{1,9},{2,10},{3,11},{4,12},{5,13},{6,14},{7,15},{8,16},{9,17... | collective-permute-start | bytes 589832 | tf_op jit(solution)/shard_map/ppermute | solution.py:342
  24.2 16.3 %all-to-all-start = ((bf16[8,2,3,64,128]{4,3,2,1,0:T(8,128)(2,1)}), bf16[8,2,3,64,128]{4,3,2,1,0:T(8,128)(2,1)S(1)}, u32[]{:S(2)}, u32[]{:S(2)}) async-start(bf16[8,2,3,64,128]{4,3,2,1,0:T(8,128)(2,1)} %copy.48), calls=%async_computation | async-start | bytes 1572864 | tf_op jit(solution)/shard_map/all_to_all | solution.py:348
  40.6 1.6 %copy-start = (bf16[8,2,3,64,128]{4,3,2,1,0:T(8,128)(2,1)}, bf16[8,2,3,64,128]{4,3,2,1,0:T(8,128)(2,1)S(1)}, u32[]{:S(2)}) copy-start(bf16[8,2,3,64,128]{4,3,2,1,0:T(8,128)(2,1)S(1)} %all-to-all-done) | copy-start | bytes 2359300
  77.7 17.8 %copy-start.3 = (f32[128,512]{1,0:T(8,128)S(1)}, f32[128,512]{1,0:T(8,128)}, u32[]{:S(2)}) copy-start(f32[128,512]{1,0:T(8,128)} %get-tuple-element.22) | copy-start | bytes 786436
  77.7 17.9 %copy-start.2 = (f32[128,512]{1,0:T(8,128)S(1)}, f32[128,512]{1,0:T(8,128)}, u32[]{:S(2)}) copy-start(f32[128,512]{1,0:T(8,128)} %get-tuple-element.23) | copy-start | bytes 786436
  94.7 7.2 %copy-start.4 = (bf16[4,3,64,128]{3,2,1,0:T(8,128)(2,1)S(1)}, bf16[4,3,64,128]{3,2,1,0:T(8,128)(2,1)}, u32[]{:S(2)}) copy-start(bf16[4,3,64,128]{3,2,1,0:T(8,128)(2,1)} %get-tuple-element.21) | copy-start | bytes 589828
  96.8 23.7 %all-to-all-start.2 = ((f32[32,40,128]{2,1,0:T(8,128)}), f32[32,40,128]{2,1,0:T(8,128)S(1)}, u32[]{:S(2)}, u32[]{:S(2)}) async-start(f32[32,40,128]{2,1,0:T(8,128)} %bitcast.35), calls=%async_computation.2 | async-start | bytes 1310720 | tf_op jit(solution)/shard_map/all_to_all | solution.py:358
  102.0 17.0 %collective-permute-start.5 = (bf16[4,3,64,128]{3,2,1,0:T(8,128)(2,1)S(1)}, bf16[4,3,64,128]{3,2,1,0:T(8,128)(2,1)S(1)}, u32[]{:S(2)}, u32[]{:S(2)}) collective-permute-start(bf16[4,3,64,128]{3,2,1,0:T(8,128)(2,1)S(1)} %copy-done.4), channel_id=1, source_target_pairs={{8,0},{9,1},{10,2},{11,3},{12,4},{13,5},{14,6},{15,7},{16,8},{17,9... | collective-permute-start | bytes 589832 | tf_op jit(solution)/shard_map/ppermute | solution.py:343
  103.3 15.7 %collective-permute-start.4 = (bf16[4,3,64,128]{3,2,1,0:T(8,128)(2,1)S(1)}, bf16[4,3,64,128]{3,2,1,0:T(8,128)(2,1)S(1)}, u32[]{:S(2)}, u32[]{:S(2)}) collective-permute-start(bf16[4,3,64,128]{3,2,1,0:T(8,128)(2,1)S(1)} %copy-done.4), channel_id=1, source_target_pairs={{0,8},{1,9},{2,10},{3,11},{4,12},{5,13},{6,14},{7,15},{8,16},{9,17... | collective-permute-start | bytes 589832 | tf_op jit(solution)/shard_map/ppermute | solution.py:342
  120.6 16.2 %all-to-all-start.1 = ((bf16[8,2,3,64,128]{4,3,2,1,0:T(8,128)(2,1)}), bf16[8,2,3,64,128]{4,3,2,1,0:T(8,128)(2,1)S(1)}, u32[]{:S(2)}, u32[]{:S(2)}) async-start(bf16[8,2,3,64,128]{4,3,2,1,0:T(8,128)(2,1)} %bitcast.27), calls=%async_computation.1 | async-start | bytes 1572864 | tf_op jit(solution)/shard_map/all_to_all | solution.py:348
  136.8 6.9 %copy-start.1 = (bf16[8,2,3,64,128]{4,3,2,1,0:T(8,128)(2,1)}, bf16[8,2,3,64,128]{4,3,2,1,0:T(8,128)(2,1)S(1)}, u32[]{:S(2)}) copy-start(bf16[8,2,3,64,128]{4,3,2,1,0:T(8,128)(2,1)S(1)} %all-to-all-done.1) | copy-start | bytes 2359300
  137.6 21.8 %all-to-all-start.3 = ((bf16[32,40,128]{2,1,0:T(8,128)(2,1)}), bf16[32,40,128]{2,1,0:T(8,128)(2,1)S(1)}, u32[]{:S(2)}, u32[]{:S(2)}) async-start(bf16[32,40,128]{2,1,0:T(8,128)(2,1)} %broadcast_in_dim.63), calls=%async_computation.3 | async-start | bytes 655360 | tf_op jit(solution)/shard_map/all_to_all | solution.py:360

commit v3 on v2

--- a/solution.py
+++ b/solution.py
@@ -25,15 +25,25 @@
 BF16 = jnp.bfloat16
 
 
-def tap_matrices(kernel):
-    channels = kernel.shape[2]
+def tap_rows(kernel):
     wide = jnp.pad(kernel, ((1, 1), (0, 0), (0, 0)))
-    first = wide[1:9]
-    second = wide[0:8]
-    both = jnp.stack([first, second], axis=1).transpose(2, 0, 1, 3).astype(BF16)
-    eye = jnp.eye(channels, dtype=BF16)
-    spread = both[:, :, None, :, :] * eye[None, None, :, None, :]
-    return spread.reshape(TAPS * 8 * channels, 2 * channels)
+    both = jnp.concatenate([wide[1:9], wide[0:8]], axis=2)
+    return both.transpose(1, 0, 2).reshape(TAPS * 8, 256)
+
+
+def build_taps(rows, taps):
+    shape = (128, 256)
+    across = lax.broadcasted_iota(jnp.int32, shape, 1)
+    down = lax.broadcasted_iota(jnp.int32, shape, 0)
+    eye = ((across == down) | (across == down + 128)).astype(F32)
+
+    def body(tap, carry):
+        for position in range(8):
+            at = tap * 8 + position
+            taps[pl.ds(pl.multiple_of(at * 128, 128), 128), :] = (eye * rows[pl.ds(at, 1), :]).astype(BF16)
+        return carry
+
+    lax.fori_loop(0, TAPS, body, 0)
 
 
 def place_strips(pick, padded, stage):
@@ -89,11 +99,12 @@
 
 
 def core_body(
-    slot, listed, fields, arrived, cotangent, mask, taps, conv_bias, ln_gain, ln_bias, weight_in,
+    slot, listed, fields, arrived, cotangent, mask, tap_table, conv_bias, ln_gain, ln_bias, weight_in,
     bias_in, weight_out, bias_out, layer_scale,
     updated, d_conv, strips, padded, d_weight_in, d_weight_out, d_bias_in, small,
-    shifted, stage,
+    shifted, stage, taps,
 ):
+    build_taps(tap_table, taps)
     place_strips(picker(slot, listed, arrived), padded, stage)
 
     def fill(i, carry):
@@ -106,8 +117,9 @@
     d_weight_out[...] = jnp.zeros_like(d_weight_out)
     d_bias_in[...] = jnp.zeros_like(d_bias_in)
     small[...] = jnp.zeros_like(small)
-    d_conv[0:6] = jnp.zeros((6, SIDE, 128), F32)
-    d_conv[SIDE + 6 : SIDE + 12] = jnp.zeros((6, SIDE, 128), F32)
+    d_conv[...] = jnp.zeros_like(d_conv)
+    half_in = weight_in[...] * jnp.bfloat16(0.5)
+    half_bias = bias_in[...] * 0.5
     count = BLOCK // 2
     points = BLOCK * SIDE
 
@@ -122,23 +134,23 @@
     def fold(value):
         return jnp.sum(value.reshape(-1, 8, value.shape[-1]), axis=0)
 
-    def step(index, carry):
+    def step(index, both, last=False):
         at = index * BLOCK
-        both = conv_block(shifted, taps, index * count, count)
         conv = jnp.concatenate([both[:, :128], both[:, 128:]], axis=0) + conv_bias[...]
+        following = both if last else conv_block(shifted, taps, (index + 1) * count, count)
         live = by_half(mask, at)
         signal = by_half(cotangent, at) * live
         centred = conv - jnp.mean(conv, axis=-1, keepdims=True)
         inv_std = lax.rsqrt(jnp.mean(centred * centred, axis=-1, keepdims=True) + EPS)
         normed = centred * inv_std
         lifted = (normed * ln_gain[...] + ln_bias[...]).astype(BF16)
-        hidden = jnp.dot(lifted, weight_in[...], preferred_element_type=F32) + bias_in[...]
-        square = hidden * hidden
-        tanh_part = jnp.tanh(hidden * (GELU_K + GELU_K * GELU_C * square))
-        half = 0.5 * hidden
-        activated = (half + half * tanh_part).astype(BF16)
-        slope = (0.5 + 0.5 * tanh_part) + half * (1.0 - tanh_part * tanh_part) * (
-            GELU_K + 3.0 * GELU_K * GELU_C * square
+        half = jnp.dot(lifted, half_in, preferred_element_type=F32) + half_bias
+        square = half * half
+        tanh_part = jnp.tanh(half * (2.0 * GELU_K + 8.0 * GELU_K * GELU_C * square))
+        above = 1.0 + tanh_part
+        activated = (half * above).astype(BF16)
+        slope = above * (
+            0.5 + (half * (GELU_K + 12.0 * GELU_K * GELU_C * square)) * (1.0 - tanh_part)
         )
         branch = jnp.dot(activated, weight_out[...], preferred_element_type=F32) + bias_out[...]
         d_branch = signal * layer_scale[...]
@@ -158,7 +170,9 @@
         )
         masked = by_half(fields, at) * live
         updated[pl.ds(at, BLOCK)] = by_row(live * (masked + layer_scale[...] * branch)).astype(BF16)
-        d_conv[pl.ds(at + 6, BLOCK)] = by_row(d_out)
+        rows = by_row(d_out)
+        for i in range(BLOCK):
+            d_conv[pl.ds((at + i + RADIUS) * PITCH + RADIUS, SIDE), :] = rows[i]
         d_weight_out[...] += lax.dot_general(
             branch_low, activated, CONTRACT_ROWS, preferred_element_type=F32
         )
@@ -171,72 +185,128 @@
         small[16:24] += fold(d_lifted * normed)
         small[24:32] += fold(d_lifted)
         small[32:40] += fold(d_out)
-        return carry
-
-    lax.fori_loop(0, SIDE // BLOCK, step, 0)
+        return following
+
+    both = conv_block(shifted, taps, 0, count)
+    both = lax.fori_loop(0, SIDE // BLOCK - 1, step, both)
+    step(SIDE // BLOCK - 1, both, last=True)
     for r in range(RADIUS):
-        strips[0, r] = d_conv[6 + r].astype(BF16)
-        strips[1, r] = d_conv[6 + SIDE - RADIUS + r].astype(BF16)
-        flat = d_conv.reshape((SIDE + 12) * SIDE, 128)
-        strips[2, r] = flat[pl.ds(6 * SIDE + r, SIDE, stride=SIDE), :].astype(BF16)
-        strips[3, r] = flat[pl.ds(7 * SIDE - RADIUS + r, SIDE, stride=SIDE), :].astype(BF16)
-
-
-def kernel_grad_body(padded, d_conv, out):
-    flat = d_conv.reshape((SIDE + 12) * SIDE, 128)
-    for low, high in ((0, 4), (4, 7)):
-        taps_here = high - low
-
-        def column(block, sums, low=low, taps_here=taps_here):
-            left = block * 8
-
-            def row(i, state):
-                sums, recent = state
-                newest = flat[pl.ds(pl.multiple_of((i + 6 - low) * SIDE + left, 8), 8), :]
-                window = (newest,) + recent
-                new = []
-                at = i * PITCH + left
-                pieces = [padded[pl.ds(at + b, 8), :] for b in range(TAPS)]
-                for a in range(taps_here):
-                    for b in range(TAPS):
-                        new.append(sums[a * TAPS + b] + pieces[b] * window[a])
-                return tuple(new), window[:-1]
-
-            start = tuple(
-                flat[pl.ds(pl.multiple_of((5 - low - a) * SIDE + left, 8), 8), :]
-                for a in range(taps_here - 1)
-            )
-            sums, _ = lax.fori_loop(0, ROWS, row, (sums, start), unroll=2)
-            return sums
-
-        zero = tuple(jnp.zeros((8, 128), F32) for _ in range(taps_here * TAPS))
-        sums = lax.fori_loop(0, SIDE // 8, column, zero)
-        for a in range(taps_here):
-            for b in range(TAPS):
-                at = (low + a) * TAPS + b
-                out[at : at + 1, :] = jnp.sum(sums[a * TAPS + b], axis=0, keepdims=True)
-
-
-def back_body(slot, listed, d_conv, arrived, cotangent, mask, taps, d_fields, padded, shifted, stage):
-    place_strips(picker(slot, listed, arrived), padded, stage)
-
-    def fill(i, carry):
-        padded[pl.ds((i + RADIUS) * PITCH + RADIUS, SIDE), :] = d_conv[i + 6]
-        return carry
-
-    lax.fori_loop(0, SIDE, fill, 0)
-    shift_copies(padded, shifted)
+        corner = RADIUS * PITCH + RADIUS
+        far = SIDE - RADIUS + r
+        strips[0, r] = d_conv[corner + r * PITCH : corner + r * PITCH + SIDE, :].astype(BF16)
+        strips[1, r] = d_conv[corner + far * PITCH : corner + far * PITCH + SIDE, :].astype(BF16)
+        strips[2, r] = d_conv[pl.ds(corner + r, SIDE, stride=PITCH), :].astype(BF16)
+        strips[3, r] = d_conv[pl.ds(corner + far, SIDE, stride=PITCH), :].astype(BF16)
+
+
+def inner_body(padded, d_conv, cotangent, mask, tap_table, d_kernel, d_fields, sums, shifted, taps):
+    build_taps(tap_table, taps)
+    shift_copies(d_conv, shifted)
+    sums[...] = jnp.zeros_like(sums)
     count = BLOCK // 2
 
     def step(index, carry):
         at = index * BLOCK
         both = conv_block(shifted, taps, index * count, count).reshape(count, SIDE, 256)
+        for b in range(TAPS):
+            part = [None] * TAPS
+            for left in range(0, SIDE, 8):
+                near = [
+                    d_conv[pl.ds((at + i + RADIUS) * PITCH + RADIUS + left, 8), :] for i in range(BLOCK)
+                ]
+                for row in range(BLOCK + TAPS - 1):
+                    piece = padded[pl.ds((at + row) * PITCH + left + b, 8), :]
+                    for a in range(TAPS):
+                        if 0 <= row - a < BLOCK:
+                            term = piece * near[row - a]
+                            part[a] = term if part[a] is None else part[a] + term
+            for a in range(TAPS):
+                sums[a * TAPS + b] += part[a]
         back = jnp.stack([both[:, :, :128], both[:, :, 128:]], axis=1).reshape(BLOCK, SIDE, 128)
         live = mask[pl.ds(at, BLOCK)].astype(F32)
         d_fields[pl.ds(at, BLOCK)] = live * (live * cotangent[pl.ds(at, BLOCK)].astype(F32) + back)
         return carry
 
     lax.fori_loop(0, SIDE // BLOCK, step, 0)
+    d_kernel[...] = jnp.sum(sums[...], axis=1)
+
+
+def edge_body(slot, listed, partial, arrived, mask_strips, weights, d_fields,
+              frame, columns, beside, top, bottom, left, right, sems):
+    inner = SIDE - 2 * RADIUS
+    parts = (
+        (top, (pl.ds(0, RADIUS),)),
+        (bottom, (pl.ds(SIDE - RADIUS, RADIUS),)),
+        (left, (pl.ds(RADIUS, inner), pl.ds(0, 8))),
+        (right, (pl.ds(RADIUS, inner), pl.ds(SIDE - 8, 8))),
+    )
+    loads = [
+        pltpu.make_async_copy(partial.at[where], held, sems.at[i])
+        for i, (held, where) in enumerate(parts)
+    ]
+    for load in loads:
+        load.start()
+    pick = picker(slot, listed, arrived)
+    frame[...] = jnp.zeros_like(frame)
+    columns[...] = jnp.zeros_like(columns)
+    for r in range(RADIUS):
+        frame[0, r, RADIUS : RADIUS + SIDE, :] = pick(0, r)
+        frame[1, r, RADIUS : RADIUS + SIDE, :] = pick(1, r)
+        columns[0, r, RADIUS : RADIUS + SIDE, :] = pick(2, r)
+        columns[1, r, RADIUS : RADIUS + SIDE, :] = pick(3, r)
+        frame[0, r, 0:RADIUS, :] = pick(4, r)[SIDE - RADIUS :]
+        frame[0, r, RADIUS + SIDE : 2 * RADIUS + SIDE, :] = pick(5, r)[:RADIUS]
+        frame[1, r, 0:RADIUS, :] = pick(6, r)[SIDE - RADIUS :]
+        frame[1, r, RADIUS + SIDE : 2 * RADIUS + SIDE, :] = pick(7, r)[:RADIUS]
+
+    def rim(source, far, line, at, tap):
+        total = None
+        for r in range(RADIUS):
+            across = r + 6 - line if far else r - line
+            if 0 <= across < TAPS:
+                for along in range(TAPS):
+                    term = source[far, r, pl.ds(at + along, 8), :] * tap(across, along)
+                    total = term if total is None else total + term
+        return total
+
+    def weight_row(a, b):
+        return weights[a * TAPS + b : a * TAPS + b + 1, :]
+
+    for load in loads:
+        load.wait()
+
+    def along(step, carry):
+        at = pl.multiple_of(step * 8, 8)
+        for line in range(RADIUS):
+            for far, held in ((0, top), (1, bottom)):
+                live = mask_strips[far, line, pl.ds(at, 8), :]
+                add = rim(frame, far, line, at, weight_row)
+                held[line, pl.ds(at, 8), :] += live * add
+            for far in range(2):
+                live = mask_strips[2 + far, line, pl.ds(at, 8), :]
+                add = rim(columns, far, line, at, lambda across, along: weight_row(along, across))
+                beside[far, line, pl.ds(at, 8), :] = live * add
+        return carry
+
+    lax.fori_loop(0, SIDE // 8, along, 0)
+    for far, held in ((0, left), (1, right)):
+        flat = held.reshape(inner * 8, 128)
+        for line in range(RADIUS):
+            column = 5 + line if far else line
+            flat[pl.ds(column, inner, stride=8), :] += beside[far, line, RADIUS : SIDE - RADIUS, :]
+            place = SIDE - RADIUS + line if far else line
+            for i in range(RADIUS):
+                top[i, place : place + 1, :] += beside[far, line, i : i + 1, :]
+                low = SIDE - RADIUS + i
+                bottom[i, place : place + 1, :] += beside[far, line, low : low + 1, :]
+    stores = [
+        pltpu.make_async_copy(held, d_fields.at[where], sems.at[i])
+        for i, (held, where) in enumerate(parts)
+    ]
+    for store in stores:
+        store.start()
+    for store in stores:
+        store.wait()
 
 
 VMEM_BYTES = 60 * 1024 * 1024
@@ -244,7 +314,7 @@
 IN_SMEM = pl.BlockSpec(memory_space=pltpu.SMEM)
 
 
-def run_core(slot, listed, fields, arrived, cotangent, mask, taps, vectors, weights):
+def run_core(slot, listed, fields, arrived, cotangent, mask, tap_table, vectors, weights):
     conv_bias, ln_gain, ln_bias, bias_in, bias_out, layer_scale = vectors
     weight_in, weight_out = weights
     shape = jax.ShapeDtypeStruct
@@ -252,7 +322,7 @@
         core_body,
         out_shape=(
             shape((SIDE, SIDE, 128), BF16),
-            shape((SIDE + 12, SIDE, 128), F32),
+            shape((ROWS * PITCH, 128), F32),
             shape((4, RADIUS, SIDE, 128), BF16),
             shape((ROWS * PITCH, 128), F32),
             shape((128, 512), F32),
@@ -265,40 +335,53 @@
         scratch_shapes=[
             pltpu.VMEM((TAPS, PAIRS, SIDE, 256), BF16),
             pltpu.VMEM((4 * SIDE, 128), F32),
+            pltpu.VMEM((TAPS * 1024, 256), BF16),
         ],
         compiler_params=pltpu.CompilerParams(vmem_limit_bytes=VMEM_BYTES),
         name="core",
-    )(slot, listed, fields, arrived, cotangent, mask, taps, conv_bias, ln_gain, ln_bias,
+    )(slot, listed, fields, arrived, cotangent, mask, tap_table, conv_bias, ln_gain, ln_bias,
       weight_in, bias_in, weight_out, bias_out, layer_scale)
 
 
-def run_kernel_grad(padded, d_conv):
+def run_inner(padded, d_conv, cotangent, mask, tap_table):
     return pl.pallas_call(
-        kernel_grad_body,
-        out_shape=jax.ShapeDtypeStruct((56, 128), F32),
-        in_specs=[IN_VMEM] * 2,
-        out_specs=IN_VMEM,
-        compiler_params=pltpu.CompilerParams(vmem_limit_bytes=VMEM_BYTES),
-        cost_estimate=pl.CostEstimate(flops=80_000_000, bytes_accessed=5_000_000, transcendentals=0),
-        name="kernel_grad",
-    )(padded, d_conv)
-
-
-def run_back(slot, listed, d_conv, arrived, cotangent, mask, taps):
-    return pl.pallas_call(
-        back_body,
-        out_shape=jax.ShapeDtypeStruct((SIDE, SIDE, 128), F32),
-        in_specs=[IN_SMEM, IN_SMEM] + [IN_VMEM] * 5,
-        out_specs=IN_VMEM,
+        inner_body,
+        out_shape=(
+            jax.ShapeDtypeStruct((TAPS * TAPS, 128), F32),
+            jax.ShapeDtypeStruct((SIDE, SIDE, 128), F32),
+        ),
+        in_specs=[IN_VMEM] * 5,
+        out_specs=(IN_VMEM,) * 2,
         scratch_shapes=[
-            pltpu.VMEM((ROWS * PITCH, 128), F32),
+            pltpu.VMEM((TAPS * TAPS, 8, 128), F32),
             pltpu.VMEM((TAPS, PAIRS, SIDE, 256), BF16),
-            pltpu.VMEM((4 * SIDE, 128), F32),
+            pltpu.VMEM((TAPS * 1024, 256), BF16),
         ],
         compiler_params=pltpu.CompilerParams(vmem_limit_bytes=VMEM_BYTES),
-        cost_estimate=pl.CostEstimate(flops=7_000_000_000, bytes_accessed=8_000_000, transcendentals=0),
-        name="back",
-    )(slot, listed, d_conv, arrived, cotangent, mask, taps)
+        cost_estimate=pl.CostEstimate(flops=16_000_000_000, bytes_accessed=8_000_000, transcendentals=0),
+        name="inner",
+    )(padded, d_conv, cotangent, mask, tap_table)
+
+
+def run_edge(slot, listed, partial, arrived, mask_strips, weights):
+    rim = pltpu.VMEM((RADIUS, SIDE, 128), F32)
+    side = pltpu.VMEM((SIDE - 2 * RADIUS, 8, 128), F32)
+    return pl.pallas_call(
+        edge_body,
+        out_shape=jax.ShapeDtypeStruct((SIDE, SIDE, 128), F32),
+        in_specs=[IN_SMEM, IN_SMEM, pl.BlockSpec(memory_space=pl.ANY)] + [IN_VMEM] * 3,
+        out_specs=pl.BlockSpec(memory_space=pl.ANY),
+        scratch_shapes=[
+            pltpu.VMEM((2, RADIUS, PITCH, 128), F32),
+            pltpu.VMEM((2, RADIUS, PITCH, 128), F32),
+            pltpu.VMEM((2, RADIUS, SIDE, 128), F32),
+            rim, rim, side, side,
+            pltpu.SemaphoreType.DMA((4,)),
+        ],
+        input_output_aliases={2: 0},
+        compiler_params=pltpu.CompilerParams(vmem_limit_bytes=VMEM_BYTES),
+        name="edge",
+    )(slot, listed, partial, arrived, mask_strips, weights)
 
 
 def frame_strips(tile, radius):
@@ -385,23 +468,26 @@
     tile_count = fields.shape[0]
     tile_side = fields.shape[1]
     mask = jnp.broadcast_to(ocean_mask[0].astype(BF16)[..., None], fields.shape[1:])
-    masked = fields[0] * mask
     maps = halo_maps(neighbours)
     slot, listed = maps[1], maps[2]
-    arrived = exchange(frame_strips(masked, RADIUS), maps)
+    mask_strips = frame_strips(ocean_mask[0].astype(F32)[..., None], RADIUS)
+    strips = frame_strips(fields[0], RADIUS) * mask_strips.astype(BF16)
+    arrived = exchange(strips, maps)
     vectors = [v.reshape(1, -1) for v in (conv_bias, ln_gain, ln_bias, bias_in, bias_out, layer_scale)]
     updated, d_conv, strips, padded, d_weight_in, d_weight_out, d_bias_in, small = run_core(
-        slot, listed, fields[0], arrived, cotangent[0], mask, tap_matrices(kernel), vectors,
+        slot, listed, fields[0], arrived, cotangent[0], mask, tap_rows(kernel), vectors,
         (weight_in, weight_out),
     )
     arrived_back = exchange(strips, maps)
-    d_kernel = run_kernel_grad(padded, d_conv)
+    flipped = kernel[::-1, ::-1]
+    d_kernel, partial = run_inner(padded, d_conv, cotangent[0], mask, tap_rows(flipped))
     grad_scale = 1.0 / math.sqrt(lax.axis_size("tiles") * tile_count * tile_side * tile_side)
     small = jnp.sum(small.reshape(5, 8, 128), axis=1)
-    parts = [d_weight_in, d_weight_out, jnp.sum(d_bias_in, axis=0), d_kernel[:49], small]
+    parts = [d_weight_in, d_weight_out, jnp.sum(d_bias_in, axis=0), d_kernel, small]
     totals = sum_over_tiles([part * grad_scale for part in parts])
-    d_fields = run_back(
-        slot, listed, d_conv, arrived_back, cotangent[0], mask, tap_matrices(kernel[::-1, ::-1])
+    d_fields = run_edge(
+        slot, listed, partial, arrived_back,
+        jnp.broadcast_to(mask_strips, (4, RADIUS, SIDE, 128)), flipped.reshape(TAPS * TAPS, 128),
     )
     t_in, t_out, t_bias_in, t_kernel, t_small = totals
     return (

time: 164 us -> 149 us (0.909)
  Pallas kernels: 66.7 us -> 43.4 us
  waiting for transfers between devices: 24.2 us -> 46 us
  other arithmetic: 13.6 us -> 5 us
  starting transfers between devices: 37.1 us -> 33.4 us
    pallas_call x1, Pallas kernels: 35.5 us -> 22.8 us  [run_core(): pl.pallas_call(core_body, out_shape=(shape((SIDE, SIDE, 128), BF16), shap...]
    all_to_all x2, waiting for transfers between devices: 10.5 us -> 22.8 us  [exchange(): arrived = lax.all_to_all(blocks, 'tiles', 0, 0, axis_index_groups=groups)]
    pallas_call x2, Pallas kernels: 31.2 us -> 20.6 us  [the longest x1 16.6 us: run_inner(): pl.pallas_call(inner_body, out_shape=(jax.ShapeDtypeStruct((TAPS * TAPS,...]
    ppermute x2, waiting for transfers between devices: 2.54 us -> 11.4 us  [exchange(): lax.ppermute(strips, 'tiles', [(i, i + GROUP) for i in range(peers - GROU...]
    mul x2 -> x1, other arithmetic: 8.7 us -> 0.34 us  [per_device(): strips = frame_strips(fields[0], RADIUS) * mask_strips.astype(BF16)]
    all_to_all x1, waiting for transfers between devices: 0.01 us -> 6.16 us  [sum_over_tiles(): lax.all_to_all(shared, 'tiles', 0, 0).reshape(-1, 128).astype(jnp.float32)]
    unnamed x22 -> x18, local copies, waits for them, and re-layouts: 7.85 us -> 1.79 us
    ppermute x2, waiting for transfers between devices: 11.1 us -> 5.64 us  [exchange(): lax.ppermute(strips, 'tiles', [(i + GROUP, i) for i in range(peers - GROU...]
  transfers between devices with their start and end apart: 10 -> 10, of which waited for: 4 -> 7; matrix products, arithmetic and copies ran while one was open for 13% -> 8% of each run, Pallas kernels for 10% -> 3%
where the time goes in v3:
time: 149 us; the launch traced here: 148 us
  waiting for transfers between devices  46 us (31%)
  Pallas kernels  43.4 us (29%)
  starting transfers between devices  33.4 us (22%)
  local copies, waits for them, and re-layouts  19.1 us (13%)
  other arithmetic  5 us (3%)
    all_to_all x2, waiting for transfers between devices, exchange(): arrived = lax.all_to_all(blocks, 'tiles', 0, 0, axis_index_groups=groups)  22.8 us
    pallas_call x1, Pallas kernels, run_core(): pl.pallas_call(core_body, out_shape=(shape((SIDE, SIDE, 128), BF16), shap...  22.8 us
    pallas_call x1, Pallas kernels, run_inner(): pl.pallas_call(inner_body, out_shape=(jax.ShapeDtypeStruct((TAPS * TAPS,...  16.6 us
    ppermute x2, waiting for transfers between devices, exchange(): lax.ppermute(strips, 'tiles', [(i, i + GROUP) for i in range(peers - GROU...  11.4 us
    ppermute x2, starting transfers between devices, exchange(): lax.ppermute(strips, 'tiles', [(i, i + GROUP) for i in range(peers - GROU...  8.25 us
    all_to_all x2, starting transfers between devices, exchange(): arrived = lax.all_to_all(blocks, 'tiles', 0, 0, axis_index_groups=groups)  7.34 us
    all_to_all x1, waiting for transfers between devices, sum_over_tiles(): lax.all_to_all(shared, 'tiles', 0, 0).reshape(-1, 128).astype(jnp.float32)  6.16 us
    all_to_all x1, starting transfers between devices, sum_over_tiles(): lax.all_to_all(shared, 'tiles', 0, 0).reshape(-1, 128).astype(jnp.float32)  6.02 us
  transfers between devices with their start and end apart: 10, of which 7 were waited for; matrix products, arithmetic and copies ran while one was open for 8% of the time, Pallas kernels for 3%

profile of v3, /device:TPU:0, one launch (start us, length us, event | category | flops | bytes accessed | tf_op | source)
XLA Modules:
  0.0 147.9 jit_solution(16215994573352928268)
XLA Ops:
  0.6 4.9 %collective-permute-start.2 = (s32[8]{0:T(128)}, s32[8]{0:T(128)S(1)}, u32[]{:S(2)}, u32[]{:S(2)}) collective-permute-start(s32[8]{0:T(128)} %bitcast.107), channel_id=1, source_target_pairs={{0,8},{1,9},{2,10},{3,11},{4,12},{5,13},{6,14},{7,15},{8,16},{9,17... | collective-permute-start | bytes 104 | tf_op jit(solution)/shard_map/ppermute | solution.py:405
  5.6 1.3 collective-permute-start.3
  10.4 4.6 %collective-permute-start = (bf16[4,3,64,128]{3,1,2,0:T(4,128)(2,1)S(1)}, bf16[4,3,64,128]{3,1,2,0:T(4,128)(2,1)S(1)}, u32[]{:S(2)}, u32[]{:S(2)}) collective-permute-start(bf16[4,3,64,128]{3,1,2,0:T(4,128)(2,1)S(1)} %maximum_multiply_fusion), channel_id=1, source_target_pairs={{0,8},{1,9},{2,10},{3,11},{4,12},{5,13},{6,14},{7,15},{8,16},{9,17... | collective-permute-start | bytes 589832 | tf_op jit(solution)/shard_map/ppermute | solution.py:425
  15.0 1.3 collective-permute-start.1
  19.9 4.1 %collective-permute-done.1 = bf16[4,3,64,128]{3,1,2,0:T(4,128)(2,1)S(1)} collective-permute-done((bf16[4,3,64,128]{3,1,2,0:T(4,128)(2,1)S(1)}, bf16[4,3,64,128]{3,1,2,0:T(4,128)(2,1)S(1)}, u32[]{:S(2)}, u32[]{:S(2)}) %collective-permute-start.1) | collective-permute-done | bytes 196640 | tf_op jit(solution)/shard_map/ppermute | solution.py:426
  24.6 1.4 gather_fusion
  26.1 1.1 copy.116
  27.2 3.7 %all-to-all-start = ((bf16[8,2,3,64,128]{4,3,2,1,0:T(8,128)(2,1)}), bf16[8,2,3,64,128]{4,3,2,1,0:T(8,128)(2,1)S(1)}, u32[]{:S(2)}, u32[]{:S(2)}) async-start(bf16[8,2,3,64,128]{4,3,2,1,0:T(8,128)(2,1)} %copy.116), calls=%async_computation | async-start | bytes 1572864 | tf_op jit(solution)/shard_map/all_to_all | solution.py:431
  33.2 10.3 %all-to-all-done = bf16[8,2,3,64,128]{4,3,2,1,0:T(8,128)(2,1)S(1)} async-done(((bf16[8,2,3,64,128]{4,3,2,1,0:T(8,128)(2,1)}), bf16[8,2,3,64,128]{4,3,2,1,0:T(8,128)(2,1)S(1)}, u32[]{:S(2)}, u32[]{:S(2)}) %all-to-all-start) | async-done | bytes 786464 | tf_op jit(solution)/shard_map/all_to_all | solution.py:431
  43.5 1.6 %broadcast_in_dim.64.mask = bf16[64,64,128]{2,1,0:T(8,128)(2,1)} broadcast(bf16[64,64]{1,0:T(8,128)(2,1)S(1)} %convert_bitcast_fusion), dimensions={0,1} | broadcast | bytes 1056768 | tf_op jit(solution)/shard_map/broadcast_in_dim | solution.py:470
  45.1 22.8 %core.1 = (bf16[64,64,128]{2,1,0:T(8,128)(2,1)}, f32[5040,128]{1,0:T(8,128)}, bf16[4,3,64,128]{3,2,1,0:T(8,128)(2,1)}, f32[5040,128]{1,0:T(8,128)}, f32[128,512]...) custom-call(s32[8]{0:T(128)} %compare_select_fusion.4.slot, ...), custom_call_target="tpu_custom_call" | custom-call | tf_op jit(solution)/shard_map/core/pallas_call | solution.py:321
  67.9 1.1 broadcast_multiply_fusion
  69.1 16.6 %inner.1 = (f32[49,128]{1,0:T(8,128)}, f32[64,64,128]{2,1,0:T(8,128)}) custom-call(f32[5040,128]{1,0:T(8,128)} %get-tuple-element.22.padded, f32[5040,128]{1,0:T(8,128)} %get-tuple-element.23.d_conv, bf16[64,64,128]{2,1,0:T(8,128)(2,1)} %bitcast.97, bf16[64,64,128]{2,1,0:T(8,128)(2,1)} %broadcast_in_dim.64.mask, f32[56,256]{1,0:T(8,128)} %bitcast.99), custom_call_target="tpu_custom_call" | custom-call | flops 16000000000 | bytes 8000000 | tf_op jit(solution)/shard_map/inner/pallas_call | solution.py:347
  87.8 3.0 %all-to-all-start.2 = ((f32[32,40,128]{2,1,0:T(8,128)}), f32[32,40,128]{2,1,0:T(8,128)S(1)}, u32[]{:S(2)}, u32[]{:S(2)}) async-start(f32[32,40,128]{2,1,0:T(8,128)} %bitcast.39), calls=%async_computation.2 | async-start | bytes 1310720 | tf_op jit(solution)/shard_map/all_to_all | solution.py:441
  90.8 3.7 %collective-permute-start.4 = (bf16[4,3,64,128]{3,2,1,0:T(8,128)(2,1)S(1)}, bf16[4,3,64,128]{3,2,1,0:T(8,128)(2,1)S(1)}, u32[]{:S(2)}, u32[]{:S(2)}) collective-permute-start(bf16[4,3,64,128]{3,2,1,0:T(8,128)(2,1)S(1)} %copy-done.2), channel_id=1, source_target_pairs={{0,8},{1,9},{2,10},{3,11},{4,12},{5,13},{6,14},{7,15},{8,16},{9,17... | collective-permute-start | bytes 589832 | tf_op jit(solution)/shard_map/ppermute | solution.py:425
  94.5 1.3 collective-permute-start.5
  95.8 10.5 %collective-permute-done.4 = bf16[4,3,64,128]{3,2,1,0:T(8,128)(2,1)S(1)} collective-permute-done((bf16[4,3,64,128]{3,2,1,0:T(8,128)(2,1)S(1)}, bf16[4,3,64,128]{3,2,1,0:T(8,128)(2,1)S(1)}, u32[]{:S(2)}, u32[]{:S(2)}) %collective-permute-start.4) | collective-permute-done | bytes 196640 | tf_op jit(solution)/shard_map/ppermute | solution.py:425
  106.2 1.5 %collective-permute-done.5 = bf16[4,3,64,128]{3,2,1,0:T(8,128)(2,1)S(1)} collective-permute-done((bf16[4,3,64,128]{3,2,1,0:T(8,128)(2,1)S(1)}, bf16[4,3,64,128]{3,2,1,0:T(8,128)(2,1)S(1)}, u32[]{:S(2)}, u32[]{:S(2)}) %collective-permute-start.5) | collective-permute-done | bytes 196640 | tf_op jit(solution)/shard_map/ppermute | solution.py:426
  107.8 1.5 %gather_fusion.1 = bf16[16,3,64,128]{3,2,1,0:T(8,128)(2,1)} fusion(bf16[12,3,64,128]{3,2,1,0:T(8,128)(2,1)S(1)} %pad_maximum_fusion.1, s32[1024]{0:T(1024)S(1)} %pad_clamp_fusion), kind=kCustom, calls=%fused_computation.1 | custom fusion | bytes 1572928 | tf_op jit(solution)/shard_map/jit(_take)/gather | solution.py:428
  109.4 3.6 %all-to-all-start.1 = ((bf16[8,2,3,64,128]{4,3,2,1,0:T(8,128)(2,1)}), bf16[8,2,3,64,128]{4,3,2,1,0:T(8,128)(2,1)S(1)}, u32[]{:S(2)}, u32[]{:S(2)}) async-start(bf16[8,2,3,64,128]{4,3,2,1,0:T(8,128)(2,1)} %bitcast.29), calls=%async_computation.1 | async-start | bytes 1572864 | tf_op jit(solution)/shard_map/all_to_all | solution.py:431
  113.0 12.5 %all-to-all-done.1 = bf16[8,2,3,64,128]{4,3,2,1,0:T(8,128)(2,1)S(1)} async-done(((bf16[8,2,3,64,128]{4,3,2,1,0:T(8,128)(2,1)}), bf16[8,2,3,64,128]{4,3,2,1,0:T(8,128)(2,1)S(1)}, u32[]{:S(2)}, u32[]{:S(2)}) %all-to-all-start.1) | async-done | bytes 786464 | tf_op jit(solution)/shard_map/all_to_all | solution.py:431
  126.4 6.0 %all-to-all-start.3 = ((bf16[32,40,128]{2,1,0:T(8,128)(2,1)}), bf16[32,40,128]{2,1,0:T(8,128)(2,1)S(1)}, u32[]{:S(2)}, u32[]{:S(2)}) async-start(bf16[32,40,128]{2,1,0:T(8,128)(2,1)} %broadcast_in_dim.69), calls=%async_computation.3 | async-start | bytes 655360 | tf_op jit(solution)/shard_map/all_to_all | solution.py:443
  134.3 4.0 %edge.1 = f32[64,64,128]{2,1,0:T(8,128)} custom-call(s32[8]{0:T(128)} %compare_select_fusion.4.slot, s32[8]{0:T(128)} %compare_convert_fusion.1.listed, f32[64,64,128]{2,1,0:T(8,128)} %get-tuple-element.24.partial, bf16[16,3,64,128]{3,2,1,0:T(8,128)(2,1)} %bitcast.90, ...), custom_call_target="tpu_custom_call", output_to_operand_aliasing={{}: (2, {})} | custom-call | tf_op jit(solution)/shard_map/edge/pallas_call | solution.py:369
  138.3 6.2 %all-to-all-done.3 = bf16[32,40,128]{2,1,0:T(8,128)(2,1)S(1)} async-done(((bf16[32,40,128]{2,1,0:T(8,128)(2,1)}), bf16[32,40,128]{2,1,0:T(8,128)(2,1)S(1)}, u32[]{:S(2)}, u32[]{:S(2)}) %all-to-all-start.3) | async-done | bytes 327712 | tf_op jit(solution)/shard_map/all_to_all | solution.py:443
  (79 shorter events, 18.2 us)
Async XLA Ops:
  0.6 17.3 %collective-permute-start.2 = (s32[8]{0:T(128)}, s32[8]{0:T(128)S(1)}, u32[]{:S(2)}, u32[]{:S(2)}) collective-permute-start(s32[8]{0:T(128)} %bitcast.107), channel_id=1, source_target_pairs={{0,8},{1,9},{2,10},{3,11},{4,12},{5,13},{6,14},{7,15},{8,16},{9,17... | collective-permute-start | bytes 104 | tf_op jit(solution)/shard_map/ppermute | solution.py:405
  5.6 12.4 %collective-permute-start.3 = (s32[8]{0:T(128)}, s32[8]{0:T(128)S(1)}, u32[]{:S(2)}, u32[]{:S(2)}) collective-permute-start(s32[8]{0:T(128)} %bitcast.108), channel_id=1, source_target_pairs={{8,0},{9,1},{10,2},{11,3},{12,4},{13,5},{14,6},{15,7},{16,8},{17,9... | collective-permute-start | bytes 104 | tf_op jit(solution)/shard_map/ppermute | solution.py:406
  10.4 9.5 %collective-permute-start = (bf16[4,3,64,128]{3,1,2,0:T(4,128)(2,1)S(1)}, bf16[4,3,64,128]{3,1,2,0:T(4,128)(2,1)S(1)}, u32[]{:S(2)}, u32[]{:S(2)}) collective-permute-start(bf16[4,3,64,128]{3,1,2,0:T(4,128)(2,1)S(1)} %maximum_multiply_fusion), channel_id=1, source_target_pairs={{0,8},{1,9},{2,10},{3,11},{4,12},{5,13},{6,14},{7,15},{8,16},{9,17... | collective-permute-start | bytes 589832 | tf_op jit(solution)/shard_map/ppermute | solution.py:425
  15.0 9.1 %collective-permute-start.1 = (bf16[4,3,64,128]{3,1,2,0:T(4,128)(2,1)S(1)}, bf16[4,3,64,128]{3,1,2,0:T(4,128)(2,1)S(1)}, u32[]{:S(2)}, u32[]{:S(2)}) collective-permute-start(bf16[4,3,64,128]{3,1,2,0:T(4,128)(2,1)S(1)} %maximum_multiply_fusion), channel_id=1, source_target_pairs={{8,0},{9,1},{10,2},{11,3},{12,4},{13,5},{14,6},{15,7},{16,8},{17,9... | collective-permute-start | bytes 589832 | tf_op jit(solution)/shard_map/ppermute | solution.py:426
  24.6 7.6 %copy-start.6 = (s32[1,8]{1,0:T(1,128)S(1)}, s32[1,8]{1,0:T(1,128)}, u32[]{:S(2)}) copy-start(s32[1,8]{1,0:T(1,128)} %param.17) | copy-start | bytes 100
  24.6 8.6 %copy-start.3 = (s32[1,64,64]{2,1,0:T(8,128)S(1)}, s32[1,64,64]{2,1,0:T(8,128)}, u32[]{:S(2)}) copy-start(s32[1,64,64]{2,1,0:T(8,128)} %param.16) | copy-start | bytes 49156
  27.2 16.3 %all-to-all-start = ((bf16[8,2,3,64,128]{4,3,2,1,0:T(8,128)(2,1)}), bf16[8,2,3,64,128]{4,3,2,1,0:T(8,128)(2,1)S(1)}, u32[]{:S(2)}, u32[]{:S(2)}) async-start(bf16[8,2,3,64,128]{4,3,2,1,0:T(8,128)(2,1)} %copy.116), calls=%async_computation | async-start | bytes 1572864 | tf_op jit(solution)/shard_map/all_to_all | solution.py:431
  43.5 1.6 %copy-start.1 = (bf16[8,2,3,64,128]{4,3,2,1,0:T(8,128)(2,1)}, bf16[8,2,3,64,128]{4,3,2,1,0:T(8,128)(2,1)S(1)}, u32[]{:S(2)}) copy-start(bf16[8,2,3,64,128]{4,3,2,1,0:T(8,128)(2,1)S(1)} %all-to-all-done) | copy-start | bytes 2359300
  69.0 17.5 %copy-start.4 = (f32[40,128]{1,0:T(8,128)S(1)}, f32[40,128]{1,0:T(8,128)}, u32[]{:S(2)}) copy-start(f32[40,128]{1,0:T(8,128)} %get-tuple-element.30) | copy-start | bytes 61444
  69.0 17.5 %copy-start.5 = (f32[8,512]{1,0:T(8,128)S(1)}, f32[8,512]{1,0:T(8,128)}, u32[]{:S(2)}) copy-start(f32[8,512]{1,0:T(8,128)} %get-tuple-element.28) | copy-start | bytes 49156
  85.7 5.1 %copy-start.2 = (bf16[4,3,64,128]{3,2,1,0:T(8,128)(2,1)S(1)}, bf16[4,3,64,128]{3,2,1,0:T(8,128)(2,1)}, u32[]{:S(2)}) copy-start(bf16[4,3,64,128]{3,2,1,0:T(8,128)(2,1)} %get-tuple-element.25) | copy-start | bytes 589828
  87.8 21.6 %all-to-all-start.2 = ((f32[32,40,128]{2,1,0:T(8,128)}), f32[32,40,128]{2,1,0:T(8,128)S(1)}, u32[]{:S(2)}, u32[]{:S(2)}) async-start(f32[32,40,128]{2,1,0:T(8,128)} %bitcast.39), calls=%async_computation.2 | async-start | bytes 1310720 | tf_op jit(solution)/shard_map/all_to_all | solution.py:441
  90.8 15.5 %collective-permute-start.4 = (bf16[4,3,64,128]{3,2,1,0:T(8,128)(2,1)S(1)}, bf16[4,3,64,128]{3,2,1,0:T(8,128)(2,1)S(1)}, u32[]{:S(2)}, u32[]{:S(2)}) collective-permute-start(bf16[4,3,64,128]{3,2,1,0:T(8,128)(2,1)S(1)} %copy-done.2), channel_id=1, source_target_pairs={{0,8},{1,9},{2,10},{3,11},{4,12},{5,13},{6,14},{7,15},{8,16},{9,17... | collective-permute-start | bytes 589832 | tf_op jit(solution)/shard_map/ppermute | solution.py:425
  94.5 13.3 %collective-permute-start.5 = (bf16[4,3,64,128]{3,2,1,0:T(8,128)(2,1)S(1)}, bf16[4,3,64,128]{3,2,1,0:T(8,128)(2,1)S(1)}, u32[]{:S(2)}, u32[]{:S(2)}) collective-permute-start(bf16[4,3,64,128]{3,2,1,0:T(8,128)(2,1)S(1)} %copy-done.2), channel_id=1, source_target_pairs={{8,0},{9,1},{10,2},{11,3},{12,4},{13,5},{14,6},{15,7},{16,8},{17,9... | collective-permute-start | bytes 589832 | tf_op jit(solution)/shard_map/ppermute | solution.py:426
  109.4 16.2 %all-to-all-start.1 = ((bf16[8,2,3,64,128]{4,3,2,1,0:T(8,128)(2,1)}), bf16[8,2,3,64,128]{4,3,2,1,0:T(8,128)(2,1)S(1)}, u32[]{:S(2)}, u32[]{:S(2)}) async-start(bf16[8,2,3,64,128]{4,3,2,1,0:T(8,128)(2,1)} %bitcast.29), calls=%async_computation.1 | async-start | bytes 1572864 | tf_op jit(solution)/shard_map/all_to_all | solution.py:431
  125.6 8.7 %copy-start = (bf16[8,2,3,64,128]{4,3,2,1,0:T(8,128)(2,1)}, bf16[8,2,3,64,128]{4,3,2,1,0:T(8,128)(2,1)S(1)}, u32[]{:S(2)}) copy-start(bf16[8,2,3,64,128]{4,3,2,1,0:T(8,128)(2,1)S(1)} %all-to-all-done.1) | copy-start | bytes 2359300
  126.4 18.0 %all-to-all-start.3 = ((bf16[32,40,128]{2,1,0:T(8,128)(2,1)}), bf16[32,40,128]{2,1,0:T(8,128)(2,1)S(1)}, u32[]{:S(2)}, u32[]{:S(2)}) async-start(bf16[32,40,128]{2,1,0:T(8,128)(2,1)} %broadcast_in_dim.69), calls=%async_computation.3 | async-start | bytes 655360 | tf_op jit(solution)/shard_map/all_to_all | solution.py:443

commit v4 on v3

--- a/solution.py
+++ b/solution.py
@@ -12,15 +12,21 @@
 GELU_C = 0.044715
 CONTRACT_LAST = (((1,), (1,)), ((), ()))
 CONTRACT_ROWS = (((0,), (0,)), ((), ()))
-
-
 SIDE = 64
 RADIUS = 3
+STRIP_ROWS = RADIUS * SIDE
+GROUP = 8
+STRIP_FOR = (1, 0, 3, 2, 1, 1, 0, 0)
+OPPOSITE = (1, 0, 3, 2, 7, 6, 5, 4)
 TAPS = 7
 PITCH = 72
 ROWS = SIDE + 2 * RADIUS
 PAIRS = ROWS // 2
 BLOCK = 8
+AT_KERNEL = 1024
+AT_BIAS_IN = 1080
+AT_SMALL = 1088
+PACKED_ROWS = 1096
 F32 = jnp.float32
 BF16 = jnp.bfloat16
 
@@ -90,22 +96,72 @@
     return total
 
 
-def picker(slot, listed, arrived):
+def picker(place, arrived):
+    group = lax.div(place[8], GROUP)
+
     def pick(side, r):
-        value = arrived[slot[side], r].astype(F32)
-        return jnp.where(listed[side] > 0, value, 0.0)
+        tile = place[side]
+        owner = jnp.maximum(tile, 0)
+        slot = 2 * lax.rem(owner, GROUP) + jnp.where(lax.div(owner, GROUP) != group, 1, 0)
+        at = pl.multiple_of(slot * STRIP_ROWS + r * SIDE, SIDE)
+        value = arrived[pl.ds(at, SIDE), :].astype(F32)
+        return jnp.where(tile >= 0, value, 0.0)
 
     return pick
 
 
+def outgoing_body(place, fields, mask_strips, out, near, far):
+    def fill(i, carry):
+        near[pl.ds(i * 16, 16), :] = fields[i, 0:16, :].astype(F32)
+        far[pl.ds(i * 16, 16), :] = fields[i, SIDE - 16 : SIDE, :].astype(F32)
+        return carry
+
+    lax.fori_loop(0, SIDE, fill, 0, unroll=4)
+    for r in range(RADIUS):
+        rows = (
+            fields[r].astype(F32),
+            fields[SIDE - RADIUS + r].astype(F32),
+            near[pl.ds(r, SIDE, stride=16), :],
+            far[pl.ds(16 - RADIUS + r, SIDE, stride=16), :],
+        )
+        for side in range(4):
+            at = side * STRIP_ROWS + r * SIDE
+            out[at : at + SIDE, :] = (rows[side] * mask_strips[side, r]).astype(BF16)
+    lane = lax.broadcasted_iota(jnp.int32, (16, 128), 1)
+    listing = jnp.zeros((16, 128), F32)
+    for side in range(8):
+        listing = jnp.where(lane == side, place[side].astype(F32), listing)
+    out[4 * STRIP_ROWS :, :] = listing.astype(BF16)
+
+
+def relay_body(place, lists, own, below, above, out):
+    group = lax.div(place[8], GROUP)
+    mine = lax.rem(place[8], GROUP)
+
+    def strip_for(read, tile):
+        strip = jnp.int32(0)
+        for side in range(8):
+            strip = jnp.where(read(side) == tile, STRIP_FOR[OPPOSITE[side]], strip)
+        return pl.multiple_of(strip * STRIP_ROWS, STRIP_ROWS)
+
+    for dest in range(GROUP):
+        tile = group * GROUP + dest
+        at = strip_for(lambda side: place[side], tile)
+        out[2 * dest * STRIP_ROWS : (2 * dest + 1) * STRIP_ROWS, :] = own[pl.ds(at, STRIP_ROWS), :]
+        at = strip_for(lambda side: jnp.where(dest < mine, lists[0, side], lists[1, side]), tile)
+        out[(2 * dest + 1) * STRIP_ROWS : (2 * dest + 2) * STRIP_ROWS, :] = jnp.where(
+            dest < mine, below[pl.ds(at, STRIP_ROWS), :], above[pl.ds(at, STRIP_ROWS), :]
+        )
+
+
 def core_body(
-    slot, listed, fields, arrived, cotangent, mask, tap_table, conv_bias, ln_gain, ln_bias, weight_in,
+    place, fields, arrived, cotangent, mask, tap_table, conv_bias, ln_gain, ln_bias, weight_in,
     bias_in, weight_out, bias_out, layer_scale,
     updated, d_conv, strips, padded, d_weight_in, d_weight_out, d_bias_in, small,
     shifted, stage, taps,
 ):
     build_taps(tap_table, taps)
-    place_strips(picker(slot, listed, arrived), padded, stage)
+    place_strips(picker(place, arrived), padded, stage)
 
     def fill(i, carry):
         padded[pl.ds((i + RADIUS) * PITCH + RADIUS, SIDE), :] = fields[i].astype(F32) * mask[i].astype(F32)
@@ -193,13 +249,21 @@
     for r in range(RADIUS):
         corner = RADIUS * PITCH + RADIUS
         far = SIDE - RADIUS + r
-        strips[0, r] = d_conv[corner + r * PITCH : corner + r * PITCH + SIDE, :].astype(BF16)
-        strips[1, r] = d_conv[corner + far * PITCH : corner + far * PITCH + SIDE, :].astype(BF16)
-        strips[2, r] = d_conv[pl.ds(corner + r, SIDE, stride=PITCH), :].astype(BF16)
-        strips[3, r] = d_conv[pl.ds(corner + far, SIDE, stride=PITCH), :].astype(BF16)
-
-
-def inner_body(padded, d_conv, cotangent, mask, tap_table, d_kernel, d_fields, sums, shifted, taps):
+        rows = (
+            d_conv[corner + r * PITCH : corner + r * PITCH + SIDE, :],
+            d_conv[corner + far * PITCH : corner + far * PITCH + SIDE, :],
+            d_conv[pl.ds(corner + r, SIDE, stride=PITCH), :],
+            d_conv[pl.ds(corner + far, SIDE, stride=PITCH), :],
+        )
+        for side in range(4):
+            at = side * STRIP_ROWS + r * SIDE
+            strips[at : at + SIDE, :] = rows[side].astype(BF16)
+
+
+def inner_body(
+    scale, padded, d_conv, cotangent, mask, tap_table, d_weight_in, d_weight_out, d_bias_in, small,
+    packed, d_fields, sums, shifted, taps, held,
+):
     build_taps(tap_table, taps)
     shift_copies(d_conv, shifted)
     sums[...] = jnp.zeros_like(sums)
@@ -228,10 +292,33 @@
         return carry
 
     lax.fori_loop(0, SIDE // BLOCK, step, 0)
-    d_kernel[...] = jnp.sum(sums[...], axis=1)
-
-
-def edge_body(slot, listed, partial, arrived, mask_strips, weights, d_fields,
+    for tile in range(4):
+        across = slice(tile * 128, (tile + 1) * 128)
+        held[tile * 128 : (tile + 1) * 128, :] = d_weight_in[:, across] * scale[0]
+        held[512 + tile * 128 : 512 + (tile + 1) * 128, :] = d_weight_out[:, across].T * scale[0]
+        at = AT_BIAS_IN + tile
+        held[at : at + 1, :] = jnp.sum(d_bias_in[:, across], axis=0, keepdims=True) * scale[0]
+    held[AT_KERNEL : AT_KERNEL + TAPS * TAPS, :] = jnp.sum(sums[...], axis=1) * scale[0]
+    for i in range(5):
+        at = AT_SMALL + i
+        held[at : at + 1, :] = jnp.sum(small[8 * i : 8 * i + 8, :], axis=0, keepdims=True) * scale[0]
+    held[AT_SMALL + 5 :, :] = jnp.zeros((held.shape[0] - AT_SMALL - 5, 128), F32)
+    packed[...] = held[...].astype(packed.dtype)
+
+
+def unpack_body(total, d_weight_in, d_weight_out, d_bias_in, d_kernel, small, held):
+    held[...] = total[...].astype(F32)
+    for tile in range(4):
+        across = slice(tile * 128, (tile + 1) * 128)
+        d_weight_in[:, across] = held[tile * 128 : (tile + 1) * 128, :]
+        at = AT_BIAS_IN + tile
+        d_bias_in[:, across] = held[at : at + 1, :]
+    d_weight_out[...] = held[512:1024, :]
+    d_kernel[...] = held[AT_KERNEL : AT_KERNEL + TAPS * TAPS, :]
+    small[...] = held[AT_SMALL : AT_SMALL + 8, :]
+
+
+def edge_body(place, partial, arrived, mask_strips, weights, d_fields,
               frame, columns, beside, top, bottom, left, right, sems):
     inner = SIDE - 2 * RADIUS
     parts = (
@@ -246,7 +333,7 @@
     ]
     for load in loads:
         load.start()
-    pick = picker(slot, listed, arrived)
+    pick = picker(place, arrived)
     frame[...] = jnp.zeros_like(frame)
     columns[...] = jnp.zeros_like(columns)
     for r in range(RADIUS):
@@ -314,7 +401,34 @@
 IN_SMEM = pl.BlockSpec(memory_space=pltpu.SMEM)
 
 
-def run_core(slot, listed, fields, arrived, cotangent, mask, tap_table, vectors, weights):
+def params():
+    return pltpu.CompilerParams(vmem_limit_bytes=VMEM_BYTES)
+
+
+def run_outgoing(place, fields, mask_strips):
+    return pl.pallas_call(
+        outgoing_body,
+        out_shape=jax.ShapeDtypeStruct((4 * STRIP_ROWS + 16, 128), BF16),
+        in_specs=[IN_SMEM] + [IN_VMEM] * 2,
+        out_specs=IN_VMEM,
+        scratch_shapes=[pltpu.VMEM((SIDE * 16, 128), F32)] * 2,
+        compiler_params=params(),
+        name="outgoing",
+    )(place, fields, mask_strips)
+
+
+def run_relay(place, lists, own, below, above):
+    return pl.pallas_call(
+        relay_body,
+        out_shape=jax.ShapeDtypeStruct((2 * GROUP * STRIP_ROWS, 128), BF16),
+        in_specs=[IN_SMEM] * 2 + [IN_VMEM] * 3,
+        out_specs=IN_VMEM,
+        compiler_params=params(),
+        name="relay",
+    )(place, lists, own, below, above)
+
+
+def run_core(place, fields, arrived, cotangent, mask, tap_table, vectors, weights):
     conv_bias, ln_gain, ln_bias, bias_in, bias_out, layer_scale = vectors
     weight_in, weight_out = weights
     shape = jax.ShapeDtypeStruct
@@ -323,53 +437,74 @@
         out_shape=(
             shape((SIDE, SIDE, 128), BF16),
             shape((ROWS * PITCH, 128), F32),
-            shape((4, RADIUS, SIDE, 128), BF16),
+            shape((4 * STRIP_ROWS, 128), BF16),
             shape((ROWS * PITCH, 128), F32),
             shape((128, 512), F32),
             shape((128, 512), F32),
             shape((8, 512), F32),
             shape((40, 128), F32),
         ),
-        in_specs=[IN_SMEM, IN_SMEM] + [IN_VMEM] * 13,
+        in_specs=[IN_SMEM] + [IN_VMEM] * 13,
         out_specs=(IN_VMEM,) * 8,
         scratch_shapes=[
             pltpu.VMEM((TAPS, PAIRS, SIDE, 256), BF16),
             pltpu.VMEM((4 * SIDE, 128), F32),
             pltpu.VMEM((TAPS * 1024, 256), BF16),
         ],
-        compiler_params=pltpu.CompilerParams(vmem_limit_bytes=VMEM_BYTES),
+        compiler_params=params(),
+        cost_estimate=pl.CostEstimate(flops=22_000_000_000, bytes_accessed=8_000_000, transcendentals=0),
         name="core",
-    )(slot, listed, fields, arrived, cotangent, mask, tap_table, conv_bias, ln_gain, ln_bias,
+    )(place, fields, arrived, cotangent, mask, tap_table, conv_bias, ln_gain, ln_bias,
       weight_in, bias_in, weight_out, bias_out, layer_scale)
 
 
-def run_inner(padded, d_conv, cotangent, mask, tap_table):
+def run_inner(rows, scale, padded, d_conv, cotangent, mask, tap_table, gradients):
     return pl.pallas_call(
         inner_body,
         out_shape=(
-            jax.ShapeDtypeStruct((TAPS * TAPS, 128), F32),
+            jax.ShapeDtypeStruct((rows, 128), BF16),
             jax.ShapeDtypeStruct((SIDE, SIDE, 128), F32),
         ),
-        in_specs=[IN_VMEM] * 5,
+        in_specs=[IN_SMEM] + [IN_VMEM] * 9,
         out_specs=(IN_VMEM,) * 2,
         scratch_shapes=[
             pltpu.VMEM((TAPS * TAPS, 8, 128), F32),
             pltpu.VMEM((TAPS, PAIRS, SIDE, 256), BF16),
             pltpu.VMEM((TAPS * 1024, 256), BF16),
+            pltpu.VMEM((rows, 128), F32),
         ],
-        compiler_params=pltpu.CompilerParams(vmem_limit_bytes=VMEM_BYTES),
+        compiler_params=params(),
         cost_estimate=pl.CostEstimate(flops=16_000_000_000, bytes_accessed=8_000_000, transcendentals=0),
         name="inner",
-    )(padded, d_conv, cotangent, mask, tap_table)
-
-
-def run_edge(slot, listed, partial, arrived, mask_strips, weights):
+    )(scale, padded, d_conv, cotangent, mask, tap_table, *gradients)
+
+
+def run_unpack(total):
+    shape = jax.ShapeDtypeStruct
+    return pl.pallas_call(
+        unpack_body,
+        out_shape=(
+            shape((128, 512), F32),
+            shape((512, 128), F32),
+            shape((1, 512), F32),
+            shape((TAPS * TAPS, 128), F32),
+            shape((8, 128), F32),
+        ),
+        in_specs=[IN_VMEM],
+        out_specs=(IN_VMEM,) * 5,
+        scratch_shapes=[pltpu.VMEM(total.shape, F32)],
+        compiler_params=params(),
+        name="unpack",
+    )(total)
+
+
+def run_edge(place, partial, arrived, mask_strips, weights):
     rim = pltpu.VMEM((RADIUS, SIDE, 128), F32)
     side = pltpu.VMEM((SIDE - 2 * RADIUS, 8, 128), F32)
     return pl.pallas_call(
         edge_body,
         out_shape=jax.ShapeDtypeStruct((SIDE, SIDE, 128), F32),
-        in_specs=[IN_SMEM, IN_SMEM, pl.BlockSpec(memory_space=pl.ANY)] + [IN_VMEM] * 3,
+        in_specs=[IN_SMEM, pl.BlockSpec(memory_space=pl.ANY)] + [IN_VMEM] * 3,
         out_specs=pl.BlockSpec(memory_space=pl.ANY),
         scratch_shapes=[
             pltpu.VMEM((2, RADIUS, PITCH, 128), F32),
@@ -378,76 +513,39 @@
             rim, rim, side, side,
             pltpu.SemaphoreType.DMA((4,)),
         ],
-        input_output_aliases={2: 0},
-        compiler_params=pltpu.CompilerParams(vmem_limit_bytes=VMEM_BYTES),
+        input_output_aliases={1: 0},
+        compiler_params=params(),
+        cost_estimate=pl.CostEstimate(flops=4_000_000_000, bytes_accessed=1_000_000, transcendentals=0),
         name="edge",
-    )(slot, listed, partial, arrived, mask_strips, weights)
-
-
-def frame_strips(tile, radius):
-    extent = tile.shape[0]
-    left_cols = jnp.swapaxes(tile[:, :radius], 0, 1)
-    right_cols = jnp.swapaxes(tile[:, extent - radius :], 0, 1)
-    return jnp.stack([tile[:radius], tile[extent - radius :], left_cols, right_cols], axis=0)
-
-
-GROUP = 8
-STRIP_FOR = (1, 0, 3, 2, 1, 1, 0, 0)
-OPPOSITE = (1, 0, 3, 2, 7, 6, 5, 4)
-
-
-def halo_maps(neighbours):
+    )(place, partial, arrived, mask_strips, weights)
+
+
+def strip_lines(plane):
+    far = plane.shape[0] - RADIUS
+    across = plane.T
+    return jnp.stack([plane[:RADIUS], plane[far:], across[:RADIUS], across[far:]], axis=0)
+
+
+def swap_groups(value):
     peers = lax.axis_size("tiles")
-    device = lax.axis_index("tiles")
-    group = device // GROUP
-    place = device % GROUP
-    mine = neighbours[0]
-    below = lax.ppermute(mine, "tiles", [(i, i + GROUP) for i in range(peers - GROUP)])
-    above = lax.ppermute(mine, "tiles", [(i + GROUP, i) for i in range(peers - GROUP)])
-    dest = jnp.arange(GROUP, dtype=jnp.int32)
-    strip_of_side = jnp.array([STRIP_FOR[OPPOSITE[side]] for side in range(8)], jnp.int32)
-
-    def strip_to(listing):
-        hit = listing[None, :] == (group * GROUP + dest)[:, None]
-        return jnp.sum(jnp.where(hit, strip_of_side[None, :], 0), axis=1)
-
-    own = strip_to(mine)
-    relayed = jnp.where(dest < place, 4 + strip_to(below), 8 + strip_to(above))
-    send_index = jnp.stack([own, relayed], axis=1).reshape(-1)
-    listed = mine >= 0
-    slot = jnp.where(listed, (mine % GROUP) * 2 + (mine // GROUP != group), 0)
-    return send_index, slot.astype(jnp.int32), listed.astype(jnp.int32)
-
-
-def exchange(strips, maps):
-    send_index = maps[0]
+    below = lax.ppermute(value, "tiles", [(i, i + GROUP) for i in range(peers - GROUP)])
+    above = lax.ppermute(value, "tiles", [(i + GROUP, i) for i in range(peers - GROUP)])
+    return below, above
+
+
+def within_group(blocks):
     peers = lax.axis_size("tiles")
-    below = lax.ppermute(strips, "tiles", [(i, i + GROUP) for i in range(peers - GROUP)])
-    above = lax.ppermute(strips, "tiles", [(i + GROUP, i) for i in range(peers - GROUP)])
-    table = jnp.concatenate([strips, below, above], axis=0)
-    blocks = jnp.take(table, send_index, axis=0, mode="clip")
-    blocks = blocks.reshape((GROUP, 2) + strips.shape[1:])
     groups = [list(range(g, g + GROUP)) for g in range(0, peers, GROUP)]
-    arrived = lax.all_to_all(blocks, "tiles", 0, 0, axis_index_groups=groups)
-    return arrived.reshape((GROUP * 2,) + strips.shape[1:])
-
-
-def sum_over_tiles(parts):
+    blocks = blocks.reshape(GROUP, -1, 128)
+    return lax.all_to_all(blocks, "tiles", 0, 0, axis_index_groups=groups).reshape(-1, 128)
+
+
+def sum_over_tiles(packed):
     peers = lax.axis_size("tiles")
-    flat = jnp.concatenate([part.reshape(-1, 128) for part in parts], axis=0)
-    rows = flat.shape[0]
-    block = -(-rows // (peers * 8)) * 8
-    flat = jnp.pad(flat, ((0, peers * block - rows), (0, 0))).reshape(peers, block, 128)
-    summed = jnp.sum(lax.all_to_all(flat, "tiles", 0, 0), axis=0)
-    shared = jnp.broadcast_to(summed.astype(jnp.bfloat16)[None], (peers, block, 128))
-    total = lax.all_to_all(shared, "tiles", 0, 0).reshape(-1, 128).astype(jnp.float32)
-    out = []
-    at = 0
-    for part in parts:
-        size = part.size // 128
-        out.append(total[at : at + size].reshape(part.shape))
-        at += size
-    return out
+    blocks = packed.reshape(peers, -1, 128)
+    summed = jnp.sum(lax.all_to_all(blocks, "tiles", 0, 0).astype(F32), axis=0)
+    shared = jnp.broadcast_to(summed.astype(BF16)[None], blocks.shape)
+    return lax.all_to_all(shared, "tiles", 0, 0).reshape(packed.shape)
 
 
 def per_device(
@@ -465,31 +563,34 @@
     bias_out,
     layer_scale,
 ):
-    tile_count = fields.shape[0]
-    tile_side = fields.shape[1]
+    peers = lax.axis_size("tiles")
+    device = lax.axis_index("tiles").astype(jnp.int32)
+    place = jnp.concatenate([neighbours[0], device[None]])
+    mask_strips = jnp.broadcast_to(
+        strip_lines(ocean_mask[0]).astype(F32)[..., None], (4, RADIUS, SIDE, 128)
+    )
+    own = run_outgoing(place, fields[0], mask_strips)
+    below, above = swap_groups(own)
+    lists = jnp.stack([below[-16, :8], above[-16, :8]]).astype(jnp.int32)
+    arrived = within_group(run_relay(place, lists, own, below, above))
     mask = jnp.broadcast_to(ocean_mask[0].astype(BF16)[..., None], fields.shape[1:])
-    maps = halo_maps(neighbours)
-    slot, listed = maps[1], maps[2]
-    mask_strips = frame_strips(ocean_mask[0].astype(F32)[..., None], RADIUS)
-    strips = frame_strips(fields[0], RADIUS) * mask_strips.astype(BF16)
-    arrived = exchange(strips, maps)
     vectors = [v.reshape(1, -1) for v in (conv_bias, ln_gain, ln_bias, bias_in, bias_out, layer_scale)]
-    updated, d_conv, strips, padded, d_weight_in, d_weight_out, d_bias_in, small = run_core(
-        slot, listed, fields[0], arrived, cotangent[0], mask, tap_rows(kernel), vectors,
+    updated, d_conv, strips, padded, *gradients = run_core(
+        place, fields[0], arrived, cotangent[0], mask, tap_rows(kernel), vectors,
         (weight_in, weight_out),
     )
-    arrived_back = exchange(strips, maps)
+    below, above = swap_groups(strips)
+    blocks = run_relay(place, lists, strips, below, above)
+    d_conv, blocks = lax.optimization_barrier((d_conv, blocks))
+    arrived = within_group(blocks)
     flipped = kernel[::-1, ::-1]
-    d_kernel, partial = run_inner(padded, d_conv, cotangent[0], mask, tap_rows(flipped))
-    grad_scale = 1.0 / math.sqrt(lax.axis_size("tiles") * tile_count * tile_side * tile_side)
-    small = jnp.sum(small.reshape(5, 8, 128), axis=1)
-    parts = [d_weight_in, d_weight_out, jnp.sum(d_bias_in, axis=0), d_kernel, small]
-    totals = sum_over_tiles([part * grad_scale for part in parts])
-    d_fields = run_edge(
-        slot, listed, partial, arrived_back,
-        jnp.broadcast_to(mask_strips, (4, RADIUS, SIDE, 128)), flipped.reshape(TAPS * TAPS, 128),
+    scale = jnp.full((1,), 1.0 / math.sqrt(peers * SIDE * SIDE), F32)
+    rows = -(-PACKED_ROWS // (peers * 8)) * (peers * 8)
+    packed, partial = run_inner(
+        rows, scale, padded, d_conv, cotangent[0], mask, tap_rows(flipped), gradients
     )
-    t_in, t_out, t_bias_in, t_kernel, t_small = totals
+    d_fields = run_edge(place, partial, arrived, mask_strips, flipped.reshape(TAPS * TAPS, 128))
+    t_in, t_out, t_bias_in, t_kernel, t_small = run_unpack(sum_over_tiles(packed))
     return (
         updated[None],
         d_fields[None],
@@ -498,8 +599,8 @@
         t_small[2],
         t_small[3],
         t_in,
-        t_bias_in,
-        t_out.T,
+        t_bias_in[0],
+        t_out,
         t_small[1],
         t_small[0],
     )

time: 149 us -> 147 us (0.987)
  blocking collectives: 0 us -> 18.1 us
  starting transfers between devices: 33.4 us -> 23.1 us
  Pallas kernels: 43.4 us -> 52.2 us
  local copies, waits for them, and re-layouts: 19.1 us -> 11.3 us
  waiting for transfers between devices: 46 us -> 39.1 us
  other arithmetic: 5 us -> 1.98 us
    all_to_all x0 -> x1, blocking collectives: none -> 18.1 us  [sum_over_tiles(): summed = jnp.sum(lax.all_to_all(blocks, 'tiles', 0, 0).astype(F32), axis=0)]
    ppermute x6 -> x4, waiting for transfers between devices: 17 us -> 7.33 us  [the longest x2 4.49 us: swap_groups(): lax.ppermute(value, 'tiles', [(i + GROUP, i) for i in range(peers - GROUP)])]
    pallas_call x1 -> x5, Pallas kernels: 16.6 us -> 25.3 us  [the longest x1 16.9 us: run_inner(): pl.pallas_call(inner_body, out_shape=(jax.ShapeDtypeStruct((rows, 128), B...]
    all_to_all x4 -> x3, starting transfers between devices: 16.3 us -> 10 us  [the longest x2 7.43 us: within_group(): lax.all_to_all(blocks, 'tiles', 0, 0, axis_index_groups=groups)]
    ppermute x6 -> x4, starting transfers between devices: 17.1 us -> 13.1 us  [the longest x2 10.5 us: swap_groups(): lax.ppermute(value, 'tiles', [(i, i + GROUP) for i in range(peers - GROUP)])]
    gather x2 -> x0, local copies, waits for them, and re-layouts: 2.99 us -> none  [exchange(): blocks = jnp.take(table, send_index, axis=0, mode='clip')]
    all_to_all x4 -> x3, waiting for transfers between devices: 29 us -> 31.7 us  [the longest x2 24.4 us: within_group(): lax.all_to_all(blocks, 'tiles', 0, 0, axis_index_groups=groups)]
    reshape x6 -> x0, local copies, waits for them, and re-layouts: 2.5 us -> none  [the longest x3 1.36 us: sum_over_tiles(): out.append(total[at:at + size].reshape(part.shape))]
  transfers between devices with their start and end apart: 10 -> 7, of which waited for: 7 -> 7; matrix products, arithmetic and copies ran while one was open for 8% -> 1% of each run, Pallas kernels for 3% -> 3%
where the time goes in v4:
time: 147 us; the launch traced here: 146 us
  Pallas kernels  52.2 us (36%)
  waiting for transfers between devices  39.1 us (27%)
  starting transfers between devices  23.1 us (16%)
  blocking collectives  18.1 us (12%)
  local copies, waits for them, and re-layouts  11.3 us (8%)
  other arithmetic  1.98 us (1%)
    all_to_all x2, waiting for transfers between devices, within_group(): lax.all_to_all(blocks, 'tiles', 0, 0, axis_index_groups=groups)  24.4 us
    pallas_call x1, Pallas kernels, run_core(): pl.pallas_call(core_body, out_shape=(shape((SIDE, SIDE, 128), BF16), shap...  22.8 us
    all_to_all x1, blocking collectives, sum_over_tiles(): summed = jnp.sum(lax.all_to_all(blocks, 'tiles', 0, 0).astype(F32), axis=0)  18.1 us
    pallas_call x1, Pallas kernels, run_inner(): pl.pallas_call(inner_body, out_shape=(jax.ShapeDtypeStruct((rows, 128), B...  16.9 us
    ppermute x2, starting transfers between devices, swap_groups(): lax.ppermute(value, 'tiles', [(i, i + GROUP) for i in range(peers - GROUP)])  10.5 us
    all_to_all x2, starting transfers between devices, within_group(): lax.all_to_all(blocks, 'tiles', 0, 0, axis_index_groups=groups)  7.43 us
    all_to_all x1, waiting for transfers between devices, sum_over_tiles(): return lax.all_to_all(shared, 'tiles', 0, 0).reshape(packed.shape)  7.37 us
    ppermute x2, waiting for transfers between devices, swap_groups(): lax.ppermute(value, 'tiles', [(i + GROUP, i) for i in range(peers - GROUP)])  4.49 us
  transfers between devices with their start and end apart: 7, of which 7 were waited for; matrix products, arithmetic and copies ran while one was open for 1% of the time, Pallas kernels for 3%

profile of v4, /device:TPU:0, one launch (start us, length us, event | category | flops | bytes accessed | tf_op | source)
XLA Modules:
  0.0 146.4 jit_solution(8053099661697915818)
XLA Ops:
  4.6 2.2 %outgoing.1.own = bf16[784,128]{1,0:T(8,128)(2,1)} custom-call(s32[9]{0:T(128)} %pad_add_fusion.place, bf16[64,64,128]{2,1,0:T(8,128)(2,1)} %bitcast.50, f32[4,3,64,128]{3,2,1,0:T(8,128)} %broadcast_in_dim.13.mask_strips), custom_call_target="tpu_custom_call" | custom-call | tf_op jit(solution)/shard_map/outgoing/pallas_call | solution.py:409
  6.8 1.3 collective-permute-start.1
  8.1 5.6 %collective-permute-start = (bf16[784,128]{1,0:T(8,128)(2,1)}, bf16[784,128]{1,0:T(8,128)(2,1)S(1)}, u32[]{:S(2)}, u32[]{:S(2)}) collective-permute-start(bf16[784,128]{1,0:T(8,128)(2,1)} %outgoing.1.own), channel_id=1, source_target_pairs={{0,8},{1,9},{2,10},{3,11},{4,12},{5,13},{6,14},{7,15},{8,16},{9,17... | collective-permute-start | bytes 602120 | tf_op jit(solution)/shard_map/ppermute | solution.py:531
  13.7 3.2 %collective-permute-done.1.above = bf16[784,128]{1,0:T(8,128)(2,1)S(1)} collective-permute-done((bf16[784,128]{1,0:T(8,128)(2,1)}, bf16[784,128]{1,0:T(8,128)(2,1)S(1)}, u32[]{:S(2)}, u32[]{:S(2)}) %collective-permute-start.1) | collective-permute-done | bytes 200736 | tf_op jit(solution)/shard_map/ppermute | solution.py:532
  16.9 1.3 collective-permute-done.below
  18.9 2.2 %relay.2 = bf16[3072,128]{1,0:T(8,128)(2,1)} custom-call(s32[9]{0:T(128)} %pad_add_fusion.place, s32[2,8]{1,0:T(2,128)} %maximum_convert_fusion.lists, bf16[784,128]{1,0:T(8,128)(2,1)} %outgoing.1.own, bf16[784,128]{1,0:T(8,128)(2,1)} %copy-done.5, bf16[784,128]{1,0:T(8,128)(2,1)} %copy-done.4), custom_call_target="tpu_custom_call" | custom-call | tf_op jit(solution)/shard_map/relay/pallas_call | solution.py:421
  21.1 3.9 %all-to-all-start = ((bf16[8,384,128]{2,1,0:T(8,128)(2,1)}), bf16[8,384,128]{2,1,0:T(8,128)(2,1)S(1)}, u32[]{:S(2)}, u32[]{:S(2)}) async-start(bf16[8,384,128]{2,1,0:T(8,128)(2,1)} %bitcast.48), calls=%async_computation | async-start | bytes 1572864 | tf_op jit(solution)/shard_map/all_to_all | solution.py:540
  25.7 11.9 %all-to-all-done = bf16[8,384,128]{2,1,0:T(8,128)(2,1)S(1)} async-done(((bf16[8,384,128]{2,1,0:T(8,128)(2,1)}), bf16[8,384,128]{2,1,0:T(8,128)(2,1)S(1)}, u32[]{:S(2)}, u32[]{:S(2)}) %all-to-all-start) | async-done | bytes 786464 | tf_op jit(solution)/shard_map/all_to_all | solution.py:540
  37.6 1.6 %broadcast_in_dim.14.mask = bf16[64,64,128]{2,1,0:T(8,128)(2,1)} broadcast(bf16[64,64]{1,0:T(8,128)(2,1)S(1)} %bitcast_convert_fusion), dimensions={0,1} | broadcast | bytes 1056768 | tf_op jit(solution)/shard_map/broadcast_in_dim | solution.py:576
  39.2 22.8 %core.1 = (bf16[64,64,128]{2,1,0:T(8,128)(2,1)}, f32[5040,128]{1,0:T(8,128)}, bf16[768,128]{1,0:T(8,128)(2,1)}, f32[5040,128]{1,0:T(8,128)}, f32[128,512]{1,0:T(...) custom-call(s32[9]{0:T(128)} %pad_add_fusion.place, bf16[64,64,128]{2,1,0:T(8,128)(2,1)} %bitcast.51, ...), custom_call_target="tpu_custom_call" | custom-call | flops 22000001024 | bytes 8000000 | tf_op jit(solution)/shard_map/core/pallas_call | solution.py:435
  62.1 1.3 collective-permute-start.3
  63.4 4.9 %collective-permute-start.2 = (bf16[768,128]{1,0:T(8,128)(2,1)}, bf16[768,128]{1,0:T(8,128)(2,1)S(1)}, u32[]{:S(2)}, u32[]{:S(2)}) collective-permute-start(bf16[768,128]{1,0:T(8,128)(2,1)} %get-tuple-element.31.own), channel_id=1, source_target_pairs={{0,8},{1,9},{2,10},{3,11},{4,12},{5,13},{6,14},{7,15},{8,16},{9,17... | collective-permute-start | bytes 589832 | tf_op jit(solution)/shard_map/ppermute | solution.py:531
  70.2 1.6 %collective-permute-done.2.below = bf16[768,128]{1,0:T(8,128)(2,1)S(1)} collective-permute-done((bf16[768,128]{1,0:T(8,128)(2,1)}, bf16[768,128]{1,0:T(8,128)(2,1)S(1)}, u32[]{:S(2)}, u32[]{:S(2)}) %collective-permute-start.2) | collective-permute-done | bytes 196640 | tf_op jit(solution)/shard_map/ppermute | solution.py:531
  72.4 2.3 %relay.3 = bf16[3072,128]{1,0:T(8,128)(2,1)} custom-call(s32[9]{0:T(128)} %pad_add_fusion.place, s32[2,8]{1,0:T(2,128)} %maximum_convert_fusion.lists, bf16[768,128]{1,0:T(8,128)(2,1)} %get-tuple-element.31.own, bf16[768,128]{1,0:T(8,128)(2,1)} %copy-done.7, bf16[768,128]{1,0:T(8,128)(2,1)} %copy-done.6), custom_call_target="tpu_custom_call" | custom-call | tf_op jit(solution)/shard_map/relay/pallas_call | solution.py:421
  74.7 16.9 %inner.1 = (bf16[1280,128]{1,0:T(8,128)(2,1)}, f32[64,64,128]{2,1,0:T(8,128)}) custom-call(f32[1]{0:T(128)} %constant.10.clone.1.scale, f32[5040,128]{1,0:T(8,128)} %get-tuple-element.29.padded, f32[5040,128]{1,0:T(8,128)} %get-tuple-element.32.d_conv, bf16[64,64,128]{2,1,0:T(8,128)(2,1)} %bitcast.60, bf16[64,64,128]{2,1,0:T(8,128)(2,1)} %broadcast_in_dim.14.mask, ...), custom_call_target="tpu_custom_call" | custom-call | flops 16000000000 | bytes 8000000 | tf_op jit(solution)/shard_map/inner/pallas_call | solution.py:462
  91.6 18.1 %all_to_all.20 = bf16[32,40,128]{2,1,0:T(8,128)(2,1)S(1)} all-to-all(bf16[32,40,128]{2,1,0:T(8,128)(2,1)} %bitcast.54), channel_id=1, replica_groups=mesh['tiles'=32] {'tiles'}, dimensions={0} | all-to-all | bytes 655360 | tf_op jit(solution)/shard_map/all_to_all | solution.py:546
  109.6 3.5 %all-to-all-start.1 = ((bf16[8,384,128]{2,1,0:T(8,128)(2,1)}), bf16[8,384,128]{2,1,0:T(8,128)(2,1)S(1)}, u32[]{:S(2)}, u32[]{:S(2)}) async-start(bf16[8,384,128]{2,1,0:T(8,128)(2,1)} %bitcast.23), calls=%async_computation.1 | async-start | bytes 1572864 | tf_op jit(solution)/shard_map/all_to_all | solution.py:540
  113.2 12.5 %all-to-all-done.1 = bf16[8,384,128]{2,1,0:T(8,128)(2,1)S(1)} async-done(((bf16[8,384,128]{2,1,0:T(8,128)(2,1)}), bf16[8,384,128]{2,1,0:T(8,128)(2,1)S(1)}, u32[]{:S(2)}, u32[]{:S(2)}) %all-to-all-start.1) | async-done | bytes 786464 | tf_op jit(solution)/shard_map/all_to_all | solution.py:540
  126.6 2.6 %all-to-all-start.3 = ((bf16[32,40,128]{2,1,0:T(8,128)(2,1)}), bf16[32,40,128]{2,1,0:T(8,128)(2,1)S(1)}, u32[]{:S(2)}, u32[]{:S(2)}) async-start(bf16[32,40,128]{2,1,0:T(8,128)(2,1)} %broadcast_in_dim.32), calls=%async_computation.3 | async-start | bytes 655360 | tf_op jit(solution)/shard_map/all_to_all | solution.py:548
  129.8 4.0 %edge.1 = f32[64,64,128]{2,1,0:T(8,128)} custom-call(s32[9]{0:T(128)} %pad_add_fusion.place, f32[64,64,128]{2,1,0:T(8,128)} %get-tuple-element.37.partial, bf16[3072,128]{1,0:T(8,128)(2,1)} %bitcast.53, f32[4,3,64,128]{3,2,1,0:T(8,128)} %broadcast_in_dim.13.mask_strips, f32[49,128]{1,0:T(8,128)} %reshape.123.weights), custom_call_target="tpu_custom_call", output_to_operand_aliasing={{}: (1, {})} | custom-call | flops 4000000000 | bytes 1000000 | tf_op jit(solution)/shard_map/edge/pallas_call | solution.py:504
  133.8 7.4 %all-to-all-done.3 = bf16[32,40,128]{2,1,0:T(8,128)(2,1)S(1)} async-done(((bf16[32,40,128]{2,1,0:T(8,128)(2,1)}), bf16[32,40,128]{2,1,0:T(8,128)(2,1)S(1)}, u32[]{:S(2)}, u32[]{:S(2)}) %all-to-all-start.3) | async-done | bytes 327712 | tf_op jit(solution)/shard_map/all_to_all | solution.py:548
  141.9 1.8 %unpack.1 = (f32[128,512]{1,0:T(8,128)}, f32[512,128]{1,0:T(8,128)}, f32[1,512]{1,0:T(1,128)}, f32[49,128]{1,0:T(8,128)}, f32[8,128]{1,0:T(8,128)}) custom-call(bf16[1280,128]{1,0:T(8,128)(2,1)} %bitcast.49), custom_call_target="tpu_custom_call" | custom-call | tf_op jit(solution)/shard_map/unpack/pallas_call | solution.py:484
  143.7 1.4 reshape.126
  145.0 1.4 slice_bitcast_fusion.2
  (41 shorter events, 10.1 us)
Async XLA Ops:
  2.3 22.7 %copy-start.8 = (f32[7,7,128]{2,1,0:T(8,128)S(1)}, f32[7,7,128]{2,1,0:T(8,128)}, u32[]{:S(2)}) copy-start(f32[7,7,128]{2,1,0:T(8,128)} %param.17) | copy-start | bytes 75268
  4.6 21.1 %copy-start.3 = (s32[1,64,64]{2,1,0:T(8,128)S(1)}, s32[1,64,64]{2,1,0:T(8,128)}, u32[]{:S(2)}) copy-start(s32[1,64,64]{2,1,0:T(8,128)} %param.15) | copy-start | bytes 49156
  6.8 10.1 %collective-permute-start.1 = (bf16[784,128]{1,0:T(8,128)(2,1)}, bf16[784,128]{1,0:T(8,128)(2,1)S(1)}, u32[]{:S(2)}, u32[]{:S(2)}) collective-permute-start(bf16[784,128]{1,0:T(8,128)(2,1)} %outgoing.1.own), channel_id=1, source_target_pairs={{8,0},{9,1},{10,2},{11,3},{12,4},{13,5},{14,6},{15,7},{16,8},{17,9... | collective-permute-start | bytes 602120 | tf_op jit(solution)/shard_map/ppermute | solution.py:532
  8.1 10.1 %collective-permute-start = (bf16[784,128]{1,0:T(8,128)(2,1)}, bf16[784,128]{1,0:T(8,128)(2,1)S(1)}, u32[]{:S(2)}, u32[]{:S(2)}) collective-permute-start(bf16[784,128]{1,0:T(8,128)(2,1)} %outgoing.1.own), channel_id=1, source_target_pairs={{0,8},{1,9},{2,10},{3,11},{4,12},{5,13},{6,14},{7,15},{8,16},{9,17... | collective-permute-start | bytes 602120 | tf_op jit(solution)/shard_map/ppermute | solution.py:531
  16.9 1.9 %copy-start.4 = (bf16[784,128]{1,0:T(8,128)(2,1)}, bf16[784,128]{1,0:T(8,128)(2,1)S(1)}, u32[]{:S(2)}) copy-start(bf16[784,128]{1,0:T(8,128)(2,1)S(1)} %collective-permute-done.1.above) | copy-start | bytes 602116
  18.2 0.7 copy-start.5
  21.1 16.5 %all-to-all-start = ((bf16[8,384,128]{2,1,0:T(8,128)(2,1)}), bf16[8,384,128]{2,1,0:T(8,128)(2,1)S(1)}, u32[]{:S(2)}, u32[]{:S(2)}) async-start(bf16[8,384,128]{2,1,0:T(8,128)(2,1)} %bitcast.48), calls=%async_computation | async-start | bytes 1572864 | tf_op jit(solution)/shard_map/all_to_all | solution.py:540
  37.6 1.6 %copy-start.1 = (bf16[8,384,128]{2,1,0:T(8,128)(2,1)}, bf16[8,384,128]{2,1,0:T(8,128)(2,1)S(1)}, u32[]{:S(2)}) copy-start(bf16[8,384,128]{2,1,0:T(8,128)(2,1)S(1)} %all-to-all-done) | copy-start | bytes 2359300
  62.1 8.1 %collective-permute-start.3 = (bf16[768,128]{1,0:T(8,128)(2,1)}, bf16[768,128]{1,0:T(8,128)(2,1)S(1)}, u32[]{:S(2)}, u32[]{:S(2)}) collective-permute-start(bf16[768,128]{1,0:T(8,128)(2,1)} %get-tuple-element.31.own), channel_id=1, source_target_pairs={{8,0},{9,1},{10,2},{11,3},{12,4},{13,5},{14,6},{15,7},{16,8},{17,9... | collective-permute-start | bytes 589832 | tf_op jit(solution)/shard_map/ppermute | solution.py:532
  63.4 8.4 %collective-permute-start.2 = (bf16[768,128]{1,0:T(8,128)(2,1)}, bf16[768,128]{1,0:T(8,128)(2,1)S(1)}, u32[]{:S(2)}, u32[]{:S(2)}) collective-permute-start(bf16[768,128]{1,0:T(8,128)(2,1)} %get-tuple-element.31.own), channel_id=1, source_target_pairs={{0,8},{1,9},{2,10},{3,11},{4,12},{5,13},{6,14},{7,15},{8,16},{9,17... | collective-permute-start | bytes 589832 | tf_op jit(solution)/shard_map/ppermute | solution.py:531
  70.2 1.6 %copy-start.6 = (bf16[768,128]{1,0:T(8,128)(2,1)}, bf16[768,128]{1,0:T(8,128)(2,1)S(1)}, u32[]{:S(2)}) copy-start(bf16[768,128]{1,0:T(8,128)(2,1)S(1)} %collective-permute-done.3.above) | copy-start | bytes 589828
  71.8 0.7 copy-start.7
  109.6 16.1 %all-to-all-start.1 = ((bf16[8,384,128]{2,1,0:T(8,128)(2,1)}), bf16[8,384,128]{2,1,0:T(8,128)(2,1)S(1)}, u32[]{:S(2)}, u32[]{:S(2)}) async-start(bf16[8,384,128]{2,1,0:T(8,128)(2,1)} %bitcast.23), calls=%async_computation.1 | async-start | bytes 1572864 | tf_op jit(solution)/shard_map/all_to_all | solution.py:540
  125.7 4.1 %copy-start.2 = (bf16[8,384,128]{2,1,0:T(8,128)(2,1)}, bf16[8,384,128]{2,1,0:T(8,128)(2,1)S(1)}, u32[]{:S(2)}) copy-start(bf16[8,384,128]{2,1,0:T(8,128)(2,1)S(1)} %all-to-all-done.1) | copy-start | bytes 2359300
  126.6 14.6 %all-to-all-start.3 = ((bf16[32,40,128]{2,1,0:T(8,128)(2,1)}), bf16[32,40,128]{2,1,0:T(8,128)(2,1)S(1)}, u32[]{:S(2)}, u32[]{:S(2)}) async-start(bf16[32,40,128]{2,1,0:T(8,128)(2,1)} %broadcast_in_dim.32), calls=%async_computation.3 | async-start | bytes 655360 | tf_op jit(solution)/shard_map/all_to_all | solution.py:548
  141.1 0.7 copy-start

commit v5 on v4

--- a/solution.py
+++ b/solution.py
@@ -96,11 +96,11 @@
     return total
 
 
-def picker(place, arrived):
-    group = lax.div(place[8], GROUP)
+def picker(place, device, arrived):
+    group = lax.div(device[0], GROUP)
 
     def pick(side, r):
-        tile = place[side]
+        tile = place[0, side]
         owner = jnp.maximum(tile, 0)
         slot = 2 * lax.rem(owner, GROUP) + jnp.where(lax.div(owner, GROUP) != group, 1, 0)
         at = pl.multiple_of(slot * STRIP_ROWS + r * SIDE, SIDE)
@@ -110,33 +110,38 @@
     return pick
 
 
-def outgoing_body(place, fields, mask_strips, out, near, far):
+def outgoing_body(place, fields, ocean_mask, out, mask_strips, near, far):
     def fill(i, carry):
         near[pl.ds(i * 16, 16), :] = fields[i, 0:16, :].astype(F32)
         far[pl.ds(i * 16, 16), :] = fields[i, SIDE - 16 : SIDE, :].astype(F32)
         return carry
 
     lax.fori_loop(0, SIDE, fill, 0, unroll=4)
+    live = ocean_mask[...].astype(F32)
+    across = live.T
     for r in range(RADIUS):
+        back = SIDE - RADIUS + r
         rows = (
-            fields[r].astype(F32),
-            fields[SIDE - RADIUS + r].astype(F32),
-            near[pl.ds(r, SIDE, stride=16), :],
-            far[pl.ds(16 - RADIUS + r, SIDE, stride=16), :],
-        )
-        for side in range(4):
+            (fields[r].astype(F32), across[:, r : r + 1]),
+            (fields[back].astype(F32), across[:, back : back + 1]),
+            (near[pl.ds(r, SIDE, stride=16), :], live[:, r : r + 1]),
+            (far[pl.ds(16 - RADIUS + r, SIDE, stride=16), :], live[:, back : back + 1]),
+        )
+        for side, (values, column) in enumerate(rows):
             at = side * STRIP_ROWS + r * SIDE
-            out[at : at + SIDE, :] = (rows[side] * mask_strips[side, r]).astype(BF16)
+            wide = jnp.broadcast_to(column, (SIDE, 128))
+            mask_strips[side, r] = wide
+            out[at : at + SIDE, :] = (values * wide).astype(BF16)
     lane = lax.broadcasted_iota(jnp.int32, (16, 128), 1)
     listing = jnp.zeros((16, 128), F32)
     for side in range(8):
-        listing = jnp.where(lane == side, place[side].astype(F32), listing)
+        listing = jnp.where(lane == side, place[0, side].astype(F32), listing)
     out[4 * STRIP_ROWS :, :] = listing.astype(BF16)
 
 
-def relay_body(place, lists, own, below, above, out):
-    group = lax.div(place[8], GROUP)
-    mine = lax.rem(place[8], GROUP)
+def relay_body(place, device, lists, own, paired, other, out):
+    group = lax.div(device[0], GROUP)
+    mine = lax.rem(device[0], GROUP)
 
     def strip_for(read, tile):
         strip = jnp.int32(0)
@@ -146,22 +151,23 @@
 
     for dest in range(GROUP):
         tile = group * GROUP + dest
-        at = strip_for(lambda side: place[side], tile)
+        at = strip_for(lambda side: place[0, side], tile)
         out[2 * dest * STRIP_ROWS : (2 * dest + 1) * STRIP_ROWS, :] = own[pl.ds(at, STRIP_ROWS), :]
-        at = strip_for(lambda side: jnp.where(dest < mine, lists[0, side], lists[1, side]), tile)
+        use_pair = (dest < mine) == (lax.rem(group, 2) == 1)
+        at = strip_for(lambda side: jnp.where(use_pair, lists[0, side], lists[1, side]), tile)
         out[(2 * dest + 1) * STRIP_ROWS : (2 * dest + 2) * STRIP_ROWS, :] = jnp.where(
-            dest < mine, below[pl.ds(at, STRIP_ROWS), :], above[pl.ds(at, STRIP_ROWS), :]
+            use_pair, paired[pl.ds(at, STRIP_ROWS), :], other[pl.ds(at, STRIP_ROWS), :]
         )
 
 
 def core_body(
-    place, fields, arrived, cotangent, mask, tap_table, conv_bias, ln_gain, ln_bias, weight_in,
+    place, device, fields, arrived, cotangent, mask, tap_table, conv_bias, ln_gain, ln_bias, weight_in,
     bias_in, weight_out, bias_out, layer_scale,
     updated, d_conv, strips, padded, d_weight_in, d_weight_out, d_bias_in, small,
     shifted, stage, taps,
 ):
     build_taps(tap_table, taps)
-    place_strips(picker(place, arrived), padded, stage)
+    place_strips(picker(place, device, arrived), padded, stage)
 
     def fill(i, carry):
         padded[pl.ds((i + RADIUS) * PITCH + RADIUS, SIDE), :] = fields[i].astype(F32) * mask[i].astype(F32)
@@ -306,7 +312,8 @@
     packed[...] = held[...].astype(packed.dtype)
 
 
-def unpack_body(total, d_weight_in, d_weight_out, d_bias_in, d_kernel, small, held):
+def unpack_body(total, d_weight_in, d_weight_out, d_bias_in, d_kernel, *rest):
+    small, held = rest[:5], rest[5]
     held[...] = total[...].astype(F32)
     for tile in range(4):
         across = slice(tile * 128, (tile + 1) * 128)
@@ -314,11 +321,13 @@
         at = AT_BIAS_IN + tile
         d_bias_in[:, across] = held[at : at + 1, :]
     d_weight_out[...] = held[512:1024, :]
-    d_kernel[...] = held[AT_KERNEL : AT_KERNEL + TAPS * TAPS, :]
-    small[...] = held[AT_SMALL : AT_SMALL + 8, :]
-
-
-def edge_body(place, partial, arrived, mask_strips, weights, d_fields,
+    for a in range(TAPS):
+        d_kernel[a] = held[AT_KERNEL + a * TAPS : AT_KERNEL + (a + 1) * TAPS, :]
+    for i in range(5):
+        small[i][...] = held[AT_SMALL + i : AT_SMALL + i + 1, :]
+
+
+def edge_body(place, device, partial, arrived, mask_strips, weights, d_fields,
               frame, columns, beside, top, bottom, left, right, sems):
     inner = SIDE - 2 * RADIUS
     parts = (
@@ -333,7 +342,7 @@
     ]
     for load in loads:
         load.start()
-    pick = picker(place, arrived)
+    pick = picker(place, device, arrived)
     frame[...] = jnp.zeros_like(frame)
     columns[...] = jnp.zeros_like(columns)
     for r in range(RADIUS):
@@ -405,30 +414,33 @@
     return pltpu.CompilerParams(vmem_limit_bytes=VMEM_BYTES)
 
 
-def run_outgoing(place, fields, mask_strips):
+def run_outgoing(place, fields, ocean_mask):
     return pl.pallas_call(
         outgoing_body,
-        out_shape=jax.ShapeDtypeStruct((4 * STRIP_ROWS + 16, 128), BF16),
+        out_shape=(
+            jax.ShapeDtypeStruct((4 * STRIP_ROWS + 16, 128), BF16),
+            jax.ShapeDtypeStruct((4, RADIUS, SIDE, 128), F32),
+        ),
         in_specs=[IN_SMEM] + [IN_VMEM] * 2,
-        out_specs=IN_VMEM,
+        out_specs=(IN_VMEM,) * 2,
         scratch_shapes=[pltpu.VMEM((SIDE * 16, 128), F32)] * 2,
         compiler_params=params(),
         name="outgoing",
-    )(place, fields, mask_strips)
-
-
-def run_relay(place, lists, own, below, above):
+    )(place, fields, ocean_mask)
+
+
+def run_relay(place, device, lists, own, paired, other):
     return pl.pallas_call(
         relay_body,
         out_shape=jax.ShapeDtypeStruct((2 * GROUP * STRIP_ROWS, 128), BF16),
-        in_specs=[IN_SMEM] * 2 + [IN_VMEM] * 3,
+        in_specs=[IN_SMEM] * 3 + [IN_VMEM] * 3,
         out_specs=IN_VMEM,
         compiler_params=params(),
         name="relay",
-    )(place, lists, own, below, above)
-
-
-def run_core(place, fields, arrived, cotangent, mask, tap_table, vectors, weights):
+    )(place, device, lists, own, paired, other)
+
+
+def run_core(place, device, fields, arrived, cotangent, mask, tap_table, vectors, weights):
     conv_bias, ln_gain, ln_bias, bias_in, bias_out, layer_scale = vectors
     weight_in, weight_out = weights
     shape = jax.ShapeDtypeStruct
@@ -444,7 +456,7 @@
             shape((8, 512), F32),
             shape((40, 128), F32),
         ),
-        in_specs=[IN_SMEM] + [IN_VMEM] * 13,
+        in_specs=[IN_SMEM] * 2 + [IN_VMEM] * 13,
         out_specs=(IN_VMEM,) * 8,
         scratch_shapes=[
             pltpu.VMEM((TAPS, PAIRS, SIDE, 256), BF16),
@@ -454,7 +466,7 @@
         compiler_params=params(),
         cost_estimate=pl.CostEstimate(flops=22_000_000_000, bytes_accessed=8_000_000, transcendentals=0),
         name="core",
-    )(place, fields, arrived, cotangent, mask, tap_table, conv_bias, ln_gain, ln_bias,
+    )(place, device, fields, arrived, cotangent, mask, tap_table, conv_bias, ln_gain, ln_bias,
       weight_in, bias_in, weight_out, bias_out, layer_scale)
 
 
@@ -487,24 +499,24 @@
             shape((128, 512), F32),
             shape((512, 128), F32),
             shape((1, 512), F32),
-            shape((TAPS * TAPS, 128), F32),
-            shape((8, 128), F32),
-        ),
+            shape((TAPS, TAPS, 128), F32),
+        )
+        + (shape((1, 128), F32),) * 5,
         in_specs=[IN_VMEM],
-        out_specs=(IN_VMEM,) * 5,
+        out_specs=(IN_VMEM,) * 9,
         scratch_shapes=[pltpu.VMEM(total.shape, F32)],
         compiler_params=params(),
         name="unpack",
     )(total)
 
 
-def run_edge(place, partial, arrived, mask_strips, weights):
+def run_edge(place, device, partial, arrived, mask_strips, weights):
     rim = pltpu.VMEM((RADIUS, SIDE, 128), F32)
     side = pltpu.VMEM((SIDE - 2 * RADIUS, 8, 128), F32)
     return pl.pallas_call(
         edge_body,
         out_shape=jax.ShapeDtypeStruct((SIDE, SIDE, 128), F32),
-        in_specs=[IN_SMEM, pl.BlockSpec(memory_space=pl.ANY)] + [IN_VMEM] * 3,
+        in_specs=[IN_SMEM, IN_SMEM, pl.BlockSpec(memory_space=pl.ANY)] + [IN_VMEM] * 3,
         out_specs=pl.BlockSpec(memory_space=pl.ANY),
         scratch_shapes=[
             pltpu.VMEM((2, RADIUS, PITCH, 128), F32),
@@ -513,24 +525,24 @@
             rim, rim, side, side,
             pltpu.SemaphoreType.DMA((4,)),
         ],
-        input_output_aliases={1: 0},
+        input_output_aliases={2: 0},
         compiler_params=params(),
         cost_estimate=pl.CostEstimate(flops=4_000_000_000, bytes_accessed=1_000_000, transcendentals=0),
         name="edge",
-    )(place, partial, arrived, mask_strips, weights)
-
-
-def strip_lines(plane):
-    far = plane.shape[0] - RADIUS
-    across = plane.T
-    return jnp.stack([plane[:RADIUS], plane[far:], across[:RADIUS], across[far:]], axis=0)
+    )(place, device, partial, arrived, mask_strips, weights)
 
 
 def swap_groups(value):
-    peers = lax.axis_size("tiles")
-    below = lax.ppermute(value, "tiles", [(i, i + GROUP) for i in range(peers - GROUP)])
-    above = lax.ppermute(value, "tiles", [(i + GROUP, i) for i in range(peers - GROUP)])
-    return below, above
+    groups = lax.axis_size("tiles") // GROUP
+
+    def swap(first):
+        pairs = []
+        for low in range(first, groups - 1, 2):
+            for i in range(low * GROUP, (low + 1) * GROUP):
+                pairs += [(i, i + GROUP), (i + GROUP, i)]
+        return lax.ppermute(value, "tiles", pairs)
+
+    return swap(0), swap(1)
 
 
 def within_group(blocks):
@@ -564,23 +576,20 @@
     layer_scale,
 ):
     peers = lax.axis_size("tiles")
-    device = lax.axis_index("tiles").astype(jnp.int32)
-    place = jnp.concatenate([neighbours[0], device[None]])
-    mask_strips = jnp.broadcast_to(
-        strip_lines(ocean_mask[0]).astype(F32)[..., None], (4, RADIUS, SIDE, 128)
-    )
-    own = run_outgoing(place, fields[0], mask_strips)
-    below, above = swap_groups(own)
-    lists = jnp.stack([below[-16, :8], above[-16, :8]]).astype(jnp.int32)
-    arrived = within_group(run_relay(place, lists, own, below, above))
+    device = lax.axis_index("tiles").astype(jnp.int32).reshape(1)
+    own, mask_strips = run_outgoing(neighbours, fields[0], ocean_mask[0])
+    paired, other = swap_groups(own)
     mask = jnp.broadcast_to(ocean_mask[0].astype(BF16)[..., None], fields.shape[1:])
+    lists = jnp.stack([paired[-16, :8], other[-16, :8]]).astype(jnp.int32)
+    lists, mask = lax.optimization_barrier((lists, mask))
+    arrived = within_group(run_relay(neighbours, device, lists, own, paired, other))
     vectors = [v.reshape(1, -1) for v in (conv_bias, ln_gain, ln_bias, bias_in, bias_out, layer_scale)]
     updated, d_conv, strips, padded, *gradients = run_core(
-        place, fields[0], arrived, cotangent[0], mask, tap_rows(kernel), vectors,
+        neighbours, device, fields[0], arrived, cotangent[0], mask, tap_rows(kernel), vectors,
         (weight_in, weight_out),
     )
-    below, above = swap_groups(strips)
-    blocks = run_relay(place, lists, strips, below, above)
+    paired, other = swap_groups(strips)
+    blocks = run_relay(neighbours, device, lists, strips, paired, other)
     d_conv, blocks = lax.optimization_barrier((d_conv, blocks))
     arrived = within_group(blocks)
     flipped = kernel[::-1, ::-1]
@@ -589,20 +598,22 @@
     packed, partial = run_inner(
         rows, scale, padded, d_conv, cotangent[0], mask, tap_rows(flipped), gradients
     )
-    d_fields = run_edge(place, partial, arrived, mask_strips, flipped.reshape(TAPS * TAPS, 128))
-    t_in, t_out, t_bias_in, t_kernel, t_small = run_unpack(sum_over_tiles(packed))
+    packed, arrived = lax.optimization_barrier((packed, arrived))
+    weights = flipped.reshape(TAPS * TAPS, 128)
+    d_fields = run_edge(neighbours, device, partial, arrived, mask_strips, weights)
+    t_in, t_out, t_bias_in, t_kernel, *t_small = run_unpack(sum_over_tiles(packed))
     return (
         updated[None],
         d_fields[None],
-        t_kernel.reshape(kernel.shape),
-        t_small[4],
-        t_small[2],
-        t_small[3],
+        t_kernel,
+        t_small[4][0],
+        t_small[2][0],
+        t_small[3][0],
         t_in,
         t_bias_in[0],
         t_out,
-        t_small[1],
-        t_small[0],
+        t_small[1][0],
+        t_small[0][0],
     )
 
 

time: 147 us -> 127 us (0.86)
  waiting for transfers between devices: 39.1 us -> 26.6 us
  local copies, waits for them, and re-layouts: 11.3 us -> 6.62 us
  starting transfers between devices: 23.1 us -> 20.6 us
    all_to_all x2, waiting for transfers between devices: 24.4 us -> 11.9 us  [within_group(): lax.all_to_all(blocks, 'tiles', 0, 0, axis_index_groups=groups)]
    ppermute x4, starting transfers between devices: 13.1 us -> 10.7 us  [swap(): return lax.ppermute(value, 'tiles', pairs)]
  transfers between devices with their start and end apart: 7 -> 7, of which waited for: 7 -> 4; matrix products, arithmetic and copies ran while one was open for 1% -> 2% of each run, Pallas kernels for 3% -> 17%
where the time goes in v5:
time: 127 us; the launch traced here: 126 us
  Pallas kernels  52.5 us (41%)
  waiting for transfers between devices  26.6 us (21%)
  starting transfers between devices  20.6 us (16%)
  blocking collectives  17.7 us (14%)
  local copies, waits for them, and re-layouts  6.62 us (5%)
  other arithmetic  1.46 us (1%)
    pallas_call x1, Pallas kernels, run_core(): pl.pallas_call(core_body, out_shape=(shape((SIDE, SIDE, 128), BF16), shap...  22.9 us
    all_to_all x1, blocking collectives, sum_over_tiles(): summed = jnp.sum(lax.all_to_all(blocks, 'tiles', 0, 0).astype(F32), axis=0)  17.7 us
    pallas_call x1, Pallas kernels, run_inner(): pl.pallas_call(inner_body, out_shape=(jax.ShapeDtypeStruct((rows, 128), B...  16.9 us
    all_to_all x2, waiting for transfers between devices, within_group(): lax.all_to_all(blocks, 'tiles', 0, 0, axis_index_groups=groups)  11.9 us
    ppermute x4, starting transfers between devices, swap(): return lax.ppermute(value, 'tiles', pairs)  10.7 us
    all_to_all x1, waiting for transfers between devices, sum_over_tiles(): return lax.all_to_all(shared, 'tiles', 0, 0).reshape(packed.shape)  7.37 us
    ppermute x4, waiting for transfers between devices, swap(): return lax.ppermute(value, 'tiles', pairs)  7.35 us
    all_to_all x2, starting transfers between devices, within_group(): lax.all_to_all(blocks, 'tiles', 0, 0, axis_index_groups=groups)  7.27 us
  transfers between devices with their start and end apart: 7, of which 4 were waited for; matrix products, arithmetic and copies ran while one was open for 2% of the time, Pallas kernels for 17%

profile of v5, /device:TPU:0, one launch (start us, length us, event | category | flops | bytes accessed | tf_op | source)
XLA Modules:
  0.0 126.2 jit_solution(14582440436503500218)
XLA Ops:
  0.7 2.4 %outgoing.1 = (bf16[784,128]{1,0:T(8,128)(2,1)}, f32[4,3,64,128]{3,2,1,0:T(8,128)}) custom-call(s32[1,8]{1,0:T(1,128)} %place.9, bf16[64,64,128]{2,1,0:T(8,128)(2,1)} %bitcast.38, s32[64,64]{1,0:T(8,128)} %bitcast.43), custom_call_target="tpu_custom_call" | custom-call | tf_op jit(solution)/shard_map/outgoing/pallas_call | solution.py:418
  3.7 5.9 %collective-permute-start = (bf16[784,128]{1,0:T(8,128)(2,1)}, bf16[784,128]{1,0:T(8,128)(2,1)S(1)}, u32[]{:S(2)}, u32[]{:S(2)}) collective-permute-start(bf16[784,128]{1,0:T(8,128)(2,1)} %get-tuple-element.38.own), channel_id=1, source_target_pairs={{0,8},{8,0},{1,9},{9,1},{2,10},{10,2},{3,11},{11,3},{4,12},{12,4},... | collective-permute-start | bytes 602120 | tf_op jit(solution)/shard_map/ppermute | solution.py:543
  9.6 0.8 bitcast_convert_fusion
  10.4 4.1 %collective-permute-done.paired = bf16[784,128]{1,0:T(8,128)(2,1)S(1)} collective-permute-done((bf16[784,128]{1,0:T(8,128)(2,1)}, bf16[784,128]{1,0:T(8,128)(2,1)S(1)}, u32[]{:S(2)}, u32[]{:S(2)}) %collective-permute-start) | collective-permute-done | bytes 200736 | tf_op jit(solution)/shard_map/ppermute | solution.py:543
  15.2 1.6 %broadcast_in_dim.8.mask = bf16[64,64,128]{2,1,0:T(8,128)(2,1)} broadcast(bf16[64,64]{1,0:T(8,128)(2,1)S(1)} %bitcast_convert_fusion), dimensions={0,1} | broadcast | bytes 1056768 | tf_op jit(solution)/shard_map/broadcast_in_dim | solution.py:582
  16.8 2.2 %relay.2 = bf16[3072,128]{1,0:T(8,128)(2,1)} custom-call(s32[1,8]{1,0:T(1,128)} %place.9, s32[1]{0:T(128)} %bitcast.device, s32[2,8]{1,0:T(2,128)} %maximum_convert_fusion.lists, bf16[784,128]{1,0:T(8,128)(2,1)} %get-tuple-element.38.own, bf16[784,128]{1,0:T(8,128)(2,1)} %copy-done.4, bf16[784,128]{1,0:T(8,128)(2,1)} %copy-done.3), custom_call_target="tpu_custom_call" | custom-call | tf_op jit(solution)/shard_map/relay/pallas_call | solution.py:433
  19.1 3.7 %all-to-all-start = ((bf16[8,384,128]{2,1,0:T(8,128)(2,1)}), bf16[8,384,128]{2,1,0:T(8,128)(2,1)S(1)}, u32[]{:S(2)}, u32[]{:S(2)}) async-start(bf16[8,384,128]{2,1,0:T(8,128)(2,1)} %bitcast.36), calls=%async_computation | async-start | bytes 1572864 | tf_op jit(solution)/shard_map/all_to_all | solution.py:552
  23.5 11.9 %all-to-all-done = bf16[8,384,128]{2,1,0:T(8,128)(2,1)S(1)} async-done(((bf16[8,384,128]{2,1,0:T(8,128)(2,1)}), bf16[8,384,128]{2,1,0:T(8,128)(2,1)S(1)}, u32[]{:S(2)}, u32[]{:S(2)}) %all-to-all-start) | async-done | bytes 786464 | tf_op jit(solution)/shard_map/all_to_all | solution.py:552
  35.4 0.9 copy-done.2
  36.3 22.9 %core.1 = (bf16[64,64,128]{2,1,0:T(8,128)(2,1)}, f32[5040,128]{1,0:T(8,128)}, bf16[768,128]{1,0:T(8,128)(2,1)}, f32[5040,128]{1,0:T(8,128)}, f32[128,512]{1,0:T(...) custom-call(s32[1,8]{1,0:T(1,128)} %place.9, s32[1]{0:T(128)} %bitcast.device, ...), custom_call_target="tpu_custom_call" | custom-call | flops 22000001024 | bytes 8000000 | tf_op jit(solution)/shard_map/core/pallas_call | solution.py:447
  59.1 0.7 collective-permute-start.3
  59.8 3.5 %collective-permute-start.2 = (bf16[768,128]{1,0:T(8,128)(2,1)}, bf16[768,128]{1,0:T(8,128)(2,1)S(1)}, u32[]{:S(2)}, u32[]{:S(2)}) collective-permute-start(bf16[768,128]{1,0:T(8,128)(2,1)} %get-tuple-element.44.own), channel_id=1, source_target_pairs={{0,8},{8,0},{1,9},{9,1},{2,10},{10,2},{3,11},{11,3},{4,12},{12,4},... | collective-permute-start | bytes 589832 | tf_op jit(solution)/shard_map/ppermute | solution.py:543
  63.9 3.2 %collective-permute-done.2.paired = bf16[768,128]{1,0:T(8,128)(2,1)S(1)} collective-permute-done((bf16[768,128]{1,0:T(8,128)(2,1)}, bf16[768,128]{1,0:T(8,128)(2,1)S(1)}, u32[]{:S(2)}, u32[]{:S(2)}) %collective-permute-start.2) | collective-permute-done | bytes 196640 | tf_op jit(solution)/shard_map/ppermute | solution.py:543
  67.1 0.7 copy-done.6
  67.8 2.3 %relay.3 = bf16[3072,128]{1,0:T(8,128)(2,1)} custom-call(s32[1,8]{1,0:T(1,128)} %place.9, s32[1]{0:T(128)} %bitcast.device, s32[2,8]{1,0:T(2,128)} %maximum_convert_fusion.lists, bf16[768,128]{1,0:T(8,128)(2,1)} %get-tuple-element.44.own, bf16[768,128]{1,0:T(8,128)(2,1)} %copy-done.6, bf16[768,128]{1,0:T(8,128)(2,1)} %copy-done.5), custom_call_target="tpu_custom_call" | custom-call | tf_op jit(solution)/shard_map/relay/pallas_call | solution.py:433
  70.1 3.5 %all-to-all-start.1 = ((bf16[8,384,128]{2,1,0:T(8,128)(2,1)}), bf16[8,384,128]{2,1,0:T(8,128)(2,1)S(1)}, u32[]{:S(2)}, u32[]{:S(2)}) async-start(bf16[8,384,128]{2,1,0:T(8,128)(2,1)} %bitcast.35), calls=%async_computation.1 | async-start | bytes 1572864 | tf_op jit(solution)/shard_map/all_to_all | solution.py:552
  73.6 16.9 %inner.1 = (bf16[1280,128]{1,0:T(8,128)(2,1)}, f32[64,64,128]{2,1,0:T(8,128)}) custom-call(f32[1]{0:T(128)} %constant.10.clone.1.scale, f32[5040,128]{1,0:T(8,128)} %get-tuple-element.42.padded, f32[5040,128]{1,0:T(8,128)} %get-tuple-element.45.d_conv, bf16[64,64,128]{2,1,0:T(8,128)(2,1)} %bitcast.47, bf16[64,64,128]{2,1,0:T(8,128)(2,1)} %broadcast_in_dim.8.mask, ...), custom_call_target="tpu_custom_call" | custom-call | flops 16000000000 | bytes 8000000 | tf_op jit(solution)/shard_map/inner/pallas_call | solution.py:474
  90.5 17.7 %all_to_all.20 = bf16[32,40,128]{2,1,0:T(8,128)(2,1)S(1)} all-to-all(bf16[32,40,128]{2,1,0:T(8,128)(2,1)} %bitcast.42), channel_id=1, replica_groups=mesh['tiles'=32] {'tiles'}, dimensions={0} | all-to-all | bytes 655360 | tf_op jit(solution)/shard_map/all_to_all | solution.py:558
  108.3 0.8 broadcast_in_dim.21
  109.0 2.6 %all-to-all-start.3 = ((bf16[32,40,128]{2,1,0:T(8,128)(2,1)}), bf16[32,40,128]{2,1,0:T(8,128)(2,1)S(1)}, u32[]{:S(2)}, u32[]{:S(2)}) async-start(bf16[32,40,128]{2,1,0:T(8,128)(2,1)} %broadcast_in_dim.21), calls=%async_computation.3 | async-start | bytes 655360 | tf_op jit(solution)/shard_map/all_to_all | solution.py:560
  112.2 4.0 %edge.1 = f32[64,64,128]{2,1,0:T(8,128)} custom-call(s32[1,8]{1,0:T(1,128)} %place.9, s32[1]{0:T(128)} %bitcast.device, f32[64,64,128]{2,1,0:T(8,128)} %get-tuple-element.50.partial, bf16[3072,128]{1,0:T(8,128)(2,1)} %bitcast.40, f32[4,3,64,128]{3,2,1,0:T(8,128)} %get-tuple-element.54.mask_strips, ...), custom_call_target="tpu_custom_call", output_to_operand_aliasing={{}: (2, {})} | custom-call | flops 4000000000 | bytes 1000000 | tf_op jit(solution)/shard_map/edge/pallas_call | solution.py:516
  116.2 7.4 %all-to-all-done.3 = bf16[32,40,128]{2,1,0:T(8,128)(2,1)S(1)} async-done(((bf16[32,40,128]{2,1,0:T(8,128)(2,1)}), bf16[32,40,128]{2,1,0:T(8,128)(2,1)S(1)}, u32[]{:S(2)}, u32[]{:S(2)}) %all-to-all-start.3) | async-done | bytes 327712 | tf_op jit(solution)/shard_map/all_to_all | solution.py:560
  123.6 0.7 copy-done
  124.4 1.8 %unpack.1 = (f32[128,512]{1,0:T(8,128)}, f32[512,128]{1,0:T(8,128)}, f32[1,512]{1,0:T(1,128)}, f32[7,7,128]{2,1,0:T(8,128)}, f32[1,128]{1,0:T(1,128)}, /*index=5...) custom-call(bf16[1280,128]{1,0:T(8,128)(2,1)} %bitcast.37), custom_call_target="tpu_custom_call" | custom-call | tf_op jit(solution)/shard_map/unpack/pallas_call | solution.py:496
  (29 shorter events, 3.3 us)
Async XLA Ops:
  0.6 22.1 %copy-start.7 = (f32[7,7,128]{2,1,0:T(8,128)S(1)}, f32[7,7,128]{2,1,0:T(8,128)}, u32[]{:S(2)}) copy-start(f32[7,7,128]{2,1,0:T(8,128)} %param.17) | copy-start | bytes 75268
  3.1 7.3 %collective-permute-start.1 = (bf16[784,128]{1,0:T(8,128)(2,1)}, bf16[784,128]{1,0:T(8,128)(2,1)S(1)}, u32[]{:S(2)}, u32[]{:S(2)}) collective-permute-start(bf16[784,128]{1,0:T(8,128)(2,1)} %get-tuple-element.38.own), channel_id=1, source_target_pairs={{8,16},{16,8},{9,17},{17,9},{10,18},{18,10},{11,19},{19,11},{12,20... | collective-permute-start | bytes 602120 | tf_op jit(solution)/shard_map/ppermute | solution.py:543
  3.7 10.8 %collective-permute-start = (bf16[784,128]{1,0:T(8,128)(2,1)}, bf16[784,128]{1,0:T(8,128)(2,1)S(1)}, u32[]{:S(2)}, u32[]{:S(2)}) collective-permute-start(bf16[784,128]{1,0:T(8,128)(2,1)} %get-tuple-element.38.own), channel_id=1, source_target_pairs={{0,8},{8,0},{1,9},{9,1},{2,10},{10,2},{3,11},{11,3},{4,12},{12,4},... | collective-permute-start | bytes 602120 | tf_op jit(solution)/shard_map/ppermute | solution.py:543
  10.4 6.4 %copy-start.3 = (bf16[784,128]{1,0:T(8,128)(2,1)}, bf16[784,128]{1,0:T(8,128)(2,1)S(1)}, u32[]{:S(2)}) copy-start(bf16[784,128]{1,0:T(8,128)(2,1)S(1)} %collective-permute-done.1.other) | copy-start | bytes 602116
  14.6 2.2 %copy-start.4 = (bf16[784,128]{1,0:T(8,128)(2,1)}, bf16[784,128]{1,0:T(8,128)(2,1)S(1)}, u32[]{:S(2)}) copy-start(bf16[784,128]{1,0:T(8,128)(2,1)S(1)} %collective-permute-done.paired) | copy-start | bytes 602116
  19.1 16.3 %all-to-all-start = ((bf16[8,384,128]{2,1,0:T(8,128)(2,1)}), bf16[8,384,128]{2,1,0:T(8,128)(2,1)S(1)}, u32[]{:S(2)}, u32[]{:S(2)}) async-start(bf16[8,384,128]{2,1,0:T(8,128)(2,1)} %bitcast.36), calls=%async_computation | async-start | bytes 1572864 | tf_op jit(solution)/shard_map/all_to_all | solution.py:552
  35.4 0.9 copy-start.2
  59.1 4.8 %collective-permute-start.3 = (bf16[768,128]{1,0:T(8,128)(2,1)}, bf16[768,128]{1,0:T(8,128)(2,1)S(1)}, u32[]{:S(2)}, u32[]{:S(2)}) collective-permute-start(bf16[768,128]{1,0:T(8,128)(2,1)} %get-tuple-element.44.own), channel_id=1, source_target_pairs={{8,16},{16,8},{9,17},{17,9},{10,18},{18,10},{11,19},{19,11},{12,20... | collective-permute-start | bytes 589832 | tf_op jit(solution)/shard_map/ppermute | solution.py:543
  59.8 7.3 %collective-permute-start.2 = (bf16[768,128]{1,0:T(8,128)(2,1)}, bf16[768,128]{1,0:T(8,128)(2,1)S(1)}, u32[]{:S(2)}, u32[]{:S(2)}) collective-permute-start(bf16[768,128]{1,0:T(8,128)(2,1)} %get-tuple-element.44.own), channel_id=1, source_target_pairs={{0,8},{8,0},{1,9},{9,1},{2,10},{10,2},{3,11},{11,3},{4,12},{12,4},... | collective-permute-start | bytes 589832 | tf_op jit(solution)/shard_map/ppermute | solution.py:543
  63.9 3.2 %copy-start.5 = (bf16[768,128]{1,0:T(8,128)(2,1)}, bf16[768,128]{1,0:T(8,128)(2,1)S(1)}, u32[]{:S(2)}) copy-start(bf16[768,128]{1,0:T(8,128)(2,1)S(1)} %collective-permute-done.3.other) | copy-start | bytes 589828
  67.1 0.7 copy-start.6
  70.1 20.4 %all-to-all-start.1 = ((bf16[8,384,128]{2,1,0:T(8,128)(2,1)}), bf16[8,384,128]{2,1,0:T(8,128)(2,1)S(1)}, u32[]{:S(2)}, u32[]{:S(2)}) async-start(bf16[8,384,128]{2,1,0:T(8,128)(2,1)} %bitcast.35), calls=%async_computation.1 | async-start | bytes 1572864 | tf_op jit(solution)/shard_map/all_to_all | solution.py:552
  90.5 21.7 %copy-start.1 = (bf16[8,384,128]{2,1,0:T(8,128)(2,1)}, bf16[8,384,128]{2,1,0:T(8,128)(2,1)S(1)}, u32[]{:S(2)}) copy-start(bf16[8,384,128]{2,1,0:T(8,128)(2,1)S(1)} %all-to-all-done.1) | copy-start | bytes 2359300
  109.0 14.6 %all-to-all-start.3 = ((bf16[32,40,128]{2,1,0:T(8,128)(2,1)}), bf16[32,40,128]{2,1,0:T(8,128)(2,1)S(1)}, u32[]{:S(2)}, u32[]{:S(2)}) async-start(bf16[32,40,128]{2,1,0:T(8,128)(2,1)} %broadcast_in_dim.21), calls=%async_computation.3 | async-start | bytes 655360 | tf_op jit(solution)/shard_map/all_to_all | solution.py:560
  123.6 0.7 copy-start

commit v6 on v5

--- a/solution.py
+++ b/solution.py
@@ -22,7 +22,7 @@
 PITCH = 72
 ROWS = SIDE + 2 * RADIUS
 PAIRS = ROWS // 2
-BLOCK = 8
+BLOCK = 16
 AT_KERNEL = 1024
 AT_BIAS_IN = 1080
 AT_SMALL = 1088
@@ -110,6 +110,19 @@
     return pick
 
 
+def start_all(pairs, sems):
+    copies = [pltpu.make_async_copy(src, dst, sems.at[i]) for i, (src, dst) in enumerate(pairs)]
+    for copy in copies:
+        copy.start()
+    return copies
+
+
+def mask_body(ocean_mask, mask):
+    across = ocean_mask[...].astype(F32).T
+    for i in range(SIDE):
+        mask[i] = jnp.broadcast_to(across[:, i : i + 1], (SIDE, 128)).astype(BF16)
+
+
 def outgoing_body(place, fields, ocean_mask, out, mask_strips, near, far):
     def fill(i, carry):
         near[pl.ds(i * 16, 16), :] = fields[i, 0:16, :].astype(F32)
@@ -163,10 +176,17 @@
 def core_body(
     place, device, fields, arrived, cotangent, mask, tap_table, conv_bias, ln_gain, ln_bias, weight_in,
     bias_in, weight_out, bias_out, layer_scale,
-    updated, d_conv, strips, padded, d_weight_in, d_weight_out, d_bias_in, small,
-    shifted, stage, taps,
+    updated_out, d_conv_out, strips, padded_out, d_weight_in, d_weight_out, d_bias_in, small,
+    shifted, stage, taps, fields_in, arrived_in, cotangent_in, mask_in, updated, d_conv, padded,
+    in_sems, out_sems, row_sems,
 ):
+    loads = start_all(
+        ((mask, mask_in), (fields, fields_in), (arrived, arrived_in), (cotangent, cotangent_in)), in_sems
+    )
+    mask, fields, arrived, cotangent = mask_in, fields_in, arrived_in, cotangent_in
     build_taps(tap_table, taps)
+    for load in loads[:3]:
+        load.wait()
     place_strips(picker(place, device, arrived), padded, stage)
 
     def fill(i, carry):
@@ -174,7 +194,9 @@
         return carry
 
     lax.fori_loop(0, SIDE, fill, 0)
+    stores = start_all(((padded, padded_out),), out_sems)
     shift_copies(padded, shifted)
+    loads[3].wait()
     d_weight_in[...] = jnp.zeros_like(d_weight_in)
     d_weight_out[...] = jnp.zeros_like(d_weight_out)
     d_bias_in[...] = jnp.zeros_like(d_bias_in)
@@ -247,11 +269,26 @@
         small[16:24] += fold(d_lifted * normed)
         small[24:32] += fold(d_lifted)
         small[32:40] += fold(d_out)
+        for store in rows_out(index):
+            store.start()
         return following
+
+    def rows_out(index):
+        rows = pl.ds(index * BLOCK, BLOCK)
+        wide = pl.ds(pl.multiple_of((index * BLOCK + RADIUS) * PITCH, 8), BLOCK * PITCH)
+        return (
+            pltpu.make_async_copy(updated.at[rows], updated_out.at[rows], row_sems.at[0, index]),
+            pltpu.make_async_copy(d_conv.at[wide], d_conv_out.at[wide], row_sems.at[1, index]),
+        )
 
     both = conv_block(shifted, taps, 0, count)
     both = lax.fori_loop(0, SIDE // BLOCK - 1, step, both)
     step(SIDE // BLOCK - 1, both, last=True)
+    edge = RADIUS * PITCH
+    for i, rows in enumerate((pl.ds(0, edge), pl.ds(edge + SIDE * PITCH, edge))):
+        store = pltpu.make_async_copy(d_conv.at[rows], d_conv_out.at[rows], out_sems.at[1 + i])
+        store.start()
+        stores.append(store)
     for r in range(RADIUS):
         corner = RADIUS * PITCH + RADIUS
         far = SIDE - RADIUS + r
@@ -264,15 +301,27 @@
         for side in range(4):
             at = side * STRIP_ROWS + r * SIDE
             strips[at : at + SIDE, :] = rows[side].astype(BF16)
+    for index in range(SIDE // BLOCK):
+        stores += rows_out(index)
+    for store in stores:
+        store.wait()
 
 
 def inner_body(
     scale, padded, d_conv, cotangent, mask, tap_table, d_weight_in, d_weight_out, d_bias_in, small,
-    packed, d_fields, sums, shifted, taps, held,
+    packed, d_fields_out, sums, shifted, taps, held, padded_in, d_conv_in, cotangent_in, mask_in, d_fields,
+    in_sems, row_sems,
 ):
+    loads = start_all(
+        ((d_conv, d_conv_in), (padded, padded_in), (mask, mask_in), (cotangent, cotangent_in)), in_sems
+    )
+    d_conv, padded, mask, cotangent = d_conv_in, padded_in, mask_in, cotangent_in
     build_taps(tap_table, taps)
+    loads[0].wait()
     shift_copies(d_conv, shifted)
     sums[...] = jnp.zeros_like(sums)
+    for load in loads[1:]:
+        load.wait()
     count = BLOCK // 2
 
     def step(index, carry):
@@ -295,7 +344,12 @@
         back = jnp.stack([both[:, :, :128], both[:, :, 128:]], axis=1).reshape(BLOCK, SIDE, 128)
         live = mask[pl.ds(at, BLOCK)].astype(F32)
         d_fields[pl.ds(at, BLOCK)] = live * (live * cotangent[pl.ds(at, BLOCK)].astype(F32) + back)
+        rows_out(index).start()
         return carry
+
+    def rows_out(index):
+        rows = pl.ds(index * BLOCK, BLOCK)
+        return pltpu.make_async_copy(d_fields.at[rows], d_fields_out.at[rows], row_sems.at[index])
 
     lax.fori_loop(0, SIDE // BLOCK, step, 0)
     for tile in range(4):
@@ -310,6 +364,8 @@
         held[at : at + 1, :] = jnp.sum(small[8 * i : 8 * i + 8, :], axis=0, keepdims=True) * scale[0]
     held[AT_SMALL + 5 :, :] = jnp.zeros((held.shape[0] - AT_SMALL - 5, 128), F32)
     packed[...] = held[...].astype(packed.dtype)
+    for index in range(SIDE // BLOCK):
+        rows_out(index).wait()
 
 
 def unpack_body(total, d_weight_in, d_weight_out, d_bias_in, d_kernel, *rest):
@@ -405,13 +461,14 @@
         store.wait()
 
 
-VMEM_BYTES = 60 * 1024 * 1024
+MIB = 1024 * 1024
 IN_VMEM = pl.BlockSpec(memory_space=pltpu.VMEM)
 IN_SMEM = pl.BlockSpec(memory_space=pltpu.SMEM)
-
-
-def params():
-    return pltpu.CompilerParams(vmem_limit_bytes=VMEM_BYTES)
+ANYWHERE = pl.BlockSpec(memory_space=pl.ANY)
+
+
+def params(mib):
+    return pltpu.CompilerParams(vmem_limit_bytes=mib * MIB)
 
 
 def run_outgoing(place, fields, ocean_mask):
@@ -424,9 +481,21 @@
         in_specs=[IN_SMEM] + [IN_VMEM] * 2,
         out_specs=(IN_VMEM,) * 2,
         scratch_shapes=[pltpu.VMEM((SIDE * 16, 128), F32)] * 2,
-        compiler_params=params(),
+        compiler_params=params(64),
         name="outgoing",
     )(place, fields, ocean_mask)
+
+
+def run_mask(ocean_mask):
+    return pl.pallas_call(
+        mask_body,
+        out_shape=jax.ShapeDtypeStruct((SIDE, SIDE, 128), BF16),
+        in_specs=[IN_VMEM],
+        out_specs=IN_VMEM,
+        compiler_params=params(64),
+        cost_estimate=pl.CostEstimate(flops=4_000_000_000, bytes_accessed=1_000_000, transcendentals=0),
+        name="mask",
+    )(ocean_mask)
 
 
 def run_relay(place, device, lists, own, paired, other):
@@ -435,7 +504,7 @@
         out_shape=jax.ShapeDtypeStruct((2 * GROUP * STRIP_ROWS, 128), BF16),
         in_specs=[IN_SMEM] * 3 + [IN_VMEM] * 3,
         out_specs=IN_VMEM,
-        compiler_params=params(),
+        compiler_params=params(64),
         name="relay",
     )(place, device, lists, own, paired, other)
 
@@ -456,14 +525,24 @@
             shape((8, 512), F32),
             shape((40, 128), F32),
         ),
-        in_specs=[IN_SMEM] * 2 + [IN_VMEM] * 13,
-        out_specs=(IN_VMEM,) * 8,
+        in_specs=[IN_SMEM] * 2 + [ANYWHERE] * 4 + [IN_VMEM] * 9,
+        out_specs=(ANYWHERE, ANYWHERE, IN_VMEM, ANYWHERE) + (IN_VMEM,) * 4,
         scratch_shapes=[
             pltpu.VMEM((TAPS, PAIRS, SIDE, 256), BF16),
             pltpu.VMEM((4 * SIDE, 128), F32),
             pltpu.VMEM((TAPS * 1024, 256), BF16),
+            pltpu.VMEM((SIDE, SIDE, 128), BF16),
+            pltpu.VMEM((2 * GROUP * STRIP_ROWS, 128), BF16),
+            pltpu.VMEM((SIDE, SIDE, 128), BF16),
+            pltpu.VMEM((SIDE, SIDE, 128), BF16),
+            pltpu.VMEM((SIDE, SIDE, 128), BF16),
+            pltpu.VMEM((ROWS * PITCH, 128), F32),
+            pltpu.VMEM((ROWS * PITCH, 128), F32),
+            pltpu.SemaphoreType.DMA((4,)),
+            pltpu.SemaphoreType.DMA((3,)),
+            pltpu.SemaphoreType.DMA((2, SIDE // BLOCK)),
         ],
-        compiler_params=params(),
+        compiler_params=params(64),
         cost_estimate=pl.CostEstimate(flops=22_000_000_000, bytes_accessed=8_000_000, transcendentals=0),
         name="core",
     )(place, device, fields, arrived, cotangent, mask, tap_table, conv_bias, ln_gain, ln_bias,
@@ -477,15 +556,22 @@
             jax.ShapeDtypeStruct((rows, 128), BF16),
             jax.ShapeDtypeStruct((SIDE, SIDE, 128), F32),
         ),
-        in_specs=[IN_SMEM] + [IN_VMEM] * 9,
-        out_specs=(IN_VMEM,) * 2,
+        in_specs=[IN_SMEM] + [ANYWHERE] * 4 + [IN_VMEM] * 5,
+        out_specs=(IN_VMEM, ANYWHERE),
         scratch_shapes=[
             pltpu.VMEM((TAPS * TAPS, 8, 128), F32),
             pltpu.VMEM((TAPS, PAIRS, SIDE, 256), BF16),
             pltpu.VMEM((TAPS * 1024, 256), BF16),
             pltpu.VMEM((rows, 128), F32),
+            pltpu.VMEM((ROWS * PITCH, 128), F32),
+            pltpu.VMEM((ROWS * PITCH, 128), F32),
+            pltpu.VMEM((SIDE, SIDE, 128), BF16),
+            pltpu.VMEM((SIDE, SIDE, 128), BF16),
+            pltpu.VMEM((SIDE, SIDE, 128), F32),
+            pltpu.SemaphoreType.DMA((4,)),
+            pltpu.SemaphoreType.DMA((SIDE // BLOCK,)),
         ],
-        compiler_params=params(),
+        compiler_params=params(64),
         cost_estimate=pl.CostEstimate(flops=16_000_000_000, bytes_accessed=8_000_000, transcendentals=0),
         name="inner",
     )(scale, padded, d_conv, cotangent, mask, tap_table, *gradients)
@@ -505,7 +591,7 @@
         in_specs=[IN_VMEM],
         out_specs=(IN_VMEM,) * 9,
         scratch_shapes=[pltpu.VMEM(total.shape, F32)],
-        compiler_params=params(),
+        compiler_params=params(6),
         name="unpack",
     )(total)
 
@@ -516,8 +602,8 @@
     return pl.pallas_call(
         edge_body,
         out_shape=jax.ShapeDtypeStruct((SIDE, SIDE, 128), F32),
-        in_specs=[IN_SMEM, IN_SMEM, pl.BlockSpec(memory_space=pl.ANY)] + [IN_VMEM] * 3,
-        out_specs=pl.BlockSpec(memory_space=pl.ANY),
+        in_specs=[IN_SMEM, IN_SMEM, ANYWHERE] + [IN_VMEM] * 3,
+        out_specs=ANYWHERE,
         scratch_shapes=[
             pltpu.VMEM((2, RADIUS, PITCH, 128), F32),
             pltpu.VMEM((2, RADIUS, PITCH, 128), F32),
@@ -526,7 +612,7 @@
             pltpu.SemaphoreType.DMA((4,)),
         ],
         input_output_aliases={2: 0},
-        compiler_params=params(),
+        compiler_params=params(6),
         cost_estimate=pl.CostEstimate(flops=4_000_000_000, bytes_accessed=1_000_000, transcendentals=0),
         name="edge",
     )(place, device, partial, arrived, mask_strips, weights)
@@ -579,9 +665,8 @@
     device = lax.axis_index("tiles").astype(jnp.int32).reshape(1)
     own, mask_strips = run_outgoing(neighbours, fields[0], ocean_mask[0])
     paired, other = swap_groups(own)
-    mask = jnp.broadcast_to(ocean_mask[0].astype(BF16)[..., None], fields.shape[1:])
+    mask = run_mask(ocean_mask[0])
     lists = jnp.stack([paired[-16, :8], other[-16, :8]]).astype(jnp.int32)
-    lists, mask = lax.optimization_barrier((lists, mask))
     arrived = within_group(run_relay(neighbours, device, lists, own, paired, other))
     vectors = [v.reshape(1, -1) for v in (conv_bias, ln_gain, ln_bias, bias_in, bias_out, layer_scale)]
     updated, d_conv, strips, padded, *gradients = run_core(

time: 127 us -> 122 us (0.961)
  waiting for transfers between devices: 26.6 us -> 19.9 us
  local copies, waits for them, and re-layouts: 6.62 us -> 8.84 us
  starting transfers between devices: 20.6 us -> 22.3 us
    all_to_all x2, waiting for transfers between devices: 11.9 us -> 7.46 us  [within_group(): lax.all_to_all(blocks, 'tiles', 0, 0, axis_index_groups=groups)]
    pallas_call x0 -> x1, Pallas kernels: none -> 2.3 us  [run_mask(): pl.pallas_call(mask_body, out_shape=jax.ShapeDtypeStruct((SIDE, SIDE, 128...]
    all_to_all x1, waiting for transfers between devices: 7.37 us -> 5.69 us  [sum_over_tiles(): return lax.all_to_all(shared, 'tiles', 0, 0).reshape(packed.shape)]
    slice x2, local copies, waits for them, and re-layouts: 0.01 us -> 1.65 us  [tap_rows(): both = jnp.concatenate([wide[1:9], wide[0:8]], axis=2)]
    broadcast_in_dim x1 -> x0, local copies, waits for them, and re-layouts: 1.62 us -> none  [per_device(): jnp.broadcast_to(ocean_mask[0].astype(BF16)[..., None], fields.shape[1:])]
    pallas_call x1, Pallas kernels: 16.9 us -> 15.5 us  [run_inner(): pl.pallas_call(inner_body, out_shape=(jax.ShapeDtypeStruct((rows, 128), B...]
    rev x1, local copies, waits for them, and re-layouts: 0.02 us -> 1.37 us  [per_device(): flipped = kernel[::-1, ::-1]]
    all_to_all x2, starting transfers between devices: 7.27 us -> 8.59 us  [within_group(): lax.all_to_all(blocks, 'tiles', 0, 0, axis_index_groups=groups)]
  transfers between devices with their start and end apart: 7 -> 7, of which waited for: 4 -> 4; matrix products, arithmetic and copies ran while one was open for 2% -> 4% of each run, Pallas kernels for 17% -> 18%
where the time goes in v6:
time: 122 us; the launch traced here: 121 us
  Pallas kernels  51.9 us (43%)
  starting transfers between devices  22.3 us (18%)
  waiting for transfers between devices  19.9 us (16%)
  blocking collectives  17.1 us (14%)
  local copies, waits for them, and re-layouts  8.84 us (7%)
    pallas_call x1, Pallas kernels, run_core(): pl.pallas_call(core_body, out_shape=(shape((SIDE, SIDE, 128), BF16), shap...  22.5 us
    all_to_all x1, blocking collectives, sum_over_tiles(): summed = jnp.sum(lax.all_to_all(blocks, 'tiles', 0, 0).astype(F32), axis=0)  17.1 us
    pallas_call x1, Pallas kernels, run_inner(): pl.pallas_call(inner_body, out_shape=(jax.ShapeDtypeStruct((rows, 128), B...  15.5 us
    ppermute x4, starting transfers between devices, swap(): return lax.ppermute(value, 'tiles', pairs)  11.2 us
    all_to_all x2, starting transfers between devices, within_group(): lax.all_to_all(blocks, 'tiles', 0, 0, axis_index_groups=groups)  8.59 us
    all_to_all x2, waiting for transfers between devices, within_group(): lax.all_to_all(blocks, 'tiles', 0, 0, axis_index_groups=groups)  7.46 us
    ppermute x4, waiting for transfers between devices, swap(): return lax.ppermute(value, 'tiles', pairs)  6.73 us
    all_to_all x1, waiting for transfers between devices, sum_over_tiles(): return lax.all_to_all(shared, 'tiles', 0, 0).reshape(packed.shape)  5.69 us
  transfers between devices with their start and end apart: 7, of which 4 were waited for; matrix products, arithmetic and copies ran while one was open for 4% of the time, Pallas kernels for 18%

profile of v6, /device:TPU:0, one launch (start us, length us, event | category | flops | bytes accessed | tf_op | source)
XLA Modules:
  0.0 121.4 jit_solution(9840512491006903679)
XLA Ops:
  0.6 2.4 %outgoing.1 = (bf16[784,128]{1,0:T(8,128)(2,1)}, f32[4,3,64,128]{3,2,1,0:T(8,128)}) custom-call(s32[1,8]{1,0:T(1,128)} %place.9, bf16[64,64,128]{2,1,0:T(8,128)(2,1)} %bitcast.37, s32[64,64]{1,0:T(8,128)} %bitcast.42), custom_call_target="tpu_custom_call" | custom-call | tf_op jit(solution)/shard_map/outgoing/pallas_call | solution.py:475
  3.7 5.9 %collective-permute-start = (bf16[784,128]{1,0:T(8,128)(2,1)}, bf16[784,128]{1,0:T(8,128)(2,1)S(1)}, u32[]{:S(2)}, u32[]{:S(2)}) collective-permute-start(bf16[784,128]{1,0:T(8,128)(2,1)} %get-tuple-element.36.own), channel_id=1, source_target_pairs={{0,8},{8,0},{1,9},{9,1},{2,10},{10,2},{3,11},{11,3},{4,12},{12,4},... | collective-permute-start | bytes 602120 | tf_op jit(solution)/shard_map/ppermute | solution.py:629
  10.3 4.2 %collective-permute-done.paired = bf16[784,128]{1,0:T(8,128)(2,1)S(1)} collective-permute-done((bf16[784,128]{1,0:T(8,128)(2,1)}, bf16[784,128]{1,0:T(8,128)(2,1)S(1)}, u32[]{:S(2)}, u32[]{:S(2)}) %collective-permute-start) | collective-permute-done | bytes 200736 | tf_op jit(solution)/shard_map/ppermute | solution.py:629
  15.8 2.2 %relay.2 = bf16[3072,128]{1,0:T(8,128)(2,1)} custom-call(s32[1,8]{1,0:T(1,128)} %place.9, s32[1]{0:T(128)} %bitcast.device, s32[2,8]{1,0:T(2,128)} %maximum_convert_fusion.lists, bf16[784,128]{1,0:T(8,128)(2,1)} %get-tuple-element.36.own, bf16[784,128]{1,0:T(8,128)(2,1)} %copy-done.3, bf16[784,128]{1,0:T(8,128)(2,1)} %copy-done.2), custom_call_target="tpu_custom_call" | custom-call | tf_op jit(solution)/shard_map/relay/pallas_call | solution.py:502
  18.1 4.2 %all-to-all-start = ((bf16[8,384,128]{2,1,0:T(8,128)(2,1)}), bf16[8,384,128]{2,1,0:T(8,128)(2,1)}, u32[]{:S(2)}, u32[]{:S(2)}) async-start(bf16[8,384,128]{2,1,0:T(8,128)(2,1)} %bitcast.36), calls=%async_computation | async-start | bytes 1572864 | tf_op jit(solution)/shard_map/all_to_all | solution.py:638
  22.3 1.4 %rev.3 = f32[7,7,128]{2,1,0:T(8,128)} reverse(f32[7,7,128]{2,1,0:T(8,128)} %param.17), dimensions={0,1} | reverse | bytes 50176 | tf_op jit(solution)/shard_map/rev | solution.py:680
  23.6 0.8 pad_slice_fusion.3
  25.1 2.3 %mask.1 = bf16[64,64,128]{2,1,0:T(8,128)(2,1)} custom-call(s32[64,64]{1,0:T(8,128)} %bitcast.43), custom_call_target="tpu_custom_call" | custom-call | flops 4000000000 | bytes 1000000 | tf_op jit(solution)/shard_map/mask/pallas_call | solution.py:490
  27.4 7.5 %all-to-all-done = bf16[8,384,128]{2,1,0:T(8,128)(2,1)} async-done(((bf16[8,384,128]{2,1,0:T(8,128)(2,1)}), bf16[8,384,128]{2,1,0:T(8,128)(2,1)}, u32[]{:S(2)}, u32[]{:S(2)}) %all-to-all-start) | async-done | bytes 786464 | tf_op jit(solution)/shard_map/all_to_all | solution.py:638
  34.9 22.5 %core.1 = (bf16[64,64,128]{2,1,0:T(8,128)(2,1)}, f32[5040,128]{1,0:T(8,128)}, bf16[768,128]{1,0:T(8,128)(2,1)}, f32[5040,128]{1,0:T(8,128)}, f32[128,512]{1,0:T(...) custom-call(s32[1,8]{1,0:T(1,128)} %place.9, s32[1]{0:T(128)} %bitcast.device, ...), custom_call_target="tpu_custom_call" | custom-call | flops 22000001024 | bytes 8000000 | tf_op jit(solution)/shard_map/core/pallas_call | solution.py:516
  57.4 1.3 %collective-permute-start.3 = (bf16[768,128]{1,0:T(8,128)(2,1)}, bf16[768,128]{1,0:T(8,128)(2,1)}, u32[]{:S(2)}, u32[]{:S(2)}) collective-permute-start(bf16[768,128]{1,0:T(8,128)(2,1)} %get-tuple-element.40.own), channel_id=1, source_target_pairs={{8,16},{16,8},{9,17},{17,9},{10,18},{18,10},{11,19},{19,11},{12,20... | collective-permute-start | bytes 589832 | tf_op jit(solution)/shard_map/ppermute | solution.py:629
  58.8 3.2 %collective-permute-start.2 = (bf16[768,128]{1,0:T(8,128)(2,1)}, bf16[768,128]{1,0:T(8,128)(2,1)}, u32[]{:S(2)}, u32[]{:S(2)}) collective-permute-start(bf16[768,128]{1,0:T(8,128)(2,1)} %get-tuple-element.40.own), channel_id=1, source_target_pairs={{0,8},{8,0},{1,9},{9,1},{2,10},{10,2},{3,11},{11,3},{4,12},{12,4},... | collective-permute-start | bytes 589832 | tf_op jit(solution)/shard_map/ppermute | solution.py:629
  62.0 0.8 pad_slice_fusion.1
  63.5 2.5 %collective-permute-done.2.paired = bf16[768,128]{1,0:T(8,128)(2,1)} collective-permute-done((bf16[768,128]{1,0:T(8,128)(2,1)}, bf16[768,128]{1,0:T(8,128)(2,1)}, u32[]{:S(2)}, u32[]{:S(2)}) %collective-permute-start.2) | collective-permute-done | bytes 196640 | tf_op jit(solution)/shard_map/ppermute | solution.py:629
  66.0 2.2 %relay.3 = bf16[3072,128]{1,0:T(8,128)(2,1)} custom-call(s32[1,8]{1,0:T(1,128)} %place.9, s32[1]{0:T(128)} %bitcast.device, s32[2,8]{1,0:T(2,128)} %maximum_convert_fusion.lists, bf16[768,128]{1,0:T(8,128)(2,1)} %get-tuple-element.40.own, bf16[768,128]{1,0:T(8,128)(2,1)} %collective-permute-done.2.paired, bf16[768,128]{1,0:T(8,128)(2,1)} %collective-permute-done.3.other), custom_call_target="tpu_custom_call" | custom-call | tf_op jit(solution)/shard_map/relay/pallas_call | solution.py:502
  68.2 4.4 %all-to-all-start.1 = ((bf16[8,384,128]{2,1,0:T(8,128)(2,1)}), bf16[8,384,128]{2,1,0:T(8,128)(2,1)}, u32[]{:S(2)}, u32[]{:S(2)}) async-start(bf16[8,384,128]{2,1,0:T(8,128)(2,1)} %bitcast.35), calls=%async_computation.1 | async-start | bytes 1572864 | tf_op jit(solution)/shard_map/all_to_all | solution.py:638
  72.6 15.5 %inner.1 = (bf16[1280,128]{1,0:T(8,128)(2,1)}, f32[64,64,128]{2,1,0:T(8,128)}) custom-call(f32[1]{0:T(128)} %constant.10.clone.1.scale, f32[5040,128]{1,0:T(8,128)} %get-tuple-element.38.padded, f32[5040,128]{1,0:T(8,128)} %get-tuple-element.41.d_conv, bf16[64,64,128]{2,1,0:T(8,128)(2,1)} %bitcast.45, bf16[64,64,128]{2,1,0:T(8,128)(2,1)} %mask.1, ...), custom_call_target="tpu_custom_call" | custom-call | flops 16000000000 | bytes 8000000 | tf_op jit(solution)/shard_map/inner/pallas_call | solution.py:553
  88.1 17.1 %all_to_all.20 = bf16[32,40,128]{2,1,0:T(8,128)(2,1)S(1)} all-to-all(bf16[32,40,128]{2,1,0:T(8,128)(2,1)} %bitcast.39), channel_id=1, replica_groups=mesh['tiles'=32] {'tiles'}, dimensions={0} | all-to-all | bytes 655360 | tf_op jit(solution)/shard_map/all_to_all | solution.py:644
  105.2 0.8 broadcast_in_dim.14
  106.0 2.6 %all-to-all-start.3 = ((bf16[32,40,128]{2,1,0:T(8,128)(2,1)}), bf16[32,40,128]{2,1,0:T(8,128)(2,1)S(1)}, u32[]{:S(2)}, u32[]{:S(2)}) async-start(bf16[32,40,128]{2,1,0:T(8,128)(2,1)} %broadcast_in_dim.14), calls=%async_computation.3 | async-start | bytes 655360 | tf_op jit(solution)/shard_map/all_to_all | solution.py:646
  110.0 1.0 copy-done.1
  111.0 3.9 %edge.1 = f32[64,64,128]{2,1,0:T(8,128)} custom-call(s32[1,8]{1,0:T(1,128)S(1)} %copy-done, s32[1]{0:T(128)} %bitcast.device, f32[64,64,128]{2,1,0:T(8,128)} %get-tuple-element.46.partial, bf16[3072,128]{1,0:T(8,128)(2,1)} %bitcast.18.arrived, f32[4,3,64,128]{3,2,1,0:T(8,128)S(1)} %copy-done.1, ...), custom_call_target="tpu_custom_call", output_to_operand_aliasing={{}: (2, {})} | custom-call | flops 4000000000 | bytes 1000000 | tf_op jit(solution)/shard_map/edge/pallas_call | solution.py:602
  114.9 5.7 %all-to-all-done.3 = bf16[32,40,128]{2,1,0:T(8,128)(2,1)S(1)} async-done(((bf16[32,40,128]{2,1,0:T(8,128)(2,1)}), bf16[32,40,128]{2,1,0:T(8,128)(2,1)S(1)}, u32[]{:S(2)}, u32[]{:S(2)}) %all-to-all-start.3) | async-done | bytes 327712 | tf_op jit(solution)/shard_map/all_to_all | solution.py:646
  120.6 0.8 unpack.1
  (20 shorter events, 5.4 us)
Async XLA Ops:
  3.1 6.6 %collective-permute-start.1 = (bf16[784,128]{1,0:T(8,128)(2,1)}, bf16[784,128]{1,0:T(8,128)(2,1)S(1)}, u32[]{:S(2)}, u32[]{:S(2)}) collective-permute-start(bf16[784,128]{1,0:T(8,128)(2,1)} %get-tuple-element.36.own), channel_id=1, source_target_pairs={{8,16},{16,8},{9,17},{17,9},{10,18},{18,10},{11,19},{19,11},{12,20... | collective-permute-start | bytes 602120 | tf_op jit(solution)/shard_map/ppermute | solution.py:629
  3.7 10.8 %collective-permute-start = (bf16[784,128]{1,0:T(8,128)(2,1)}, bf16[784,128]{1,0:T(8,128)(2,1)S(1)}, u32[]{:S(2)}, u32[]{:S(2)}) collective-permute-start(bf16[784,128]{1,0:T(8,128)(2,1)} %get-tuple-element.36.own), channel_id=1, source_target_pairs={{0,8},{8,0},{1,9},{9,1},{2,10},{10,2},{3,11},{11,3},{4,12},{12,4},... | collective-permute-start | bytes 602120 | tf_op jit(solution)/shard_map/ppermute | solution.py:629
  9.6 0.7 copy-start.2
  14.6 0.7 copy-start.3
  18.1 16.8 %all-to-all-start = ((bf16[8,384,128]{2,1,0:T(8,128)(2,1)}), bf16[8,384,128]{2,1,0:T(8,128)(2,1)}, u32[]{:S(2)}, u32[]{:S(2)}) async-start(bf16[8,384,128]{2,1,0:T(8,128)(2,1)} %bitcast.36), calls=%async_computation | async-start | bytes 1572864 | tf_op jit(solution)/shard_map/all_to_all | solution.py:638
  57.4 6.1 %collective-permute-start.3 = (bf16[768,128]{1,0:T(8,128)(2,1)}, bf16[768,128]{1,0:T(8,128)(2,1)}, u32[]{:S(2)}, u32[]{:S(2)}) collective-permute-start(bf16[768,128]{1,0:T(8,128)(2,1)} %get-tuple-element.40.own), channel_id=1, source_target_pairs={{8,16},{16,8},{9,17},{17,9},{10,18},{18,10},{11,19},{19,11},{12,20... | collective-permute-start | bytes 589832 | tf_op jit(solution)/shard_map/ppermute | solution.py:629
  58.8 7.2 %collective-permute-start.2 = (bf16[768,128]{1,0:T(8,128)(2,1)}, bf16[768,128]{1,0:T(8,128)(2,1)}, u32[]{:S(2)}, u32[]{:S(2)}) collective-permute-start(bf16[768,128]{1,0:T(8,128)(2,1)} %get-tuple-element.40.own), channel_id=1, source_target_pairs={{0,8},{8,0},{1,9},{9,1},{2,10},{10,2},{3,11},{11,3},{4,12},{12,4},... | collective-permute-start | bytes 589832 | tf_op jit(solution)/shard_map/ppermute | solution.py:629
  68.2 19.9 %all-to-all-start.1 = ((bf16[8,384,128]{2,1,0:T(8,128)(2,1)}), bf16[8,384,128]{2,1,0:T(8,128)(2,1)}, u32[]{:S(2)}, u32[]{:S(2)}) async-start(bf16[8,384,128]{2,1,0:T(8,128)(2,1)} %bitcast.35), calls=%async_computation.1 | async-start | bytes 1572864 | tf_op jit(solution)/shard_map/all_to_all | solution.py:638
  106.0 14.6 %all-to-all-start.3 = ((bf16[32,40,128]{2,1,0:T(8,128)(2,1)}), bf16[32,40,128]{2,1,0:T(8,128)(2,1)S(1)}, u32[]{:S(2)}, u32[]{:S(2)}) async-start(bf16[32,40,128]{2,1,0:T(8,128)(2,1)} %broadcast_in_dim.14), calls=%async_computation.3 | async-start | bytes 655360 | tf_op jit(solution)/shard_map/all_to_all | solution.py:646
  109.3 0.7 copy-start
  110.0 1.0 copy-start.1

commit v7 on v6

--- a/solution.py
+++ b/solution.py
@@ -96,18 +96,26 @@
     return total
 
 
-def picker(place, device, arrived):
+def picker(place, device, arrived, swapped):
     group = lax.div(device[0], GROUP)
+    mine = lax.rem(device[0], GROUP)
 
     def pick(side, r):
         tile = place[0, side]
         owner = jnp.maximum(tile, 0)
-        slot = 2 * lax.rem(owner, GROUP) + jnp.where(lax.div(owner, GROUP) != group, 1, 0)
+        source = lax.rem(owner, GROUP)
+        slot = 2 * (source ^ mine if swapped else source) + jnp.where(lax.div(owner, GROUP) != group, 1, 0)
         at = pl.multiple_of(slot * STRIP_ROWS + r * SIDE, SIDE)
-        value = arrived[pl.ds(at, SIDE), :].astype(F32)
-        return jnp.where(tile >= 0, value, 0.0)
+        return jnp.where(tile >= 0, arrived[pl.ds(at, SIDE), :].astype(F32), 0.0)
 
     return pick
+
+
+def arrivals(blocks, held):
+    pairs = []
+    for k in range(1, GROUP):
+        pairs.append((blocks[k - 1], held.at[pl.ds(2 * k * STRIP_ROWS, 2 * STRIP_ROWS)]))
+    return tuple(pairs)
 
 
 def start_all(pairs, sems):
@@ -152,25 +160,33 @@
     out[4 * STRIP_ROWS :, :] = listing.astype(BF16)
 
 
-def relay_body(place, device, lists, own, paired, other, out):
+def strip_for(read, tile):
+    strip = jnp.int32(0)
+    for side in range(8):
+        strip = jnp.where(read(side) == tile, STRIP_FOR[OPPOSITE[side]], strip)
+    return pl.ds(pl.multiple_of(strip * STRIP_ROWS, STRIP_ROWS), STRIP_ROWS)
+
+
+def relayed_strip(device, lists, paired, other, dest):
+    group = lax.div(device[0], GROUP)
+    use_pair = (dest < lax.rem(device[0], GROUP)) == (lax.rem(group, 2) == 1)
+    rows = strip_for(lambda side: jnp.where(use_pair, lists[0, side], lists[1, side]), group * GROUP + dest)
+    return jnp.where(use_pair, paired[rows, :], other[rows, :])
+
+
+def relay_body(place, device, lists, own, paired, other, *out):
     group = lax.div(device[0], GROUP)
     mine = lax.rem(device[0], GROUP)
-
-    def strip_for(read, tile):
-        strip = jnp.int32(0)
-        for side in range(8):
-            strip = jnp.where(read(side) == tile, STRIP_FOR[OPPOSITE[side]], strip)
-        return pl.multiple_of(strip * STRIP_ROWS, STRIP_ROWS)
-
-    for dest in range(GROUP):
-        tile = group * GROUP + dest
-        at = strip_for(lambda side: place[0, side], tile)
-        out[2 * dest * STRIP_ROWS : (2 * dest + 1) * STRIP_ROWS, :] = own[pl.ds(at, STRIP_ROWS), :]
-        use_pair = (dest < mine) == (lax.rem(group, 2) == 1)
-        at = strip_for(lambda side: jnp.where(use_pair, lists[0, side], lists[1, side]), tile)
-        out[(2 * dest + 1) * STRIP_ROWS : (2 * dest + 2) * STRIP_ROWS, :] = jnp.where(
-            use_pair, paired[pl.ds(at, STRIP_ROWS), :], other[pl.ds(at, STRIP_ROWS), :]
-        )
+    for k in range(GROUP):
+        if len(out) == 1:
+            block, at, dest = out[0], 2 * k * STRIP_ROWS, k
+        elif k:
+            block, at, dest = out[k - 1], 0, mine ^ k
+        else:
+            continue
+        rows = strip_for(lambda side: place[0, side], group * GROUP + dest)
+        block[at : at + STRIP_ROWS, :] = own[rows, :]
+        block[at + STRIP_ROWS : at + 2 * STRIP_ROWS, :] = relayed_strip(device, lists, paired, other, dest)
 
 
 def core_body(
@@ -185,9 +201,9 @@
     )
     mask, fields, arrived, cotangent = mask_in, fields_in, arrived_in, cotangent_in
     build_taps(tap_table, taps)
-    for load in loads[:3]:
+    for load in loads[:-1]:
         load.wait()
-    place_strips(picker(place, device, arrived), padded, stage)
+    place_strips(picker(place, device, arrived, False), padded, stage)
 
     def fill(i, carry):
         padded[pl.ds((i + RADIUS) * PITCH + RADIUS, SIDE), :] = fields[i].astype(F32) * mask[i].astype(F32)
@@ -196,7 +212,7 @@
     lax.fori_loop(0, SIDE, fill, 0)
     stores = start_all(((padded, padded_out),), out_sems)
     shift_copies(padded, shifted)
-    loads[3].wait()
+    loads[-1].wait()
     d_weight_in[...] = jnp.zeros_like(d_weight_in)
     d_weight_out[...] = jnp.zeros_like(d_weight_out)
     d_bias_in[...] = jnp.zeros_like(d_bias_in)
@@ -383,8 +399,10 @@
         small[i][...] = held[AT_SMALL + i : AT_SMALL + i + 1, :]
 
 
-def edge_body(place, device, partial, arrived, mask_strips, weights, d_fields,
-              frame, columns, beside, top, bottom, left, right, sems):
+def edge_body(place, device, partial, a1, a2, a3, a4, a5, a6, a7, mask_strips, weights, d_fields,
+              frame, columns, beside, top, bottom, left, right, sems, arrived, in_sems):
+    waits = start_all(arrivals((a1, a2, a3, a4, a5, a6, a7), arrived), in_sems)
+    arrived[0 : 2 * STRIP_ROWS, :] = jnp.zeros((2 * STRIP_ROWS, 128), BF16)
     inner = SIDE - 2 * RADIUS
     parts = (
         (top, (pl.ds(0, RADIUS),)),
@@ -398,9 +416,11 @@
     ]
     for load in loads:
         load.start()
-    pick = picker(place, device, arrived)
+    pick = picker(place, device, arrived, True)
     frame[...] = jnp.zeros_like(frame)
     columns[...] = jnp.zeros_like(columns)
+    for wait in waits:
+        wait.wait()
     for r in range(RADIUS):
         frame[0, r, RADIUS : RADIUS + SIDE, :] = pick(0, r)
         frame[1, r, RADIUS : RADIUS + SIDE, :] = pick(1, r)
@@ -498,13 +518,16 @@
     )(ocean_mask)
 
 
-def run_relay(place, device, lists, own, paired, other):
+def run_relay(place, device, lists, own, paired, other, swapped):
+    pair = 2 * STRIP_ROWS
+    shapes = [(pair, 128)] * (GROUP - 1) if swapped else [(GROUP * pair, 128)]
     return pl.pallas_call(
         relay_body,
-        out_shape=jax.ShapeDtypeStruct((2 * GROUP * STRIP_ROWS, 128), BF16),
+        out_shape=tuple(jax.ShapeDtypeStruct(shape, BF16) for shape in shapes),
         in_specs=[IN_SMEM] * 3 + [IN_VMEM] * 3,
-        out_specs=IN_VMEM,
+        out_specs=(IN_VMEM,) * len(shapes),
         compiler_params=params(64),
+        cost_estimate=pl.CostEstimate(flops=2_000_000_000, bytes_accessed=1_000_000, transcendentals=0),
         name="relay",
     )(place, device, lists, own, paired, other)
 
@@ -602,7 +625,7 @@
     return pl.pallas_call(
         edge_body,
         out_shape=jax.ShapeDtypeStruct((SIDE, SIDE, 128), F32),
-        in_specs=[IN_SMEM, IN_SMEM, ANYWHERE] + [IN_VMEM] * 3,
+        in_specs=[IN_SMEM, IN_SMEM, ANYWHERE] + [ANYWHERE] * 7 + [IN_VMEM] * 2,
         out_specs=ANYWHERE,
         scratch_shapes=[
             pltpu.VMEM((2, RADIUS, PITCH, 128), F32),
@@ -610,12 +633,14 @@
             pltpu.VMEM((2, RADIUS, SIDE, 128), F32),
             rim, rim, side, side,
             pltpu.SemaphoreType.DMA((4,)),
+            pltpu.VMEM((2 * GROUP * STRIP_ROWS, 128), BF16),
+            pltpu.SemaphoreType.DMA((GROUP - 1,)),
         ],
         input_output_aliases={2: 0},
         compiler_params=params(6),
         cost_estimate=pl.CostEstimate(flops=4_000_000_000, bytes_accessed=1_000_000, transcendentals=0),
         name="edge",
-    )(place, device, partial, arrived, mask_strips, weights)
+    )(place, device, partial, *arrived, mask_strips, weights)
 
 
 def swap_groups(value):
@@ -638,12 +663,21 @@
     return lax.all_to_all(blocks, "tiles", 0, 0, axis_index_groups=groups).reshape(-1, 128)
 
 
-def sum_over_tiles(packed):
+def swap_within_group(blocks):
+    peers = lax.axis_size("tiles")
+    return [
+        lax.ppermute(block, "tiles", [(i, i ^ k) for i in range(peers)])
+        for k, block in enumerate(blocks, start=1)
+    ]
+
+
+def sum_over_tiles(packed, tie):
     peers = lax.axis_size("tiles")
     blocks = packed.reshape(peers, -1, 128)
     summed = jnp.sum(lax.all_to_all(blocks, "tiles", 0, 0).astype(F32), axis=0)
+    summed, *tie = lax.optimization_barrier((summed, *tie))
     shared = jnp.broadcast_to(summed.astype(BF16)[None], blocks.shape)
-    return lax.all_to_all(shared, "tiles", 0, 0).reshape(packed.shape)
+    return lax.all_to_all(shared, "tiles", 0, 0).reshape(packed.shape), tie
 
 
 def per_device(
@@ -667,26 +701,26 @@
     paired, other = swap_groups(own)
     mask = run_mask(ocean_mask[0])
     lists = jnp.stack([paired[-16, :8], other[-16, :8]]).astype(jnp.int32)
-    arrived = within_group(run_relay(neighbours, device, lists, own, paired, other))
+    (blocks,) = run_relay(neighbours, device, lists, own, paired, other, False)
+    arrived = within_group(blocks)
     vectors = [v.reshape(1, -1) for v in (conv_bias, ln_gain, ln_bias, bias_in, bias_out, layer_scale)]
     updated, d_conv, strips, padded, *gradients = run_core(
         neighbours, device, fields[0], arrived, cotangent[0], mask, tap_rows(kernel), vectors,
         (weight_in, weight_out),
     )
     paired, other = swap_groups(strips)
-    blocks = run_relay(neighbours, device, lists, strips, paired, other)
-    d_conv, blocks = lax.optimization_barrier((d_conv, blocks))
-    arrived = within_group(blocks)
     flipped = kernel[::-1, ::-1]
     scale = jnp.full((1,), 1.0 / math.sqrt(peers * SIDE * SIDE), F32)
     rows = -(-PACKED_ROWS // (peers * 8)) * (peers * 8)
     packed, partial = run_inner(
         rows, scale, padded, d_conv, cotangent[0], mask, tap_rows(flipped), gradients
     )
-    packed, arrived = lax.optimization_barrier((packed, arrived))
+    packed, paired, other = lax.optimization_barrier((packed, paired, other))
+    arrived = swap_within_group(run_relay(neighbours, device, lists, strips, paired, other, True))
     weights = flipped.reshape(TAPS * TAPS, 128)
+    total, arrived = sum_over_tiles(packed, arrived)
     d_fields = run_edge(neighbours, device, partial, arrived, mask_strips, weights)
-    t_in, t_out, t_bias_in, t_kernel, *t_small = run_unpack(sum_over_tiles(packed))
+    t_in, t_out, t_bias_in, t_kernel, *t_small = run_unpack(total)
     return (
         updated[None],
         d_fields[None],

time: 122 us -> 115 us (0.943)
  blocking collectives: 17.1 us -> 0 us
  starting transfers between devices: 22.3 us -> 29.9 us
  other arithmetic: 0.65 us -> 2.44 us
    all_to_all x1 -> x0, blocking collectives: 17.1 us -> none  [sum_over_tiles(): summed = jnp.sum(lax.all_to_all(blocks, 'tiles', 0, 0).astype(F32), axis=0)]
    ppermute x0 -> x7, starting transfers between devices: none -> 7.67 us  [swap_within_group(): lax.ppermute(block, 'tiles', [(i, i ^ k) for i in range(peers)])]
    ppermute x0 -> x7, waiting for transfers between devices: none -> 5.75 us  [swap_within_group(): lax.ppermute(block, 'tiles', [(i, i ^ k) for i in range(peers)])]
    all_to_all x1 -> x2, starting transfers between devices: 2.59 us -> 8.16 us  [the longest x1 4.84 us: sum_over_tiles(): return (lax.all_to_all(shared, 'tiles', 0, 0).reshape(packed.shape), tie)]
    ppermute x4, waiting for transfers between devices: 6.73 us -> 1.72 us  [swap(): return lax.ppermute(value, 'tiles', pairs)]
    all_to_all x2 -> x1, starting transfers between devices: 8.59 us -> 4.22 us  [within_group(): lax.all_to_all(blocks, 'tiles', 0, 0, axis_index_groups=groups)]
    ppermute x4, starting transfers between devices: 11.2 us -> 9.81 us  [swap(): return lax.ppermute(value, 'tiles', pairs)]
    unnamed x8, local copies, waits for them, and re-layouts: 3.01 us -> 1.75 us
  transfers between devices with their start and end apart: 7 -> 14, of which waited for: 4 -> 7; matrix products, arithmetic and copies ran while one was open for 4% -> 7% of each run, Pallas kernels for 18% -> 21%
where the time goes in v7:
time: 115 us; the launch traced here: 114 us
  Pallas kernels  52.1 us (45%)
  starting transfers between devices  29.9 us (26%)
  waiting for transfers between devices  20.2 us (18%)
  local copies, waits for them, and re-layouts  8.21 us (7%)
  other arithmetic  2.44 us (2%)
    pallas_call x1, Pallas kernels, run_core(): pl.pallas_call(core_body, out_shape=(shape((SIDE, SIDE, 128), BF16), shap...  22.5 us
    pallas_call x1, Pallas kernels, run_inner(): pl.pallas_call(inner_body, out_shape=(jax.ShapeDtypeStruct((rows, 128), B...  15.4 us
    ppermute x4, starting transfers between devices, swap(): return lax.ppermute(value, 'tiles', pairs)  9.81 us
    ppermute x7, starting transfers between devices, swap_within_group(): lax.ppermute(block, 'tiles', [(i, i ^ k) for i in range(peers)])  7.67 us
    all_to_all x1, waiting for transfers between devices, within_group(): lax.all_to_all(blocks, 'tiles', 0, 0, axis_index_groups=groups)  7.41 us
    ppermute x7, waiting for transfers between devices, swap_within_group(): lax.ppermute(block, 'tiles', [(i, i ^ k) for i in range(peers)])  5.75 us
    all_to_all x1, waiting for transfers between devices, sum_over_tiles(): return (lax.all_to_all(shared, 'tiles', 0, 0).reshape(packed.shape), tie)  5.33 us
    all_to_all x1, starting transfers between devices, sum_over_tiles(): return (lax.all_to_all(shared, 'tiles', 0, 0).reshape(packed.shape), tie)  4.84 us
  transfers between devices with their start and end apart: 14, of which 7 were waited for; matrix products, arithmetic and copies ran while one was open for 7% of the time, Pallas kernels for 21%

profile of v7, /device:TPU:0, one launch (start us, length us, event | category | flops | bytes accessed | tf_op | source)
XLA Modules:
  0.0 113.6 jit_solution(10110555120135568350)
XLA Ops:
  0.6 2.4 %outgoing.1 = (bf16[784,128]{1,0:T(8,128)(2,1)}, f32[4,3,64,128]{3,2,1,0:T(8,128)}) custom-call(s32[1,8]{1,0:T(1,128)} %place.9, bf16[64,64,128]{2,1,0:T(8,128)(2,1)} %bitcast.33, s32[64,64]{1,0:T(8,128)} %bitcast.39), custom_call_target="tpu_custom_call" | custom-call | tf_op jit(solution)/shard_map/outgoing/pallas_call | solution.py:495
  3.1 3.0 %collective-permute-start = (bf16[784,128]{1,0:T(8,128)(2,1)}, bf16[784,128]{1,0:T(8,128)(2,1)S(1)}, u32[]{:S(2)}, u32[]{:S(2)}) collective-permute-start(bf16[784,128]{1,0:T(8,128)(2,1)} %get-tuple-element.50.own), channel_id=1, source_target_pairs={{0,8},{8,0},{1,9},{9,1},{2,10},{10,2},{3,11},{11,3},{4,12},{12,4},... | collective-permute-start | bytes 602120 | tf_op jit(solution)/shard_map/ppermute | solution.py:654
  6.8 1.4 %rev.3 = f32[7,7,128]{2,1,0:T(8,128)} reverse(f32[7,7,128]{2,1,0:T(8,128)} %param.17), dimensions={0,1} | reverse | bytes 50176 | tf_op jit(solution)/shard_map/rev | solution.py:712
  8.1 1.4 %pad_slice_fusion.3 = (f32[8,7,128]{2,1,0:T(8,128)}, f32[8,7,128]{2,1,0:T(8,128)}) fusion(f32[7,7,128]{2,1,0:T(8,128)} %param.17), kind=kLoop, calls=%fused_computation.8 | loop fusion | bytes 82432 | tf_op jit(solution)/shard_map/slice | solution.py:36
  9.6 1.7 %collective-permute-done.paired = bf16[784,128]{1,0:T(8,128)(2,1)S(1)} collective-permute-done((bf16[784,128]{1,0:T(8,128)(2,1)}, bf16[784,128]{1,0:T(8,128)(2,1)S(1)}, u32[]{:S(2)}, u32[]{:S(2)}) %collective-permute-start) | collective-permute-done | bytes 200736 | tf_op jit(solution)/shard_map/ppermute | solution.py:654
  12.0 2.2 %relay.2 = bf16[3072,128]{1,0:T(8,128)(2,1)} custom-call(s32[1,8]{1,0:T(1,128)} %place.9, s32[1]{0:T(128)} %bitcast.device, s32[2,8]{1,0:T(2,128)} %maximum_convert_fusion.lists, bf16[784,128]{1,0:T(8,128)(2,1)} %get-tuple-element.50.own, bf16[784,128]{1,0:T(8,128)(2,1)} %copy-done.2, bf16[784,128]{1,0:T(8,128)(2,1)} %copy-done.3), custom_call_target="tpu_custom_call" | custom-call | flops 2000000000 | bytes 1000000 | tf_op jit(solution)/shard_map/relay/pallas_call | solution.py:524
  14.3 4.2 %all-to-all-start = ((bf16[8,384,128]{2,1,0:T(8,128)(2,1)}), bf16[8,384,128]{2,1,0:T(8,128)(2,1)}, u32[]{:S(2)}, u32[]{:S(2)}) async-start(bf16[8,384,128]{2,1,0:T(8,128)(2,1)} %bitcast.35), calls=%async_computation | async-start | bytes 1572864 | tf_op jit(solution)/shard_map/all_to_all | solution.py:663
  21.4 2.3 %mask.1 = bf16[64,64,128]{2,1,0:T(8,128)(2,1)} custom-call(s32[64,64]{1,0:T(8,128)} %bitcast.40), custom_call_target="tpu_custom_call" | custom-call | flops 4000000000 | bytes 1000000 | tf_op jit(solution)/shard_map/mask/pallas_call | solution.py:510
  23.7 7.4 %all-to-all-done = bf16[8,384,128]{2,1,0:T(8,128)(2,1)} async-done(((bf16[8,384,128]{2,1,0:T(8,128)(2,1)}), bf16[8,384,128]{2,1,0:T(8,128)(2,1)}, u32[]{:S(2)}, u32[]{:S(2)}) %all-to-all-start) | async-done | bytes 786464 | tf_op jit(solution)/shard_map/all_to_all | solution.py:663
  31.1 22.5 %core.1 = (bf16[64,64,128]{2,1,0:T(8,128)(2,1)}, f32[5040,128]{1,0:T(8,128)}, bf16[768,128]{1,0:T(8,128)(2,1)}, f32[5040,128]{1,0:T(8,128)}, f32[128,512]{1,0:T(...) custom-call(s32[1,8]{1,0:T(1,128)} %place.9, s32[1]{0:T(128)} %bitcast.device, ...), custom_call_target="tpu_custom_call" | custom-call | flops 22000001024 | bytes 8000000 | tf_op jit(solution)/shard_map/core/pallas_call | solution.py:539
  53.6 4.8 %collective-permute-start.2 = (bf16[768,128]{1,0:T(8,128)(2,1)}, bf16[768,128]{1,0:T(8,128)(2,1)}, u32[]{:S(2)}, u32[]{:S(2)}) collective-permute-start(bf16[768,128]{1,0:T(8,128)(2,1)} %get-tuple-element.60.own), channel_id=1, source_target_pairs={{0,8},{8,0},{1,9},{9,1},{2,10},{10,2},{3,11},{11,3},{4,12},{12,4},... | collective-permute-start | bytes 589832 | tf_op jit(solution)/shard_map/ppermute | solution.py:654
  58.4 1.4 %collective-permute-start.3 = (bf16[768,128]{1,0:T(8,128)(2,1)}, bf16[768,128]{1,0:T(8,128)(2,1)}, u32[]{:S(2)}, u32[]{:S(2)}) collective-permute-start(bf16[768,128]{1,0:T(8,128)(2,1)} %get-tuple-element.60.own), channel_id=1, source_target_pairs={{8,16},{16,8},{9,17},{17,9},{10,18},{18,10},{11,19},{19,11},{12,20... | collective-permute-start | bytes 589832 | tf_op jit(solution)/shard_map/ppermute | solution.py:654
  59.7 15.4 %inner.1 = (bf16[1280,128]{1,0:T(8,128)(2,1)}, f32[64,64,128]{2,1,0:T(8,128)}) custom-call(f32[1]{0:T(128)} %constant.2.clone.1.scale, f32[5040,128]{1,0:T(8,128)} %get-tuple-element.52.padded, f32[5040,128]{1,0:T(8,128)} %get-tuple-element.53.d_conv, bf16[64,64,128]{2,1,0:T(8,128)(2,1)} %bitcast.42, bf16[64,64,128]{2,1,0:T(8,128)(2,1)} %mask.1, ...), custom_call_target="tpu_custom_call" | custom-call | flops 16000000000 | bytes 8000000 | tf_op jit(solution)/shard_map/inner/pallas_call | solution.py:576
  75.2 3.3 %all-to-all-start.1 = ((bf16[32,40,128]{2,1,0:T(8,128)(2,1)}), bf16[32,40,128]{2,1,0:T(8,128)(2,1)}, u32[]{:S(2)}, u32[]{:S(2)}) async-start(bf16[32,40,128]{2,1,0:T(8,128)(2,1)} %bitcast.36), calls=%async_computation.1 | async-start | bytes 655360 | tf_op jit(solution)/shard_map/all_to_all | solution.py:677
  78.5 2.1 %relay.3 = (bf16[384,128]{1,0:T(8,128)(2,1)}, bf16[384,128]{1,0:T(8,128)(2,1)}, bf16[384,128]{1,0:T(8,128)(2,1)}, bf16[384,128]{1,0:T(8,128)(2,1)}, bf16[384,128...) custom-call(s32[1,8]{1,0:T(1,128)} %place.9, s32[1]{0:T(128)} %bitcast.device, ...), custom_call_target="tpu_custom_call" | custom-call | flops 2000000000 | bytes 1000000 | tf_op jit(solution)/shard_map/relay/pallas_call | solution.py:524
  80.7 2.3 %collective-permute-start.10 = (bf16[384,128]{1,0:T(8,128)(2,1)}, bf16[384,128]{1,0:T(8,128)(2,1)S(1)}, u32[]{:S(2)}, u32[]{:S(2)}) collective-permute-start(bf16[384,128]{1,0:T(8,128)(2,1)} %get-tuple-element.70), channel_id=1, source_target_pairs={{0,7},{1,6},{2,5},{3,4},{4,3},{5,2},{6,1},{7,0},{8,15},{9,14},{10,... | collective-permute-start | bytes 294920 | tf_op jit(solution)/shard_map/ppermute | solution.py:669
  85.3 2.3 %collective-permute-done.10.a7 = bf16[384,128]{1,0:T(8,128)(2,1)S(1)} collective-permute-done((bf16[384,128]{1,0:T(8,128)(2,1)}, bf16[384,128]{1,0:T(8,128)(2,1)S(1)}, u32[]{:S(2)}, u32[]{:S(2)}) %collective-permute-start.10) | collective-permute-done | bytes 98336 | tf_op jit(solution)/shard_map/ppermute | solution.py:669
  87.6 1.6 %collective-permute-start.8 = (bf16[384,128]{1,0:T(8,128)(2,1)}, bf16[384,128]{1,0:T(8,128)(2,1)S(1)}, u32[]{:S(2)}, u32[]{:S(2)}) collective-permute-start(bf16[384,128]{1,0:T(8,128)(2,1)} %get-tuple-element.68), channel_id=1, source_target_pairs={{0,5},{1,4},{2,7},{3,6},{4,1},{5,0},{6,3},{7,2},{8,13},{9,12},{10,... | collective-permute-start | bytes 294920 | tf_op jit(solution)/shard_map/ppermute | solution.py:669
  89.3 1.4 %collective-permute-start.9 = (bf16[384,128]{1,0:T(8,128)(2,1)}, bf16[384,128]{1,0:T(8,128)(2,1)S(1)}, u32[]{:S(2)}, u32[]{:S(2)}) collective-permute-start(bf16[384,128]{1,0:T(8,128)(2,1)} %get-tuple-element.69), channel_id=1, source_target_pairs={{0,6},{1,7},{2,4},{3,5},{4,2},{5,3},{6,0},{7,1},{8,14},{9,15},{10,... | collective-permute-start | bytes 294920 | tf_op jit(solution)/shard_map/ppermute | solution.py:669
  90.6 1.0 convert_reduce_fusion
  92.3 1.9 %collective-permute-done.8.a5 = bf16[384,128]{1,0:T(8,128)(2,1)S(1)} collective-permute-done((bf16[384,128]{1,0:T(8,128)(2,1)}, bf16[384,128]{1,0:T(8,128)(2,1)S(1)}, u32[]{:S(2)}, u32[]{:S(2)}) %collective-permute-start.8) | collective-permute-done | bytes 98336 | tf_op jit(solution)/shard_map/ppermute | solution.py:669
  95.9 4.8 %all-to-all-start.2 = ((bf16[32,40,128]{2,1,0:T(8,128)(2,1)}), bf16[32,40,128]{2,1,0:T(8,128)(2,1)S(1)}, u32[]{:S(2)}, u32[]{:S(2)}) async-start(bf16[32,40,128]{2,1,0:T(8,128)(2,1)} %broadcast_in_dim.14), calls=%async_computation.2 | async-start | bytes 655360 | tf_op jit(solution)/shard_map/all_to_all | solution.py:680
  103.2 4.2 %edge.1 = f32[64,64,128]{2,1,0:T(8,128)} custom-call(s32[1,8]{1,0:T(1,128)S(1)} %copy-done, s32[1]{0:T(128)} %bitcast.device, f32[64,64,128]{2,1,0:T(8,128)} %get-tuple-element.58.partial, bf16[384,128]{1,0:T(8,128)(2,1)S(1)} %collective-permute-done.4.a1, bf16[384,128]{1,0:T(8,128)(2,1)S(1)} %collective-permute-done.5.a2, ...), custom_call_target="tpu_custom_call", output_to_operand_aliasing={{}: (2, {})} | custom-call | flops 4000000000 | bytes 1000000 | tf_op jit(solution)/shard_map/edge/pallas_call | solution.py:625
  107.4 5.3 %all-to-all-done.2 = bf16[32,40,128]{2,1,0:T(8,128)(2,1)S(1)} async-done(((bf16[32,40,128]{2,1,0:T(8,128)(2,1)}), bf16[32,40,128]{2,1,0:T(8,128)(2,1)S(1)}, u32[]{:S(2)}, u32[]{:S(2)}) %all-to-all-start.2) | async-done | bytes 327712 | tf_op jit(solution)/shard_map/all_to_all | solution.py:680
  (33 shorter events, 12.3 us)
Async XLA Ops:
  3.1 8.2 %collective-permute-start = (bf16[784,128]{1,0:T(8,128)(2,1)}, bf16[784,128]{1,0:T(8,128)(2,1)S(1)}, u32[]{:S(2)}, u32[]{:S(2)}) collective-permute-start(bf16[784,128]{1,0:T(8,128)(2,1)} %get-tuple-element.50.own), channel_id=1, source_target_pairs={{0,8},{8,0},{1,9},{9,1},{2,10},{10,2},{3,11},{11,3},{4,12},{12,4},... | collective-permute-start | bytes 602120 | tf_op jit(solution)/shard_map/ppermute | solution.py:654
  6.1 5.2 %collective-permute-start.1 = (bf16[784,128]{1,0:T(8,128)(2,1)}, bf16[784,128]{1,0:T(8,128)(2,1)S(1)}, u32[]{:S(2)}, u32[]{:S(2)}) collective-permute-start(bf16[784,128]{1,0:T(8,128)(2,1)} %get-tuple-element.50.own), channel_id=1, source_target_pairs={{8,16},{16,8},{9,17},{17,9},{10,18},{18,10},{11,19},{19,11},{12,20... | collective-permute-start | bytes 602120 | tf_op jit(solution)/shard_map/ppermute | solution.py:654
  11.3 0.7 copy-start.2
  11.3 0.7 copy-start.3
  14.3 16.8 %all-to-all-start = ((bf16[8,384,128]{2,1,0:T(8,128)(2,1)}), bf16[8,384,128]{2,1,0:T(8,128)(2,1)}, u32[]{:S(2)}, u32[]{:S(2)}) async-start(bf16[8,384,128]{2,1,0:T(8,128)(2,1)} %bitcast.35), calls=%async_computation | async-start | bytes 1572864 | tf_op jit(solution)/shard_map/all_to_all | solution.py:663
  53.6 21.6 %collective-permute-start.2 = (bf16[768,128]{1,0:T(8,128)(2,1)}, bf16[768,128]{1,0:T(8,128)(2,1)}, u32[]{:S(2)}, u32[]{:S(2)}) collective-permute-start(bf16[768,128]{1,0:T(8,128)(2,1)} %get-tuple-element.60.own), channel_id=1, source_target_pairs={{0,8},{8,0},{1,9},{9,1},{2,10},{10,2},{3,11},{11,3},{4,12},{12,4},... | collective-permute-start | bytes 589832 | tf_op jit(solution)/shard_map/ppermute | solution.py:654
  58.4 16.8 %collective-permute-start.3 = (bf16[768,128]{1,0:T(8,128)(2,1)}, bf16[768,128]{1,0:T(8,128)(2,1)}, u32[]{:S(2)}, u32[]{:S(2)}) collective-permute-start(bf16[768,128]{1,0:T(8,128)(2,1)} %get-tuple-element.60.own), channel_id=1, source_target_pairs={{8,16},{16,8},{9,17},{17,9},{10,18},{18,10},{11,19},{19,11},{12,20... | collective-permute-start | bytes 589832 | tf_op jit(solution)/shard_map/ppermute | solution.py:654
  75.2 15.4 %all-to-all-start.1 = ((bf16[32,40,128]{2,1,0:T(8,128)(2,1)}), bf16[32,40,128]{2,1,0:T(8,128)(2,1)}, u32[]{:S(2)}, u32[]{:S(2)}) async-start(bf16[32,40,128]{2,1,0:T(8,128)(2,1)} %bitcast.36), calls=%async_computation.1 | async-start | bytes 655360 | tf_op jit(solution)/shard_map/all_to_all | solution.py:677
  80.7 6.9 %collective-permute-start.10 = (bf16[384,128]{1,0:T(8,128)(2,1)}, bf16[384,128]{1,0:T(8,128)(2,1)S(1)}, u32[]{:S(2)}, u32[]{:S(2)}) collective-permute-start(bf16[384,128]{1,0:T(8,128)(2,1)} %get-tuple-element.70), channel_id=1, source_target_pairs={{0,7},{1,6},{2,5},{3,4},{4,3},{5,2},{6,1},{7,0},{8,15},{9,14},{10,... | collective-permute-start | bytes 294920 | tf_op jit(solution)/shard_map/ppermute | solution.py:669
  82.9 6.3 %collective-permute-start.4 = (bf16[384,128]{1,0:T(8,128)(2,1)}, bf16[384,128]{1,0:T(8,128)(2,1)S(1)}, u32[]{:S(2)}, u32[]{:S(2)}) collective-permute-start(bf16[384,128]{1,0:T(8,128)(2,1)} %get-tuple-element.64), channel_id=1, source_target_pairs={{0,1},{1,0},{2,3},{3,2},{4,5},{5,4},{6,7},{7,6},{8,9},{9,8},{10,11... | collective-permute-start | bytes 294920 | tf_op jit(solution)/shard_map/ppermute | solution.py:669
  83.3 8.4 %collective-permute-start.5 = (bf16[384,128]{1,0:T(8,128)(2,1)}, bf16[384,128]{1,0:T(8,128)(2,1)S(1)}, u32[]{:S(2)}, u32[]{:S(2)}) collective-permute-start(bf16[384,128]{1,0:T(8,128)(2,1)} %get-tuple-element.65), channel_id=1, source_target_pairs={{0,2},{1,3},{2,0},{3,1},{4,6},{5,7},{6,4},{7,5},{8,10},{9,11},{10,... | collective-permute-start | bytes 294920 | tf_op jit(solution)/shard_map/ppermute | solution.py:669
  83.9 8.4 %collective-permute-start.6 = (bf16[384,128]{1,0:T(8,128)(2,1)}, bf16[384,128]{1,0:T(8,128)(2,1)S(1)}, u32[]{:S(2)}, u32[]{:S(2)}) collective-permute-start(bf16[384,128]{1,0:T(8,128)(2,1)} %get-tuple-element.66), channel_id=1, source_target_pairs={{0,3},{1,2},{2,1},{3,0},{4,7},{5,6},{6,5},{7,4},{8,11},{9,10},{10,... | collective-permute-start | bytes 294920 | tf_op jit(solution)/shard_map/ppermute | solution.py:669
  84.8 7.5 %collective-permute-start.7 = (bf16[384,128]{1,0:T(8,128)(2,1)}, bf16[384,128]{1,0:T(8,128)(2,1)S(1)}, u32[]{:S(2)}, u32[]{:S(2)}) collective-permute-start(bf16[384,128]{1,0:T(8,128)(2,1)} %get-tuple-element.67), channel_id=1, source_target_pairs={{0,4},{1,5},{2,6},{3,7},{4,0},{5,1},{6,2},{7,3},{8,12},{9,13},{10,... | collective-permute-start | bytes 294920 | tf_op jit(solution)/shard_map/ppermute | solution.py:669
  87.6 6.6 %collective-permute-start.8 = (bf16[384,128]{1,0:T(8,128)(2,1)}, bf16[384,128]{1,0:T(8,128)(2,1)S(1)}, u32[]{:S(2)}, u32[]{:S(2)}) collective-permute-start(bf16[384,128]{1,0:T(8,128)(2,1)} %get-tuple-element.68), channel_id=1, source_target_pairs={{0,5},{1,4},{2,7},{3,6},{4,1},{5,0},{6,3},{7,2},{8,13},{9,12},{10,... | collective-permute-start | bytes 294920 | tf_op jit(solution)/shard_map/ppermute | solution.py:669
  89.3 5.9 %collective-permute-start.9 = (bf16[384,128]{1,0:T(8,128)(2,1)}, bf16[384,128]{1,0:T(8,128)(2,1)S(1)}, u32[]{:S(2)}, u32[]{:S(2)}) collective-permute-start(bf16[384,128]{1,0:T(8,128)(2,1)} %get-tuple-element.69), channel_id=1, source_target_pairs={{0,6},{1,7},{2,4},{3,5},{4,2},{5,3},{6,0},{7,1},{8,14},{9,15},{10,... | collective-permute-start | bytes 294920 | tf_op jit(solution)/shard_map/ppermute | solution.py:669
  95.9 16.8 %all-to-all-start.2 = ((bf16[32,40,128]{2,1,0:T(8,128)(2,1)}), bf16[32,40,128]{2,1,0:T(8,128)(2,1)S(1)}, u32[]{:S(2)}, u32[]{:S(2)}) async-start(bf16[32,40,128]{2,1,0:T(8,128)(2,1)} %broadcast_in_dim.14), calls=%async_computation.2 | async-start | bytes 655360 | tf_op jit(solution)/shard_map/all_to_all | solution.py:680
  101.5 0.7 copy-start
  102.2 1.0 copy-start.1

commit v8 on v7

--- a/solution.py
+++ b/solution.py
@@ -125,10 +125,13 @@
     return copies
 
 
-def mask_body(ocean_mask, mask):
+def mask_body(ocean_mask, fields, cotangent, mask, masked, signal):
     across = ocean_mask[...].astype(F32).T
     for i in range(SIDE):
-        mask[i] = jnp.broadcast_to(across[:, i : i + 1], (SIDE, 128)).astype(BF16)
+        live = jnp.broadcast_to(across[:, i : i + 1], (SIDE, 128))
+        mask[i] = live.astype(BF16)
+        masked[i] = (fields[i].astype(F32) * live).astype(BF16)
+        signal[i] = (cotangent[i].astype(F32) * live).astype(BF16)
 
 
 def outgoing_body(place, fields, ocean_mask, out, mask_strips, near, far):
@@ -197,22 +200,23 @@
     in_sems, out_sems, row_sems,
 ):
     loads = start_all(
-        ((mask, mask_in), (fields, fields_in), (arrived, arrived_in), (cotangent, cotangent_in)), in_sems
+        ((fields, fields_in), (arrived, arrived_in), (mask, mask_in), (cotangent, cotangent_in)), in_sems
     )
     mask, fields, arrived, cotangent = mask_in, fields_in, arrived_in, cotangent_in
     build_taps(tap_table, taps)
-    for load in loads[:-1]:
+    for load in loads[:2]:
         load.wait()
     place_strips(picker(place, device, arrived, False), padded, stage)
 
     def fill(i, carry):
-        padded[pl.ds((i + RADIUS) * PITCH + RADIUS, SIDE), :] = fields[i].astype(F32) * mask[i].astype(F32)
+        padded[pl.ds((i + RADIUS) * PITCH + RADIUS, SIDE), :] = fields[i].astype(F32)
         return carry
 
     lax.fori_loop(0, SIDE, fill, 0)
     stores = start_all(((padded, padded_out),), out_sems)
     shift_copies(padded, shifted)
-    loads[-1].wait()
+    for load in loads[2:]:
+        load.wait()
     d_weight_in[...] = jnp.zeros_like(d_weight_in)
     d_weight_out[...] = jnp.zeros_like(d_weight_out)
     d_bias_in[...] = jnp.zeros_like(d_bias_in)
@@ -239,7 +243,7 @@
         conv = jnp.concatenate([both[:, :128], both[:, 128:]], axis=0) + conv_bias[...]
         following = both if last else conv_block(shifted, taps, (index + 1) * count, count)
         live = by_half(mask, at)
-        signal = by_half(cotangent, at) * live
+        signal = by_half(cotangent, at)
         centred = conv - jnp.mean(conv, axis=-1, keepdims=True)
         inv_std = lax.rsqrt(jnp.mean(centred * centred, axis=-1, keepdims=True) + EPS)
         normed = centred * inv_std
@@ -268,7 +272,7 @@
             - jnp.mean(d_normed, axis=-1, keepdims=True)
             - normed * jnp.mean(d_normed * normed, axis=-1, keepdims=True)
         )
-        masked = by_half(fields, at) * live
+        masked = by_half(fields, at)
         updated[pl.ds(at, BLOCK)] = by_row(live * (masked + layer_scale[...] * branch)).astype(BF16)
         rows = by_row(d_out)
         for i in range(BLOCK):
@@ -359,7 +363,7 @@
                 sums[a * TAPS + b] += part[a]
         back = jnp.stack([both[:, :, :128], both[:, :, 128:]], axis=1).reshape(BLOCK, SIDE, 128)
         live = mask[pl.ds(at, BLOCK)].astype(F32)
-        d_fields[pl.ds(at, BLOCK)] = live * (live * cotangent[pl.ds(at, BLOCK)].astype(F32) + back)
+        d_fields[pl.ds(at, BLOCK)] = live * (cotangent[pl.ds(at, BLOCK)].astype(F32) + back)
         rows_out(index).start()
         return carry
 
@@ -506,16 +510,16 @@
     )(place, fields, ocean_mask)
 
 
-def run_mask(ocean_mask):
+def run_mask(ocean_mask, fields, cotangent):
     return pl.pallas_call(
         mask_body,
-        out_shape=jax.ShapeDtypeStruct((SIDE, SIDE, 128), BF16),
-        in_specs=[IN_VMEM],
-        out_specs=IN_VMEM,
+        out_shape=(jax.ShapeDtypeStruct((SIDE, SIDE, 128), BF16),) * 3,
+        in_specs=[IN_VMEM] * 3,
+        out_specs=(IN_VMEM,) * 3,
         compiler_params=params(64),
         cost_estimate=pl.CostEstimate(flops=4_000_000_000, bytes_accessed=1_000_000, transcendentals=0),
         name="mask",
-    )(ocean_mask)
+    )(ocean_mask, fields, cotangent)
 
 
 def run_relay(place, device, lists, own, paired, other, swapped):
@@ -699,13 +703,13 @@
     device = lax.axis_index("tiles").astype(jnp.int32).reshape(1)
     own, mask_strips = run_outgoing(neighbours, fields[0], ocean_mask[0])
     paired, other = swap_groups(own)
-    mask = run_mask(ocean_mask[0])
+    mask, masked, signal = run_mask(ocean_mask[0], fields[0], cotangent[0])
     lists = jnp.stack([paired[-16, :8], other[-16, :8]]).astype(jnp.int32)
     (blocks,) = run_relay(neighbours, device, lists, own, paired, other, False)
     arrived = within_group(blocks)
     vectors = [v.reshape(1, -1) for v in (conv_bias, ln_gain, ln_bias, bias_in, bias_out, layer_scale)]
     updated, d_conv, strips, padded, *gradients = run_core(
-        neighbours, device, fields[0], arrived, cotangent[0], mask, tap_rows(kernel), vectors,
+        neighbours, device, masked, arrived, signal, mask, tap_rows(kernel), vectors,
         (weight_in, weight_out),
     )
     paired, other = swap_groups(strips)
@@ -713,7 +717,7 @@
     scale = jnp.full((1,), 1.0 / math.sqrt(peers * SIDE * SIDE), F32)
     rows = -(-PACKED_ROWS // (peers * 8)) * (peers * 8)
     packed, partial = run_inner(
-        rows, scale, padded, d_conv, cotangent[0], mask, tap_rows(flipped), gradients
+        rows, scale, padded, d_conv, signal, mask, tap_rows(flipped), gradients
     )
     packed, paired, other = lax.optimization_barrier((packed, paired, other))
     arrived = swap_within_group(run_relay(neighbours, device, lists, strips, paired, other, True))

time: 115 us -> 114 us (level)
  waiting for transfers between devices: 20.2 us -> 18.5 us
  Pallas kernels: 52.1 us -> 53.4 us
    pallas_call x1, Pallas kernels: 2.28 us -> 4.03 us  [run_mask(): pl.pallas_call(mask_body, out_shape=(jax.ShapeDtypeStruct((SIDE, SIDE, 12...]
    all_to_all x1, waiting for transfers between devices: 7.41 us -> 5.67 us  [within_group(): lax.all_to_all(blocks, 'tiles', 0, 0, axis_index_groups=groups)]
  transfers between devices with their start and end apart: 14 -> 14, of which waited for: 7 -> 7; matrix products, arithmetic and copies ran while one was open for 7% -> 7% of each run, Pallas kernels for 21% -> 23%
where the time goes in v8:
time: 114 us; the launch traced here: 113 us
  Pallas kernels  53.4 us (47%)
  starting transfers between devices  29.8 us (26%)
  waiting for transfers between devices  18.5 us (16%)
  local copies, waits for them, and re-layouts  8.21 us (7%)
  other arithmetic  2.46 us (2%)
    pallas_call x1, Pallas kernels, run_core(): pl.pallas_call(core_body, out_shape=(shape((SIDE, SIDE, 128), BF16), shap...  22 us
    pallas_call x1, Pallas kernels, run_inner(): pl.pallas_call(inner_body, out_shape=(jax.ShapeDtypeStruct((rows, 128), B...  15.4 us
    ppermute x4, starting transfers between devices, swap(): return lax.ppermute(value, 'tiles', pairs)  9.79 us
    ppermute x7, starting transfers between devices, swap_within_group(): lax.ppermute(block, 'tiles', [(i, i ^ k) for i in range(peers)])  7.68 us
    ppermute x7, waiting for transfers between devices, swap_within_group(): lax.ppermute(block, 'tiles', [(i, i ^ k) for i in range(peers)])  5.75 us
    all_to_all x1, waiting for transfers between devices, within_group(): lax.all_to_all(blocks, 'tiles', 0, 0, axis_index_groups=groups)  5.67 us
    all_to_all x1, waiting for transfers between devices, sum_over_tiles(): return (lax.all_to_all(shared, 'tiles', 0, 0).reshape(packed.shape), tie)  5.34 us
    all_to_all x1, starting transfers between devices, sum_over_tiles(): return (lax.all_to_all(shared, 'tiles', 0, 0).reshape(packed.shape), tie)  4.84 us
  transfers between devices with their start and end apart: 14, of which 7 were waited for; matrix products, arithmetic and copies ran while one was open for 7% of the time, Pallas kernels for 23%

profile of v8, /device:TPU:0, one launch (start us, length us, event | category | flops | bytes accessed | tf_op | source)
XLA Modules:
  0.0 113.1 jit_solution(2823039638032111724)
XLA Ops:
  0.6 2.4 %outgoing.1 = (bf16[784,128]{1,0:T(8,128)(2,1)}, f32[4,3,64,128]{3,2,1,0:T(8,128)}) custom-call(s32[1,8]{1,0:T(1,128)} %place.9, bf16[64,64,128]{2,1,0:T(8,128)(2,1)} %bitcast.33, s32[64,64]{1,0:T(8,128)} %bitcast.39), custom_call_target="tpu_custom_call" | custom-call | tf_op jit(solution)/shard_map/outgoing/pallas_call | solution.py:499
  3.1 3.0 %collective-permute-start = (bf16[784,128]{1,0:T(8,128)(2,1)}, bf16[784,128]{1,0:T(8,128)(2,1)S(1)}, u32[]{:S(2)}, u32[]{:S(2)}) collective-permute-start(bf16[784,128]{1,0:T(8,128)(2,1)} %get-tuple-element.54.own), channel_id=1, source_target_pairs={{0,8},{8,0},{1,9},{9,1},{2,10},{10,2},{3,11},{11,3},{4,12},{12,4},... | collective-permute-start | bytes 602120 | tf_op jit(solution)/shard_map/ppermute | solution.py:658
  6.8 1.4 %rev.3 = f32[7,7,128]{2,1,0:T(8,128)} reverse(f32[7,7,128]{2,1,0:T(8,128)} %param.17), dimensions={0,1} | reverse | bytes 50176 | tf_op jit(solution)/shard_map/rev | solution.py:716
  8.1 1.5 %pad_slice_fusion.3 = (f32[8,7,128]{2,1,0:T(8,128)}, f32[8,7,128]{2,1,0:T(8,128)}) fusion(f32[7,7,128]{2,1,0:T(8,128)} %param.17), kind=kLoop, calls=%fused_computation.8 | loop fusion | bytes 82432 | tf_op jit(solution)/shard_map/slice | solution.py:36
  9.6 1.7 %collective-permute-done.paired = bf16[784,128]{1,0:T(8,128)(2,1)S(1)} collective-permute-done((bf16[784,128]{1,0:T(8,128)(2,1)}, bf16[784,128]{1,0:T(8,128)(2,1)S(1)}, u32[]{:S(2)}, u32[]{:S(2)}) %collective-permute-start) | collective-permute-done | bytes 200736 | tf_op jit(solution)/shard_map/ppermute | solution.py:658
  12.0 2.2 %relay.2 = bf16[3072,128]{1,0:T(8,128)(2,1)} custom-call(s32[1,8]{1,0:T(1,128)} %place.9, s32[1]{0:T(128)} %bitcast.device, s32[2,8]{1,0:T(2,128)} %maximum_convert_fusion.lists, bf16[784,128]{1,0:T(8,128)(2,1)} %get-tuple-element.54.own, bf16[784,128]{1,0:T(8,128)(2,1)} %copy-done.2, bf16[784,128]{1,0:T(8,128)(2,1)} %copy-done.3), custom_call_target="tpu_custom_call" | custom-call | flops 2000000000 | bytes 1000000 | tf_op jit(solution)/shard_map/relay/pallas_call | solution.py:528
  14.3 4.2 %all-to-all-start = ((bf16[8,384,128]{2,1,0:T(8,128)(2,1)}), bf16[8,384,128]{2,1,0:T(8,128)(2,1)}, u32[]{:S(2)}, u32[]{:S(2)}) async-start(bf16[8,384,128]{2,1,0:T(8,128)(2,1)} %bitcast.35), calls=%async_computation | async-start | bytes 1572864 | tf_op jit(solution)/shard_map/all_to_all | solution.py:667
  21.4 4.0 %mask.1 = (bf16[64,64,128]{2,1,0:T(8,128)(2,1)}, bf16[64,64,128]{2,1,0:T(8,128)(2,1)}, bf16[64,64,128]{2,1,0:T(8,128)(2,1)}) custom-call(s32[64,64]{1,0:T(8,128)} %bitcast.40, bf16[64,64,128]{2,1,0:T(8,128)(2,1)} %bitcast.34, bf16[64,64,128]{2,1,0:T(8,128)(2,1)} %bitcast.41), custom_call_target="tpu_custom_call" | custom-call | flops 4000000000 | bytes 1000000 | tf_op jit(solution)/shard_map/mask/pallas_call | solution.py:514
  25.4 5.7 %all-to-all-done = bf16[8,384,128]{2,1,0:T(8,128)(2,1)} async-done(((bf16[8,384,128]{2,1,0:T(8,128)(2,1)}), bf16[8,384,128]{2,1,0:T(8,128)(2,1)}, u32[]{:S(2)}, u32[]{:S(2)}) %all-to-all-start) | async-done | bytes 786464 | tf_op jit(solution)/shard_map/all_to_all | solution.py:667
  31.1 22.0 %core.1 = (bf16[64,64,128]{2,1,0:T(8,128)(2,1)}, f32[5040,128]{1,0:T(8,128)}, bf16[768,128]{1,0:T(8,128)(2,1)}, f32[5040,128]{1,0:T(8,128)}, f32[128,512]{1,0:T(...) custom-call(s32[1,8]{1,0:T(1,128)} %place.9, s32[1]{0:T(128)} %bitcast.device, ...), custom_call_target="tpu_custom_call" | custom-call | flops 22000001024 | bytes 8000000 | tf_op jit(solution)/shard_map/core/pallas_call | solution.py:543
  53.2 4.8 %collective-permute-start.2 = (bf16[768,128]{1,0:T(8,128)(2,1)}, bf16[768,128]{1,0:T(8,128)(2,1)}, u32[]{:S(2)}, u32[]{:S(2)}) collective-permute-start(bf16[768,128]{1,0:T(8,128)(2,1)} %get-tuple-element.66.own), channel_id=1, source_target_pairs={{0,8},{8,0},{1,9},{9,1},{2,10},{10,2},{3,11},{11,3},{4,12},{12,4},... | collective-permute-start | bytes 589832 | tf_op jit(solution)/shard_map/ppermute | solution.py:658
  57.9 1.3 %collective-permute-start.3 = (bf16[768,128]{1,0:T(8,128)(2,1)}, bf16[768,128]{1,0:T(8,128)(2,1)}, u32[]{:S(2)}, u32[]{:S(2)}) collective-permute-start(bf16[768,128]{1,0:T(8,128)(2,1)} %get-tuple-element.66.own), channel_id=1, source_target_pairs={{8,16},{16,8},{9,17},{17,9},{10,18},{18,10},{11,19},{19,11},{12,20... | collective-permute-start | bytes 589832 | tf_op jit(solution)/shard_map/ppermute | solution.py:658
  59.3 15.4 %inner.1 = (bf16[1280,128]{1,0:T(8,128)(2,1)}, f32[64,64,128]{2,1,0:T(8,128)}) custom-call(f32[1]{0:T(128)} %constant.2.clone.1.scale, f32[5040,128]{1,0:T(8,128)} %get-tuple-element.58.padded, f32[5040,128]{1,0:T(8,128)} %get-tuple-element.59.d_conv, bf16[64,64,128]{2,1,0:T(8,128)(2,1)} %get-tuple-element.55.cotangent, ...), custom_call_target="tpu_custom_call" | custom-call | flops 16000000000 | bytes 8000000 | tf_op jit(solution)/shard_map/inner/pallas_call | solution.py:580
  74.7 3.3 %all-to-all-start.1 = ((bf16[32,40,128]{2,1,0:T(8,128)(2,1)}), bf16[32,40,128]{2,1,0:T(8,128)(2,1)}, u32[]{:S(2)}, u32[]{:S(2)}) async-start(bf16[32,40,128]{2,1,0:T(8,128)(2,1)} %bitcast.36), calls=%async_computation.1 | async-start | bytes 655360 | tf_op jit(solution)/shard_map/all_to_all | solution.py:681
  78.0 2.1 %relay.3 = (bf16[384,128]{1,0:T(8,128)(2,1)}, bf16[384,128]{1,0:T(8,128)(2,1)}, bf16[384,128]{1,0:T(8,128)(2,1)}, bf16[384,128]{1,0:T(8,128)(2,1)}, bf16[384,128...) custom-call(s32[1,8]{1,0:T(1,128)} %place.9, s32[1]{0:T(128)} %bitcast.device, ...), custom_call_target="tpu_custom_call" | custom-call | flops 2000000000 | bytes 1000000 | tf_op jit(solution)/shard_map/relay/pallas_call | solution.py:528
  80.2 2.3 %collective-permute-start.10 = (bf16[384,128]{1,0:T(8,128)(2,1)}, bf16[384,128]{1,0:T(8,128)(2,1)S(1)}, u32[]{:S(2)}, u32[]{:S(2)}) collective-permute-start(bf16[384,128]{1,0:T(8,128)(2,1)} %get-tuple-element.76), channel_id=1, source_target_pairs={{0,7},{1,6},{2,5},{3,4},{4,3},{5,2},{6,1},{7,0},{8,15},{9,14},{10,... | collective-permute-start | bytes 294920 | tf_op jit(solution)/shard_map/ppermute | solution.py:673
  84.8 2.3 %collective-permute-done.10.a7 = bf16[384,128]{1,0:T(8,128)(2,1)S(1)} collective-permute-done((bf16[384,128]{1,0:T(8,128)(2,1)}, bf16[384,128]{1,0:T(8,128)(2,1)S(1)}, u32[]{:S(2)}, u32[]{:S(2)}) %collective-permute-start.10) | collective-permute-done | bytes 98336 | tf_op jit(solution)/shard_map/ppermute | solution.py:673
  87.1 1.6 %collective-permute-start.8 = (bf16[384,128]{1,0:T(8,128)(2,1)}, bf16[384,128]{1,0:T(8,128)(2,1)S(1)}, u32[]{:S(2)}, u32[]{:S(2)}) collective-permute-start(bf16[384,128]{1,0:T(8,128)(2,1)} %get-tuple-element.74), channel_id=1, source_target_pairs={{0,5},{1,4},{2,7},{3,6},{4,1},{5,0},{6,3},{7,2},{8,13},{9,12},{10,... | collective-permute-start | bytes 294920 | tf_op jit(solution)/shard_map/ppermute | solution.py:673
  88.8 1.4 %collective-permute-start.9 = (bf16[384,128]{1,0:T(8,128)(2,1)}, bf16[384,128]{1,0:T(8,128)(2,1)S(1)}, u32[]{:S(2)}, u32[]{:S(2)}) collective-permute-start(bf16[384,128]{1,0:T(8,128)(2,1)} %get-tuple-element.75), channel_id=1, source_target_pairs={{0,6},{1,7},{2,4},{3,5},{4,2},{5,3},{6,0},{7,1},{8,14},{9,15},{10,... | collective-permute-start | bytes 294920 | tf_op jit(solution)/shard_map/ppermute | solution.py:673
  90.1 1.0 convert_reduce_fusion
  91.8 1.9 %collective-permute-done.8.a5 = bf16[384,128]{1,0:T(8,128)(2,1)S(1)} collective-permute-done((bf16[384,128]{1,0:T(8,128)(2,1)}, bf16[384,128]{1,0:T(8,128)(2,1)S(1)}, u32[]{:S(2)}, u32[]{:S(2)}) %collective-permute-start.8) | collective-permute-done | bytes 98336 | tf_op jit(solution)/shard_map/ppermute | solution.py:673
  95.4 4.8 %all-to-all-start.2 = ((bf16[32,40,128]{2,1,0:T(8,128)(2,1)}), bf16[32,40,128]{2,1,0:T(8,128)(2,1)S(1)}, u32[]{:S(2)}, u32[]{:S(2)}) async-start(bf16[32,40,128]{2,1,0:T(8,128)(2,1)} %broadcast_in_dim.14), calls=%async_computation.2 | async-start | bytes 655360 | tf_op jit(solution)/shard_map/all_to_all | solution.py:684
  102.7 4.2 %edge.1 = f32[64,64,128]{2,1,0:T(8,128)} custom-call(s32[1,8]{1,0:T(1,128)S(1)} %copy-done, s32[1]{0:T(128)} %bitcast.device, f32[64,64,128]{2,1,0:T(8,128)} %get-tuple-element.64.partial, bf16[384,128]{1,0:T(8,128)(2,1)S(1)} %collective-permute-done.4.a1, bf16[384,128]{1,0:T(8,128)(2,1)S(1)} %collective-permute-done.5.a2, ...), custom_call_target="tpu_custom_call", output_to_operand_aliasing={{}: (2, {})} | custom-call | flops 4000000000 | bytes 1000000 | tf_op jit(solution)/shard_map/edge/pallas_call | solution.py:629
  106.9 5.3 %all-to-all-done.2 = bf16[32,40,128]{2,1,0:T(8,128)(2,1)S(1)} async-done(((bf16[32,40,128]{2,1,0:T(8,128)(2,1)}), bf16[32,40,128]{2,1,0:T(8,128)(2,1)S(1)}, u32[]{:S(2)}, u32[]{:S(2)}) %all-to-all-start.2) | async-done | bytes 327712 | tf_op jit(solution)/shard_map/all_to_all | solution.py:684
  (33 shorter events, 12.3 us)
Async XLA Ops:
  3.1 8.2 %collective-permute-start = (bf16[784,128]{1,0:T(8,128)(2,1)}, bf16[784,128]{1,0:T(8,128)(2,1)S(1)}, u32[]{:S(2)}, u32[]{:S(2)}) collective-permute-start(bf16[784,128]{1,0:T(8,128)(2,1)} %get-tuple-element.54.own), channel_id=1, source_target_pairs={{0,8},{8,0},{1,9},{9,1},{2,10},{10,2},{3,11},{11,3},{4,12},{12,4},... | collective-permute-start | bytes 602120 | tf_op jit(solution)/shard_map/ppermute | solution.py:658
  6.1 5.2 %collective-permute-start.1 = (bf16[784,128]{1,0:T(8,128)(2,1)}, bf16[784,128]{1,0:T(8,128)(2,1)S(1)}, u32[]{:S(2)}, u32[]{:S(2)}) collective-permute-start(bf16[784,128]{1,0:T(8,128)(2,1)} %get-tuple-element.54.own), channel_id=1, source_target_pairs={{8,16},{16,8},{9,17},{17,9},{10,18},{18,10},{11,19},{19,11},{12,20... | collective-permute-start | bytes 602120 | tf_op jit(solution)/shard_map/ppermute | solution.py:658
  11.3 0.7 copy-start.2
  11.3 0.7 copy-start.3
  14.3 16.8 %all-to-all-start = ((bf16[8,384,128]{2,1,0:T(8,128)(2,1)}), bf16[8,384,128]{2,1,0:T(8,128)(2,1)}, u32[]{:S(2)}, u32[]{:S(2)}) async-start(bf16[8,384,128]{2,1,0:T(8,128)(2,1)} %bitcast.35), calls=%async_computation | async-start | bytes 1572864 | tf_op jit(solution)/shard_map/all_to_all | solution.py:667
  53.2 21.5 %collective-permute-start.2 = (bf16[768,128]{1,0:T(8,128)(2,1)}, bf16[768,128]{1,0:T(8,128)(2,1)}, u32[]{:S(2)}, u32[]{:S(2)}) collective-permute-start(bf16[768,128]{1,0:T(8,128)(2,1)} %get-tuple-element.66.own), channel_id=1, source_target_pairs={{0,8},{8,0},{1,9},{9,1},{2,10},{10,2},{3,11},{11,3},{4,12},{12,4},... | collective-permute-start | bytes 589832 | tf_op jit(solution)/shard_map/ppermute | solution.py:658
  57.9 16.8 %collective-permute-start.3 = (bf16[768,128]{1,0:T(8,128)(2,1)}, bf16[768,128]{1,0:T(8,128)(2,1)}, u32[]{:S(2)}, u32[]{:S(2)}) collective-permute-start(bf16[768,128]{1,0:T(8,128)(2,1)} %get-tuple-element.66.own), channel_id=1, source_target_pairs={{8,16},{16,8},{9,17},{17,9},{10,18},{18,10},{11,19},{19,11},{12,20... | collective-permute-start | bytes 589832 | tf_op jit(solution)/shard_map/ppermute | solution.py:658
  74.7 15.4 %all-to-all-start.1 = ((bf16[32,40,128]{2,1,0:T(8,128)(2,1)}), bf16[32,40,128]{2,1,0:T(8,128)(2,1)}, u32[]{:S(2)}, u32[]{:S(2)}) async-start(bf16[32,40,128]{2,1,0:T(8,128)(2,1)} %bitcast.36), calls=%async_computation.1 | async-start | bytes 655360 | tf_op jit(solution)/shard_map/all_to_all | solution.py:681
  80.2 6.9 %collective-permute-start.10 = (bf16[384,128]{1,0:T(8,128)(2,1)}, bf16[384,128]{1,0:T(8,128)(2,1)S(1)}, u32[]{:S(2)}, u32[]{:S(2)}) collective-permute-start(bf16[384,128]{1,0:T(8,128)(2,1)} %get-tuple-element.76), channel_id=1, source_target_pairs={{0,7},{1,6},{2,5},{3,4},{4,3},{5,2},{6,1},{7,0},{8,15},{9,14},{10,... | collective-permute-start | bytes 294920 | tf_op jit(solution)/shard_map/ppermute | solution.py:673
  82.4 6.3 %collective-permute-start.4 = (bf16[384,128]{1,0:T(8,128)(2,1)}, bf16[384,128]{1,0:T(8,128)(2,1)S(1)}, u32[]{:S(2)}, u32[]{:S(2)}) collective-permute-start(bf16[384,128]{1,0:T(8,128)(2,1)} %get-tuple-element.70), channel_id=1, source_target_pairs={{0,1},{1,0},{2,3},{3,2},{4,5},{5,4},{6,7},{7,6},{8,9},{9,8},{10,11... | collective-permute-start | bytes 294920 | tf_op jit(solution)/shard_map/ppermute | solution.py:673
  82.8 8.4 %collective-permute-start.5 = (bf16[384,128]{1,0:T(8,128)(2,1)}, bf16[384,128]{1,0:T(8,128)(2,1)S(1)}, u32[]{:S(2)}, u32[]{:S(2)}) collective-permute-start(bf16[384,128]{1,0:T(8,128)(2,1)} %get-tuple-element.71), channel_id=1, source_target_pairs={{0,2},{1,3},{2,0},{3,1},{4,6},{5,7},{6,4},{7,5},{8,10},{9,11},{10,... | collective-permute-start | bytes 294920 | tf_op jit(solution)/shard_map/ppermute | solution.py:673
  83.4 8.4 %collective-permute-start.6 = (bf16[384,128]{1,0:T(8,128)(2,1)}, bf16[384,128]{1,0:T(8,128)(2,1)S(1)}, u32[]{:S(2)}, u32[]{:S(2)}) collective-permute-start(bf16[384,128]{1,0:T(8,128)(2,1)} %get-tuple-element.72), channel_id=1, source_target_pairs={{0,3},{1,2},{2,1},{3,0},{4,7},{5,6},{6,5},{7,4},{8,11},{9,10},{10,... | collective-permute-start | bytes 294920 | tf_op jit(solution)/shard_map/ppermute | solution.py:673
  84.3 7.5 %collective-permute-start.7 = (bf16[384,128]{1,0:T(8,128)(2,1)}, bf16[384,128]{1,0:T(8,128)(2,1)S(1)}, u32[]{:S(2)}, u32[]{:S(2)}) collective-permute-start(bf16[384,128]{1,0:T(8,128)(2,1)} %get-tuple-element.73), channel_id=1, source_target_pairs={{0,4},{1,5},{2,6},{3,7},{4,0},{5,1},{6,2},{7,3},{8,12},{9,13},{10,... | collective-permute-start | bytes 294920 | tf_op jit(solution)/shard_map/ppermute | solution.py:673
  87.1 6.6 %collective-permute-start.8 = (bf16[384,128]{1,0:T(8,128)(2,1)}, bf16[384,128]{1,0:T(8,128)(2,1)S(1)}, u32[]{:S(2)}, u32[]{:S(2)}) collective-permute-start(bf16[384,128]{1,0:T(8,128)(2,1)} %get-tuple-element.74), channel_id=1, source_target_pairs={{0,5},{1,4},{2,7},{3,6},{4,1},{5,0},{6,3},{7,2},{8,13},{9,12},{10,... | collective-permute-start | bytes 294920 | tf_op jit(solution)/shard_map/ppermute | solution.py:673
  88.8 5.9 %collective-permute-start.9 = (bf16[384,128]{1,0:T(8,128)(2,1)}, bf16[384,128]{1,0:T(8,128)(2,1)S(1)}, u32[]{:S(2)}, u32[]{:S(2)}) collective-permute-start(bf16[384,128]{1,0:T(8,128)(2,1)} %get-tuple-element.75), channel_id=1, source_target_pairs={{0,6},{1,7},{2,4},{3,5},{4,2},{5,3},{6,0},{7,1},{8,14},{9,15},{10,... | collective-permute-start | bytes 294920 | tf_op jit(solution)/shard_map/ppermute | solution.py:673
  95.4 16.8 %all-to-all-start.2 = ((bf16[32,40,128]{2,1,0:T(8,128)(2,1)}), bf16[32,40,128]{2,1,0:T(8,128)(2,1)S(1)}, u32[]{:S(2)}, u32[]{:S(2)}) async-start(bf16[32,40,128]{2,1,0:T(8,128)(2,1)} %broadcast_in_dim.14), calls=%async_computation.2 | async-start | bytes 655360 | tf_op jit(solution)/shard_map/all_to_all | solution.py:684
  101.0 0.7 copy-start
  101.7 1.0 copy-start.1

commit v9 on v8

--- a/solution.py
+++ b/solution.py
@@ -34,7 +34,7 @@
 def tap_rows(kernel):
     wide = jnp.pad(kernel, ((1, 1), (0, 0), (0, 0)))
     both = jnp.concatenate([wide[1:9], wide[0:8]], axis=2)
-    return both.transpose(1, 0, 2).reshape(TAPS * 8, 256)
+    return jnp.pad(both.transpose(1, 0, 2).reshape(TAPS * 8, 256), ((0, 8), (0, 0)))
 
 
 def build_taps(rows, taps):
@@ -213,7 +213,7 @@
         return carry
 
     lax.fori_loop(0, SIDE, fill, 0)
-    stores = start_all(((padded, padded_out),), out_sems)
+    stores = start_all(((padded.at[pl.ds(0, ROWS * PITCH)], padded_out),), out_sems)
     shift_copies(padded, shifted)
     for load in loads[2:]:
         load.wait()
@@ -383,7 +383,7 @@
         at = AT_SMALL + i
         held[at : at + 1, :] = jnp.sum(small[8 * i : 8 * i + 8, :], axis=0, keepdims=True) * scale[0]
     held[AT_SMALL + 5 :, :] = jnp.zeros((held.shape[0] - AT_SMALL - 5, 128), F32)
-    packed[...] = held[...].astype(packed.dtype)
+    packed[...] = held[0 : packed.shape[0], :].astype(packed.dtype)
     for index in range(SIDE // BLOCK):
         rows_out(index).wait()
 
@@ -409,10 +409,10 @@
     arrived[0 : 2 * STRIP_ROWS, :] = jnp.zeros((2 * STRIP_ROWS, 128), BF16)
     inner = SIDE - 2 * RADIUS
     parts = (
-        (top, (pl.ds(0, RADIUS),)),
-        (bottom, (pl.ds(SIDE - RADIUS, RADIUS),)),
-        (left, (pl.ds(RADIUS, inner), pl.ds(0, 8))),
-        (right, (pl.ds(RADIUS, inner), pl.ds(SIDE - 8, 8))),
+        (top.at[pl.ds(0, RADIUS)], (pl.ds(0, RADIUS),)),
+        (bottom.at[pl.ds(0, RADIUS)], (pl.ds(SIDE - RADIUS, RADIUS),)),
+        (left.at[pl.ds(0, inner)], (pl.ds(RADIUS, inner), pl.ds(0, 8))),
+        (right.at[pl.ds(0, inner)], (pl.ds(RADIUS, inner), pl.ds(SIDE - 8, 8))),
     )
     loads = [
         pltpu.make_async_copy(partial.at[where], held, sems.at[i])
@@ -466,7 +466,7 @@
 
     lax.fori_loop(0, SIDE // 8, along, 0)
     for far, held in ((0, left), (1, right)):
-        flat = held.reshape(inner * 8, 128)
+        flat = held.reshape(SIDE * 8, 128)
         for line in range(RADIUS):
             column = 5 + line if far else line
             flat[pl.ds(column, inner, stride=8), :] += beside[far, line, RADIUS : SIDE - RADIUS, :]
@@ -563,8 +563,8 @@
             pltpu.VMEM((SIDE, SIDE, 128), BF16),
             pltpu.VMEM((SIDE, SIDE, 128), BF16),
             pltpu.VMEM((SIDE, SIDE, 128), BF16),
-            pltpu.VMEM((ROWS * PITCH, 128), F32),
-            pltpu.VMEM((ROWS * PITCH, 128), F32),
+            pltpu.VMEM((ROWS * PITCH + 8, 128), F32),
+            pltpu.VMEM((ROWS * PITCH + 8, 128), F32),
             pltpu.SemaphoreType.DMA((4,)),
             pltpu.SemaphoreType.DMA((3,)),
             pltpu.SemaphoreType.DMA((2, SIDE // BLOCK)),
@@ -589,7 +589,7 @@
             pltpu.VMEM((TAPS * TAPS, 8, 128), F32),
             pltpu.VMEM((TAPS, PAIRS, SIDE, 256), BF16),
             pltpu.VMEM((TAPS * 1024, 256), BF16),
-            pltpu.VMEM((rows, 128), F32),
+            pltpu.VMEM((rows + 8, 128), F32),
             pltpu.VMEM((ROWS * PITCH, 128), F32),
             pltpu.VMEM((ROWS * PITCH, 128), F32),
             pltpu.VMEM((SIDE, SIDE, 128), BF16),
@@ -624,17 +624,17 @@
 
 
 def run_edge(place, device, partial, arrived, mask_strips, weights):
-    rim = pltpu.VMEM((RADIUS, SIDE, 128), F32)
-    side = pltpu.VMEM((SIDE - 2 * RADIUS, 8, 128), F32)
+    rim = pltpu.VMEM((RADIUS + 1, SIDE, 128), F32)
+    side = pltpu.VMEM((SIDE, 8, 128), F32)
     return pl.pallas_call(
         edge_body,
         out_shape=jax.ShapeDtypeStruct((SIDE, SIDE, 128), F32),
         in_specs=[IN_SMEM, IN_SMEM, ANYWHERE] + [ANYWHERE] * 7 + [IN_VMEM] * 2,
         out_specs=ANYWHERE,
         scratch_shapes=[
-            pltpu.VMEM((2, RADIUS, PITCH, 128), F32),
-            pltpu.VMEM((2, RADIUS, PITCH, 128), F32),
-            pltpu.VMEM((2, RADIUS, SIDE, 128), F32),
+            pltpu.VMEM((2, RADIUS, PITCH + 8, 128), F32),
+            pltpu.VMEM((2, RADIUS, PITCH + 8, 128), F32),
+            pltpu.VMEM((2, RADIUS, SIDE + 8, 128), F32),
             rim, rim, side, side,
             pltpu.SemaphoreType.DMA((4,)),
             pltpu.VMEM((2 * GROUP * STRIP_ROWS, 128), BF16),
@@ -721,7 +721,7 @@
     )
     packed, paired, other = lax.optimization_barrier((packed, paired, other))
     arrived = swap_within_group(run_relay(neighbours, device, lists, strips, paired, other, True))
-    weights = flipped.reshape(TAPS * TAPS, 128)
+    weights = jnp.pad(flipped.reshape(TAPS * TAPS, 128), ((0, 15), (0, 0)))
     total, arrived = sum_over_tiles(packed, arrived)
     d_fields = run_edge(neighbours, device, partial, arrived, mask_strips, weights)
     t_in, t_out, t_bias_in, t_kernel, *t_small = run_unpack(total)

time: 114 us -> 114 us (level)
    pad x0 -> x3, local copies, waits for them, and re-layouts: none -> 1.27 us  [the longest x2 1.26 us: tap_rows(): jnp.pad(both.transpose(1, 0, 2).reshape(TAPS * 8, 256), ((0, 8), (0, 0)))]
    transpose x2, local copies, waits for them, and re-layouts: 1.28 us -> 0.04 us  [tap_rows(): both.transpose(1, 0, 2).reshape(TAPS * 8, 256)]
where the time goes in v9:
time: 114 us; the launch traced here: 113 us
  Pallas kernels  53.5 us (47%)
  starting transfers between devices  29.8 us (26%)
  waiting for transfers between devices  18.5 us (16%)
  local copies, waits for them, and re-layouts  8.23 us (7%)
  other arithmetic  2.46 us (2%)
    pallas_call x1, Pallas kernels, run_core(): pl.pallas_call(core_body, out_shape=(shape((SIDE, SIDE, 128), BF16), shap...  22 us
    pallas_call x1, Pallas kernels, run_inner(): pl.pallas_call(inner_body, out_shape=(jax.ShapeDtypeStruct((rows, 128), B...  15.6 us
    ppermute x4, starting transfers between devices, swap(): return lax.ppermute(value, 'tiles', pairs)  9.79 us
    ppermute x7, starting transfers between devices, swap_within_group(): lax.ppermute(block, 'tiles', [(i, i ^ k) for i in range(peers)])  7.68 us
    ppermute x7, waiting for transfers between devices, swap_within_group(): lax.ppermute(block, 'tiles', [(i, i ^ k) for i in range(peers)])  5.75 us
    all_to_all x1, waiting for transfers between devices, within_group(): lax.all_to_all(blocks, 'tiles', 0, 0, axis_index_groups=groups)  5.64 us
    all_to_all x1, waiting for transfers between devices, sum_over_tiles(): return (lax.all_to_all(shared, 'tiles', 0, 0).reshape(packed.shape), tie)  5.36 us
    all_to_all x1, starting transfers between devices, sum_over_tiles(): return (lax.all_to_all(shared, 'tiles', 0, 0).reshape(packed.shape), tie)  4.84 us
  transfers between devices with their start and end apart: 14, of which 7 were waited for; matrix products, arithmetic and copies ran while one was open for 7% of the time, Pallas kernels for 23%

profile of v9, /device:TPU:0, one launch (start us, length us, event | category | flops | bytes accessed | tf_op | source)
XLA Modules:
  0.0 113.3 jit_solution(3913740583616341053)
XLA Ops:
  0.6 2.4 %outgoing.1 = (bf16[784,128]{1,0:T(8,128)(2,1)}, f32[4,3,64,128]{3,2,1,0:T(8,128)}) custom-call(s32[1,8]{1,0:T(1,128)} %place.9, bf16[64,64,128]{2,1,0:T(8,128)(2,1)} %bitcast.33, s32[64,64]{1,0:T(8,128)} %bitcast.39), custom_call_target="tpu_custom_call" | custom-call | tf_op jit(solution)/shard_map/outgoing/pallas_call | solution.py:499
  3.1 3.0 %collective-permute-start = (bf16[784,128]{1,0:T(8,128)(2,1)}, bf16[784,128]{1,0:T(8,128)(2,1)S(1)}, u32[]{:S(2)}, u32[]{:S(2)}) collective-permute-start(bf16[784,128]{1,0:T(8,128)(2,1)} %get-tuple-element.54.own), channel_id=1, source_target_pairs={{0,8},{8,0},{1,9},{9,1},{2,10},{10,2},{3,11},{11,3},{4,12},{12,4},... | collective-permute-start | bytes 602120 | tf_op jit(solution)/shard_map/ppermute | solution.py:658
  6.8 1.4 %rev.3 = f32[7,7,128]{2,1,0:T(8,128)} reverse(f32[7,7,128]{2,1,0:T(8,128)} %param.17), dimensions={0,1} | reverse | bytes 50176 | tf_op jit(solution)/shard_map/rev | solution.py:716
  8.1 1.5 %pad_slice_fusion.3 = (f32[8,7,128]{2,1,0:T(8,128)}, f32[8,7,128]{2,1,0:T(8,128)}) fusion(f32[7,7,128]{2,1,0:T(8,128)} %param.17), kind=kLoop, calls=%fused_computation.8 | loop fusion | bytes 82432 | tf_op jit(solution)/shard_map/slice | solution.py:36
  9.6 1.7 %collective-permute-done.paired = bf16[784,128]{1,0:T(8,128)(2,1)S(1)} collective-permute-done((bf16[784,128]{1,0:T(8,128)(2,1)}, bf16[784,128]{1,0:T(8,128)(2,1)S(1)}, u32[]{:S(2)}, u32[]{:S(2)}) %collective-permute-start) | collective-permute-done | bytes 200736 | tf_op jit(solution)/shard_map/ppermute | solution.py:658
  12.0 2.2 %relay.2 = bf16[3072,128]{1,0:T(8,128)(2,1)} custom-call(s32[1,8]{1,0:T(1,128)} %place.9, s32[1]{0:T(128)} %bitcast.device, s32[2,8]{1,0:T(2,128)} %maximum_convert_fusion.lists, bf16[784,128]{1,0:T(8,128)(2,1)} %get-tuple-element.54.own, bf16[784,128]{1,0:T(8,128)(2,1)} %copy-done.2, bf16[784,128]{1,0:T(8,128)(2,1)} %copy-done.3), custom_call_target="tpu_custom_call" | custom-call | flops 2000000000 | bytes 1000000 | tf_op jit(solution)/shard_map/relay/pallas_call | solution.py:528
  14.3 4.2 %all-to-all-start = ((bf16[8,384,128]{2,1,0:T(8,128)(2,1)}), bf16[8,384,128]{2,1,0:T(8,128)(2,1)}, u32[]{:S(2)}, u32[]{:S(2)}) async-start(bf16[8,384,128]{2,1,0:T(8,128)(2,1)} %bitcast.35), calls=%async_computation | async-start | bytes 1572864 | tf_op jit(solution)/shard_map/all_to_all | solution.py:667
  21.4 4.0 %mask.1 = (bf16[64,64,128]{2,1,0:T(8,128)(2,1)}, bf16[64,64,128]{2,1,0:T(8,128)(2,1)}, bf16[64,64,128]{2,1,0:T(8,128)(2,1)}) custom-call(s32[64,64]{1,0:T(8,128)} %bitcast.40, bf16[64,64,128]{2,1,0:T(8,128)(2,1)} %bitcast.34, bf16[64,64,128]{2,1,0:T(8,128)(2,1)} %bitcast.41), custom_call_target="tpu_custom_call" | custom-call | flops 4000000000 | bytes 1000000 | tf_op jit(solution)/shard_map/mask/pallas_call | solution.py:514
  25.5 5.6 %all-to-all-done = bf16[8,384,128]{2,1,0:T(8,128)(2,1)} async-done(((bf16[8,384,128]{2,1,0:T(8,128)(2,1)}), bf16[8,384,128]{2,1,0:T(8,128)(2,1)}, u32[]{:S(2)}, u32[]{:S(2)}) %all-to-all-start) | async-done | bytes 786464 | tf_op jit(solution)/shard_map/all_to_all | solution.py:667
  31.1 22.0 %core.1 = (bf16[64,64,128]{2,1,0:T(8,128)(2,1)}, f32[5040,128]{1,0:T(8,128)}, bf16[768,128]{1,0:T(8,128)(2,1)}, f32[5040,128]{1,0:T(8,128)}, f32[128,512]{1,0:T(...) custom-call(s32[1,8]{1,0:T(1,128)} %place.9, s32[1]{0:T(128)} %bitcast.device, ...), custom_call_target="tpu_custom_call" | custom-call | flops 22000001024 | bytes 8000000 | tf_op jit(solution)/shard_map/core/pallas_call | solution.py:543
  53.2 4.8 %collective-permute-start.2 = (bf16[768,128]{1,0:T(8,128)(2,1)}, bf16[768,128]{1,0:T(8,128)(2,1)}, u32[]{:S(2)}, u32[]{:S(2)}) collective-permute-start(bf16[768,128]{1,0:T(8,128)(2,1)} %get-tuple-element.66.own), channel_id=1, source_target_pairs={{0,8},{8,0},{1,9},{9,1},{2,10},{10,2},{3,11},{11,3},{4,12},{12,4},... | collective-permute-start | bytes 589832 | tf_op jit(solution)/shard_map/ppermute | solution.py:658
  57.9 1.3 %collective-permute-start.3 = (bf16[768,128]{1,0:T(8,128)(2,1)}, bf16[768,128]{1,0:T(8,128)(2,1)}, u32[]{:S(2)}, u32[]{:S(2)}) collective-permute-start(bf16[768,128]{1,0:T(8,128)(2,1)} %get-tuple-element.66.own), channel_id=1, source_target_pairs={{8,16},{16,8},{9,17},{17,9},{10,18},{18,10},{11,19},{19,11},{12,20... | collective-permute-start | bytes 589832 | tf_op jit(solution)/shard_map/ppermute | solution.py:658
  59.3 15.6 %inner.1 = (bf16[1280,128]{1,0:T(8,128)(2,1)}, f32[64,64,128]{2,1,0:T(8,128)}) custom-call(f32[1]{0:T(128)} %constant.2.clone.1.scale, f32[5040,128]{1,0:T(8,128)} %get-tuple-element.58.padded, f32[5040,128]{1,0:T(8,128)} %get-tuple-element.59.d_conv, bf16[64,64,128]{2,1,0:T(8,128)(2,1)} %get-tuple-element.55.cotangent, ...), custom_call_target="tpu_custom_call" | custom-call | flops 16000000000 | bytes 8000000 | tf_op jit(solution)/shard_map/inner/pallas_call | solution.py:580
  74.9 3.3 %all-to-all-start.1 = ((bf16[32,40,128]{2,1,0:T(8,128)(2,1)}), bf16[32,40,128]{2,1,0:T(8,128)(2,1)}, u32[]{:S(2)}, u32[]{:S(2)}) async-start(bf16[32,40,128]{2,1,0:T(8,128)(2,1)} %bitcast.36), calls=%async_computation.1 | async-start | bytes 655360 | tf_op jit(solution)/shard_map/all_to_all | solution.py:681
  78.2 2.1 %relay.3 = (bf16[384,128]{1,0:T(8,128)(2,1)}, bf16[384,128]{1,0:T(8,128)(2,1)}, bf16[384,128]{1,0:T(8,128)(2,1)}, bf16[384,128]{1,0:T(8,128)(2,1)}, bf16[384,128...) custom-call(s32[1,8]{1,0:T(1,128)} %place.9, s32[1]{0:T(128)} %bitcast.device, ...), custom_call_target="tpu_custom_call" | custom-call | flops 2000000000 | bytes 1000000 | tf_op jit(solution)/shard_map/relay/pallas_call | solution.py:528
  80.3 2.3 %collective-permute-start.10 = (bf16[384,128]{1,0:T(8,128)(2,1)}, bf16[384,128]{1,0:T(8,128)(2,1)S(1)}, u32[]{:S(2)}, u32[]{:S(2)}) collective-permute-start(bf16[384,128]{1,0:T(8,128)(2,1)} %get-tuple-element.76), channel_id=1, source_target_pairs={{0,7},{1,6},{2,5},{3,4},{4,3},{5,2},{6,1},{7,0},{8,15},{9,14},{10,... | collective-permute-start | bytes 294920 | tf_op jit(solution)/shard_map/ppermute | solution.py:673
  85.0 2.3 %collective-permute-done.10.a7 = bf16[384,128]{1,0:T(8,128)(2,1)S(1)} collective-permute-done((bf16[384,128]{1,0:T(8,128)(2,1)}, bf16[384,128]{1,0:T(8,128)(2,1)S(1)}, u32[]{:S(2)}, u32[]{:S(2)}) %collective-permute-start.10) | collective-permute-done | bytes 98336 | tf_op jit(solution)/shard_map/ppermute | solution.py:673
  87.3 1.6 %collective-permute-start.8 = (bf16[384,128]{1,0:T(8,128)(2,1)}, bf16[384,128]{1,0:T(8,128)(2,1)S(1)}, u32[]{:S(2)}, u32[]{:S(2)}) collective-permute-start(bf16[384,128]{1,0:T(8,128)(2,1)} %get-tuple-element.74), channel_id=1, source_target_pairs={{0,5},{1,4},{2,7},{3,6},{4,1},{5,0},{6,3},{7,2},{8,13},{9,12},{10,... | collective-permute-start | bytes 294920 | tf_op jit(solution)/shard_map/ppermute | solution.py:673
  88.9 1.4 %collective-permute-start.9 = (bf16[384,128]{1,0:T(8,128)(2,1)}, bf16[384,128]{1,0:T(8,128)(2,1)S(1)}, u32[]{:S(2)}, u32[]{:S(2)}) collective-permute-start(bf16[384,128]{1,0:T(8,128)(2,1)} %get-tuple-element.75), channel_id=1, source_target_pairs={{0,6},{1,7},{2,4},{3,5},{4,2},{5,3},{6,0},{7,1},{8,14},{9,15},{10,... | collective-permute-start | bytes 294920 | tf_op jit(solution)/shard_map/ppermute | solution.py:673
  90.3 1.0 convert_reduce_fusion
  91.9 1.9 %collective-permute-done.8.a5 = bf16[384,128]{1,0:T(8,128)(2,1)S(1)} collective-permute-done((bf16[384,128]{1,0:T(8,128)(2,1)}, bf16[384,128]{1,0:T(8,128)(2,1)S(1)}, u32[]{:S(2)}, u32[]{:S(2)}) %collective-permute-start.8) | collective-permute-done | bytes 98336 | tf_op jit(solution)/shard_map/ppermute | solution.py:673
  95.6 4.8 %all-to-all-start.2 = ((bf16[32,40,128]{2,1,0:T(8,128)(2,1)}), bf16[32,40,128]{2,1,0:T(8,128)(2,1)S(1)}, u32[]{:S(2)}, u32[]{:S(2)}) async-start(bf16[32,40,128]{2,1,0:T(8,128)(2,1)} %broadcast_in_dim.14), calls=%async_computation.2 | async-start | bytes 655360 | tf_op jit(solution)/shard_map/all_to_all | solution.py:684
  102.9 4.2 %edge.1 = f32[64,64,128]{2,1,0:T(8,128)} custom-call(s32[1,8]{1,0:T(1,128)S(1)} %copy-done, s32[1]{0:T(128)} %bitcast.device, f32[64,64,128]{2,1,0:T(8,128)} %get-tuple-element.64.partial, bf16[384,128]{1,0:T(8,128)(2,1)S(1)} %collective-permute-done.4.a1, bf16[384,128]{1,0:T(8,128)(2,1)S(1)} %collective-permute-done.5.a2, ...), custom_call_target="tpu_custom_call", output_to_operand_aliasing={{}: (2, {})} | custom-call | flops 4000000000 | bytes 1000000 | tf_op jit(solution)/shard_map/edge/pallas_call | solution.py:629
  107.1 5.4 %all-to-all-done.2 = bf16[32,40,128]{2,1,0:T(8,128)(2,1)S(1)} async-done(((bf16[32,40,128]{2,1,0:T(8,128)(2,1)}), bf16[32,40,128]{2,1,0:T(8,128)(2,1)S(1)}, u32[]{:S(2)}, u32[]{:S(2)}) %all-to-all-start.2) | async-done | bytes 327712 | tf_op jit(solution)/shard_map/all_to_all | solution.py:684
  (36 shorter events, 12.3 us)
Async XLA Ops:
  3.1 8.2 %collective-permute-start = (bf16[784,128]{1,0:T(8,128)(2,1)}, bf16[784,128]{1,0:T(8,128)(2,1)S(1)}, u32[]{:S(2)}, u32[]{:S(2)}) collective-permute-start(bf16[784,128]{1,0:T(8,128)(2,1)} %get-tuple-element.54.own), channel_id=1, source_target_pairs={{0,8},{8,0},{1,9},{9,1},{2,10},{10,2},{3,11},{11,3},{4,12},{12,4},... | collective-permute-start | bytes 602120 | tf_op jit(solution)/shard_map/ppermute | solution.py:658
  6.1 5.2 %collective-permute-start.1 = (bf16[784,128]{1,0:T(8,128)(2,1)}, bf16[784,128]{1,0:T(8,128)(2,1)S(1)}, u32[]{:S(2)}, u32[]{:S(2)}) collective-permute-start(bf16[784,128]{1,0:T(8,128)(2,1)} %get-tuple-element.54.own), channel_id=1, source_target_pairs={{8,16},{16,8},{9,17},{17,9},{10,18},{18,10},{11,19},{19,11},{12,20... | collective-permute-start | bytes 602120 | tf_op jit(solution)/shard_map/ppermute | solution.py:658
  11.3 0.7 copy-start.2
  11.3 0.7 copy-start.3
  14.3 16.8 %all-to-all-start = ((bf16[8,384,128]{2,1,0:T(8,128)(2,1)}), bf16[8,384,128]{2,1,0:T(8,128)(2,1)}, u32[]{:S(2)}, u32[]{:S(2)}) async-start(bf16[8,384,128]{2,1,0:T(8,128)(2,1)} %bitcast.35), calls=%async_computation | async-start | bytes 1572864 | tf_op jit(solution)/shard_map/all_to_all | solution.py:667
  53.2 21.7 %collective-permute-start.2 = (bf16[768,128]{1,0:T(8,128)(2,1)}, bf16[768,128]{1,0:T(8,128)(2,1)}, u32[]{:S(2)}, u32[]{:S(2)}) collective-permute-start(bf16[768,128]{1,0:T(8,128)(2,1)} %get-tuple-element.66.own), channel_id=1, source_target_pairs={{0,8},{8,0},{1,9},{9,1},{2,10},{10,2},{3,11},{11,3},{4,12},{12,4},... | collective-permute-start | bytes 589832 | tf_op jit(solution)/shard_map/ppermute | solution.py:658
  57.9 16.9 %collective-permute-start.3 = (bf16[768,128]{1,0:T(8,128)(2,1)}, bf16[768,128]{1,0:T(8,128)(2,1)}, u32[]{:S(2)}, u32[]{:S(2)}) collective-permute-start(bf16[768,128]{1,0:T(8,128)(2,1)} %get-tuple-element.66.own), channel_id=1, source_target_pairs={{8,16},{16,8},{9,17},{17,9},{10,18},{18,10},{11,19},{19,11},{12,20... | collective-permute-start | bytes 589832 | tf_op jit(solution)/shard_map/ppermute | solution.py:658
  74.9 15.4 %all-to-all-start.1 = ((bf16[32,40,128]{2,1,0:T(8,128)(2,1)}), bf16[32,40,128]{2,1,0:T(8,128)(2,1)}, u32[]{:S(2)}, u32[]{:S(2)}) async-start(bf16[32,40,128]{2,1,0:T(8,128)(2,1)} %bitcast.36), calls=%async_computation.1 | async-start | bytes 655360 | tf_op jit(solution)/shard_map/all_to_all | solution.py:681
  80.3 6.9 %collective-permute-start.10 = (bf16[384,128]{1,0:T(8,128)(2,1)}, bf16[384,128]{1,0:T(8,128)(2,1)S(1)}, u32[]{:S(2)}, u32[]{:S(2)}) collective-permute-start(bf16[384,128]{1,0:T(8,128)(2,1)} %get-tuple-element.76), channel_id=1, source_target_pairs={{0,7},{1,6},{2,5},{3,4},{4,3},{5,2},{6,1},{7,0},{8,15},{9,14},{10,... | collective-permute-start | bytes 294920 | tf_op jit(solution)/shard_map/ppermute | solution.py:673
  82.6 6.3 %collective-permute-start.4 = (bf16[384,128]{1,0:T(8,128)(2,1)}, bf16[384,128]{1,0:T(8,128)(2,1)S(1)}, u32[]{:S(2)}, u32[]{:S(2)}) collective-permute-start(bf16[384,128]{1,0:T(8,128)(2,1)} %get-tuple-element.70), channel_id=1, source_target_pairs={{0,1},{1,0},{2,3},{3,2},{4,5},{5,4},{6,7},{7,6},{8,9},{9,8},{10,11... | collective-permute-start | bytes 294920 | tf_op jit(solution)/shard_map/ppermute | solution.py:673
  83.0 8.4 %collective-permute-start.5 = (bf16[384,128]{1,0:T(8,128)(2,1)}, bf16[384,128]{1,0:T(8,128)(2,1)S(1)}, u32[]{:S(2)}, u32[]{:S(2)}) collective-permute-start(bf16[384,128]{1,0:T(8,128)(2,1)} %get-tuple-element.71), channel_id=1, source_target_pairs={{0,2},{1,3},{2,0},{3,1},{4,6},{5,7},{6,4},{7,5},{8,10},{9,11},{10,... | collective-permute-start | bytes 294920 | tf_op jit(solution)/shard_map/ppermute | solution.py:673
  83.5 8.4 %collective-permute-start.6 = (bf16[384,128]{1,0:T(8,128)(2,1)}, bf16[384,128]{1,0:T(8,128)(2,1)S(1)}, u32[]{:S(2)}, u32[]{:S(2)}) collective-permute-start(bf16[384,128]{1,0:T(8,128)(2,1)} %get-tuple-element.72), channel_id=1, source_target_pairs={{0,3},{1,2},{2,1},{3,0},{4,7},{5,6},{6,5},{7,4},{8,11},{9,10},{10,... | collective-permute-start | bytes 294920 | tf_op jit(solution)/shard_map/ppermute | solution.py:673
  84.5 7.5 %collective-permute-start.7 = (bf16[384,128]{1,0:T(8,128)(2,1)}, bf16[384,128]{1,0:T(8,128)(2,1)S(1)}, u32[]{:S(2)}, u32[]{:S(2)}) collective-permute-start(bf16[384,128]{1,0:T(8,128)(2,1)} %get-tuple-element.73), channel_id=1, source_target_pairs={{0,4},{1,5},{2,6},{3,7},{4,0},{5,1},{6,2},{7,3},{8,12},{9,13},{10,... | collective-permute-start | bytes 294920 | tf_op jit(solution)/shard_map/ppermute | solution.py:673
  87.3 6.6 %collective-permute-start.8 = (bf16[384,128]{1,0:T(8,128)(2,1)}, bf16[384,128]{1,0:T(8,128)(2,1)S(1)}, u32[]{:S(2)}, u32[]{:S(2)}) collective-permute-start(bf16[384,128]{1,0:T(8,128)(2,1)} %get-tuple-element.74), channel_id=1, source_target_pairs={{0,5},{1,4},{2,7},{3,6},{4,1},{5,0},{6,3},{7,2},{8,13},{9,12},{10,... | collective-permute-start | bytes 294920 | tf_op jit(solution)/shard_map/ppermute | solution.py:673
  88.9 5.9 %collective-permute-start.9 = (bf16[384,128]{1,0:T(8,128)(2,1)}, bf16[384,128]{1,0:T(8,128)(2,1)S(1)}, u32[]{:S(2)}, u32[]{:S(2)}) collective-permute-start(bf16[384,128]{1,0:T(8,128)(2,1)} %get-tuple-element.75), channel_id=1, source_target_pairs={{0,6},{1,7},{2,4},{3,5},{4,2},{5,3},{6,0},{7,1},{8,14},{9,15},{10,... | collective-permute-start | bytes 294920 | tf_op jit(solution)/shard_map/ppermute | solution.py:673
  95.6 16.8 %all-to-all-start.2 = ((bf16[32,40,128]{2,1,0:T(8,128)(2,1)}), bf16[32,40,128]{2,1,0:T(8,128)(2,1)S(1)}, u32[]{:S(2)}, u32[]{:S(2)}) async-start(bf16[32,40,128]{2,1,0:T(8,128)(2,1)} %broadcast_in_dim.14), calls=%async_computation.2 | async-start | bytes 655360 | tf_op jit(solution)/shard_map/all_to_all | solution.py:684
  101.2 0.7 copy-start
  101.9 1.0 copy-start.1
